TPU v7x, 1024 devices: a whole 4x4x32 slice. The times are simulated.
1024 devices in a mesh: row: 32 (over y, z_lo), col: 32 (over x, z_hi, core).
Axes of the slice: x: 4, y: 4, z: 32 (z_hi: 4, z_lo: 8; z = z_hi * 8 + z_lo), core: 2. Of those that a mesh axis runs over, the one named last changes fastest.
Arguments:
- amplitudes: float32 [4096, 4096], P('row', 'col'), as said below
- coupling: bfloat16 [4096, 4096], P('row', 'col')
- source: float32 [4096, 4096], P('row', 'col')
- orbital_gaps: float32 [4096], replicated, may hold values from 2 to 6
Outputs:
- new_amplitudes: float32 [4096, 4096], P('row', 'col')
- norms: float32 [3], replicated
Inputs may be any that keep to these rules, and one draw needn't show every extreme that they name: amplitudes, coupling and source are symmetric matrices: entry (ia,jb) equals entry (jb,ia).
All inputs are finite; a program needn't handle non-finite values.
Results may differ from a plain program's by a relative error of at most 0.001.
Values may be sent and summed in bfloat16 or wider, within the bound.
No kernel may reach another device: no remote copies, remote signals or barrier semaphores. Data moves between devices by JAX's collectives and lax.ppermute only.
A program may use at most 32 MiB of HBM per device.

v0:
```python
import jax
import jax.numpy as jnp
from jax import lax
from jax.sharding import PartitionSpec as P

NO = 16
NV = 256
ITERS = 3


def body(amplitudes, coupling, source, orbital_gaps):
    rows_here, cols_here = amplitudes.shape
    row_start = lax.axis_index("row") * rows_here
    col_start = lax.axis_index("col") * cols_here
    gap_rows = lax.dynamic_slice_in_dim(orbital_gaps, row_start, rows_here)
    gap_cols = lax.dynamic_slice_in_dim(orbital_gaps, col_start, cols_here)
    delta = gap_rows[:, None] + gap_cols[None, :]
    amps = amplitudes
    coupling_cols = lax.all_gather(coupling, "row", axis=0, tiled=True)
    coupling_rows = lax.all_gather(coupling, "col", axis=1, tiled=True)
    square_list = []
    for step in range(ITERS):
        amps_low = amps.astype(jnp.bfloat16)
        amp_cols = lax.all_gather(amps_low, "row", axis=0, tiled=True)
        first_sum = jnp.dot(
            lax.all_gather(amps_low, "col", axis=1, tiled=True),
            coupling_cols,
            preferred_element_type=jnp.float32,
        )
        second_sum = jnp.dot(coupling_rows, amp_cols, preferred_element_type=jnp.float32)
        paired = first_sum + second_sum
        residual = source + delta * amps + paired + amps * paired
        local_square = jnp.sum(residual * residual)
        square_list.append(lax.psum(local_square, ("row", "col")))
        amps = amps - residual / delta
    stacked = jnp.stack(square_list)
    norms = jnp.sqrt(stacked) / (NO * NV)
    return (amps, norms)


def solution(mesh):
    in_specs = (P("row", "col"), P("row", "col"), P("row", "col"), P())
    out_specs = (P("row", "col"), P())
    return jax.shard_map(body, mesh=mesh, in_specs=in_specs, out_specs=out_specs, check_vma=False)
```

profile of v0, /device:TPU:1, one launch (start us, length us, event | category | flops | bytes accessed | tf_op | source)
XLA Modules:
  0.0 1576.9 jit_solution(15672987920111172858)
XLA Ops:
  7.2 0.0 all-gather.11.cloned.1.call-start
  7.2 0.7 all-gather.11.cloned.1.call-update
  7.9 0.0 all-gather.9.cloned.1.call-start
  7.9 1.5 convert_element_type.9
  9.4 0.0 all-gather.9.cloned.1.call-update
  9.4 0.0 all-gather.13.cloned.1.call-start
  9.5 0.7 all-gather.13.cloned.1.call-update
  10.2 0.0 all-gather.15.cloned.1.call-start
  10.2 0.5 all-gather.15.cloned.1.call-update
  10.7 0.0 all-gather.17.cloned.1.call-start
  10.8 0.8 fusion.19
  11.6 218.3 %all-gather.11.cloned.1.call-done = bf16[4096,128]{1,0:T(8,128)(2,1)} async-done(((bf16[128,128]{1,0:T(8,128)(2,1)}), bf16[4096,128]{1,0:T(8,128)(2,1)}) %all-gather.11.cloned.1.call-update) | async-done | bytes 1048592 | tf_op jit(solution)/shard_map/all_gather | solution.py:19
  229.9 144.1 %all-gather.9.cloned.1.call-done = bf16[128,4096]{1,0:T(8,128)(2,1)} async-done(((bf16[128,128]{1,0:T(8,128)(2,1)}), bf16[128,4096]{1,0:T(8,128)(2,1)}) %all-gather.9.cloned.1.call-update) | async-done | bytes 1048592 | tf_op jit(solution)/shard_map/all_gather | solution.py:26
  374.0 2.0 fusion.20
  376.0 111.0 %all-gather.13.cloned.1.call-done = bf16[128,4096]{1,0:T(8,128)(2,1)} async-done(((bf16[128,128]{1,0:T(8,128)(2,1)}), bf16[128,4096]{1,0:T(8,128)(2,1)}) %all-gather.13.cloned.1.call-update) | async-done | bytes 1048592 | tf_op jit(solution)/shard_map/all_gather | solution.py:20
  486.9 203.6 %all-gather.15.cloned.1.call-done = bf16[4096,128]{1,0:T(8,128)(2,1)} async-done(((bf16[128,128]{1,0:T(8,128)(2,1)}), bf16[4096,128]{1,0:T(8,128)(2,1)}) %all-gather.15.cloned.1.call-update) | async-done | bytes 1048592 | tf_op jit(solution)/shard_map/all_gather | solution.py:24
  690.5 3.3 fusion.17
  693.8 0.0 all-gather.19.cloned.1.call-start
  693.9 0.5 all-gather.19.cloned.1.call-update
  694.4 0.0 all-gather.21.cloned.1.call-start
  694.4 140.0 %all-gather.17.cloned.1.call-done = bf16[128,4096]{1,0:T(8,128)(2,1)} async-done(((bf16[128,128]{1,0:T(8,128)(2,1)}), bf16[128,4096]{1,0:T(8,128)(2,1)}) %all-gather.17.cloned.1.call-update) | async-done | bytes 1048592 | tf_op jit(solution)/shard_map/all_gather | solution.py:26
  834.4 1.6 fusion.21
  836.1 201.9 %all-gather.19.cloned.1.call-done = bf16[4096,128]{1,0:T(8,128)(2,1)} async-done(((bf16[128,128]{1,0:T(8,128)(2,1)}), bf16[4096,128]{1,0:T(8,128)(2,1)}) %all-gather.19.cloned.1.call-update) | async-done | bytes 1048592 | tf_op jit(solution)/shard_map/all_gather | solution.py:24
  1038.0 2.9 fusion.15
  1041.0 0.0 all-gather.23.cloned.1.call-start
  1041.0 0.7 all-gather.23.cloned.1.call-update
  1041.7 140.4 %all-gather.21.cloned.1.call-done = bf16[128,4096]{1,0:T(8,128)(2,1)} async-done(((bf16[128,128]{1,0:T(8,128)(2,1)}), bf16[128,4096]{1,0:T(8,128)(2,1)}) %all-gather.21.cloned.1.call-update) | async-done | bytes 1048592 | tf_op jit(solution)/shard_map/all_gather | solution.py:26
  1182.1 1.6 fusion.22
  1183.7 202.0 %all-gather.23.cloned.1.call-done = bf16[4096,128]{1,0:T(8,128)(2,1)} async-done(((bf16[128,128]{1,0:T(8,128)(2,1)}), bf16[4096,128]{1,0:T(8,128)(2,1)}) %all-gather.23.cloned.1.call-update) | async-done | bytes 1048592 | tf_op jit(solution)/shard_map/all_gather | solution.py:24
  1385.8 2.8 multiply_reduce_fusion
  1388.6 179.0 %all-reduce = (f32[1]{0:T(128)}, f32[1]{0:T(128)}, f32[1]{0:T(128)}) all-reduce(f32[1]{0:T(128)} %bitcast.4, f32[1]{0:T(128)} %bitcast.3, f32[1]{0:T(128)} %bitcast.2), channel_id=1, replica_groups=mesh['row'=32,'col'=32] {'row','col'}, use_global_device_ids=true, to_apply=%region_5.0 | all-reduce | flops 3 | bytes 24 | tf_op jit(solution)/shard_map/psum | solution.py:34
  1567.6 2.5 fusion.14
  (10 shorter events, 0.0 us)
Async XLA Ops:
  7.2 222.8 %all-gather.11.cloned.1.call-start = ((), (), s32[]{:S(2)}) async-start(), calls=%async_computation.1 | async-start | bytes 1081344 | tf_op jit(solution)/shard_map/all_gather | solution.py:19
  7.9 366.1 %all-gather.9.cloned.1.call-start = ((), (), s32[]{:S(2)}) async-start(), calls=%async_computation | async-start | bytes 1081344 | tf_op jit(solution)/shard_map/all_gather | solution.py:26
  9.4 477.5 %all-gather.13.cloned.1.call-start = ((), (), s32[]{:S(2)}) async-start(), calls=%async_computation.2 | async-start | bytes 1081344 | tf_op jit(solution)/shard_map/all_gather | solution.py:20
  10.2 680.3 %all-gather.15.cloned.1.call-start = ((), (), s32[]{:S(2)}) async-start(), calls=%async_computation.3 | async-start | bytes 1081344 | tf_op jit(solution)/shard_map/all_gather | solution.py:24
  10.7 823.7 %all-gather.17.cloned.1.call-start = ((), (), s32[]{:S(2)}) async-start(), calls=%async_computation.4 | async-start | bytes 1081344 | tf_op jit(solution)/shard_map/all_gather | solution.py:26
  11.6 678.9 %copy-start.2 = (f32[128,128]{1,0:T(8,128)S(1)}, f32[128,128]{1,0:T(8,128)}, u32[]{:S(2)}) copy-start(f32[128,128]{1,0:T(8,128)} %param.6) | copy-start | bytes 196612
  11.6 678.9 %copy-start.3 = (f32[128,128]{1,0:T(8,128)S(1)}, f32[128,128]{1,0:T(8,128)}, u32[]{:S(2)}) copy-start(f32[128,128]{1,0:T(8,128)} %param.4) | copy-start | bytes 196612
  690.5 143.9 %copy-start.1 = (bf16[4096,128]{1,0:T(8,128)(2,1)S(1)}, bf16[4096,128]{1,0:T(8,128)(2,1)}, u32[]{:S(2)}) copy-start(bf16[4096,128]{1,0:T(8,128)(2,1)} %all-gather.11.cloned.1.call-done) | copy-start | bytes 3145732
  693.8 344.2 %all-gather.19.cloned.1.call-start = ((), (), s32[]{:S(2)}) async-start(), calls=%async_computation.5 | async-start | bytes 1081344 | tf_op jit(solution)/shard_map/all_gather | solution.py:24
  694.4 343.6 %copy-start = (bf16[128,4096]{1,0:T(8,128)(2,1)S(1)}, bf16[128,4096]{1,0:T(8,128)(2,1)}, u32[]{:S(2)}) copy-start(bf16[128,4096]{1,0:T(8,128)(2,1)} %all-gather.13.cloned.1.call-done) | copy-start | bytes 3145732
  694.4 487.7 %all-gather.21.cloned.1.call-start = ((), (), s32[]{:S(2)}) async-start(), calls=%async_computation.6 | async-start | bytes 1081344 | tf_op jit(solution)/shard_map/all_gather | solution.py:26
  1041.0 344.8 %all-gather.23.cloned.1.call-start = ((), (), s32[]{:S(2)}) async-start(), calls=%async_computation.7 | async-start | bytes 1081344 | tf_op jit(solution)/shard_map/all_gather | solution.py:24
Sparse Core Ops, SparseCore 0:
  10.7 219.2 all-gather.10
  234.7 139.2 all-gather.8
  378.2 108.6 all-gather.12
  490.0 200.4 all-gather.14
  695.1 139.2 all-gather.16
  837.5 200.4 all-gather.18
  1042.8 139.2 all-gather.20
  1185.3 200.4 all-gather.22
where the time goes:
time: 1580 us
  waiting for transfers between devices  1360 us (86%)
  blocking collectives  179 us (11%)
    all_gather x3, waiting for transfers between devices, body(): amp_cols = lax.all_gather(amps_low, 'row', axis=0, tiled=True)  608 us
    all_gather x3, waiting for transfers between devices, body(): lax.all_gather(amps_low, 'col', axis=1, tiled=True)  424 us
    all_gather x1, waiting for transfers between devices, body(): coupling_cols = lax.all_gather(coupling, 'row', axis=0, tiled=True)  218 us
    psum x1, blocking collectives, body(): square_list.append(lax.psum(local_square, ('row', 'col')))  179 us
    all_gather x1, waiting for transfers between devices, body(): coupling_rows = lax.all_gather(coupling, 'col', axis=1, tiled=True)  111 us
  transfers between devices with their start and end apart: 8, of which 8 were waited for; matrix products, arithmetic and copies ran while one was open for 0% of the time, Pallas kernels for 0%

commit v1 on v0

v1 whole, which is shorter than its diff:
```python
import jax
import jax.numpy as jnp
from jax import lax
from jax.sharding import Mesh, PartitionSpec as P

NO = 16
NV = 256
ITERS = 3

AXES = ("y", "l", "x", "h", "c")
SIZES = (4, 8, 4, 4, 2)
SIDE = 32
ROW = ("y", "l")
COL = ("x", "h", "c")


def gather(tile, axes, count):
    copies = jnp.broadcast_to(tile[None], (count,) + tile.shape)
    return lax.all_to_all(copies, axes, 0, 0, tiled=True)


def swap(tile, axis, size, bit):
    return lax.ppermute(tile, axis, [(i, i ^ bit) for i in range(size)])


def ordered(own, other, bit):
    first = bit == 0
    return jnp.stack([jnp.where(first, own, other), jnp.where(first, other, own)])


def transpose_tiles(tile):
    pairs = [(r * SIDE + c, c * SIDE + r) for r in range(SIDE) for c in range(SIDE)]
    return lax.ppermute(tile, AXES, pairs)


def gather_amps(low):
    by_l = gather(low, "l", 8)
    by_y = gather(by_l, "y", 4)
    return by_y.reshape(-1, low.shape[1])


def body(amplitudes, coupling, source, orbital_gaps):
    n = amplitudes.shape[0]
    h = lax.axis_index("h")
    row_start = lax.axis_index(ROW) * n
    col_start = lax.axis_index(COL) * n
    gap_rows = lax.dynamic_slice_in_dim(orbital_gaps, row_start, n)
    gap_cols = lax.dynamic_slice_in_dim(orbital_gaps, col_start, n)
    delta = gap_rows[:, None] + gap_cols[None, :]

    turned = coupling.T
    far = swap(turned, "h", 4, 2)
    low = amplitudes.astype(jnp.bfloat16)
    by_l = gather(low, "l", 8)
    far, by_l = lax.optimization_barrier((far, by_l))
    pair = ordered(turned, far, h // 2)
    near = swap(pair, "h", 4, 1)
    amp_cols = gather(by_l, "y", 4).reshape(-1, n)
    near, amp_cols = lax.optimization_barrier((near, amp_cols))
    quad = jnp.swapaxes(ordered(pair, near, h % 2), 0, 1).reshape(4, n, n)
    by_x = gather(quad, "x", 4).reshape(16, n, n)
    other = swap(by_x, "c", 2, 1)
    both = ordered(by_x, other, lax.axis_index("c"))
    coupling_rows = jnp.swapaxes(both, 0, 1).reshape(-1, n)

    amps = amplitudes
    squares = []
    for step in range(ITERS):
        if step:
            amp_cols = gather_amps(amps.astype(jnp.bfloat16))
        product = lax.dot_general(
            coupling_rows,
            amp_cols,
            (((0,), (0,)), ((), ())),
            preferred_element_type=jnp.float32,
        )
        paired = product + transpose_tiles(product).T
        residual = source + delta * amps + paired + amps * paired
        squares.append(jnp.sum(residual * residual))
        amps = amps - residual / delta

    local = jnp.zeros((1, 128), jnp.float32)
    local = local.at[0, :ITERS].set(jnp.stack(squares))
    plane = jnp.sum(gather(local, ("y", "x", "c"), 32), axis=0)
    total = jnp.sum(gather(plane, ("l", "h"), 32), axis=0)
    norms = jnp.sqrt(total[0, :ITERS]) / (NO * NV)
    return (amps, norms)


def solution(mesh):
    fine = Mesh(mesh.devices.reshape(SIZES), AXES)
    in_specs = (P(ROW, COL), P(ROW, COL), P(ROW, COL), P())
    out_specs = (P(ROW, COL), P())
    return jax.shard_map(body, mesh=fine, in_specs=in_specs, out_specs=out_specs, check_vma=False)
```

time: 1580 us -> 302 us (0.19)
  waiting for transfers between devices: 1360 us -> 32.6 us
  starting transfers between devices: 0.32 us -> 99.7 us
  blocking collectives: 179 us -> 155 us
    all_gather x8 -> x0, waiting for transfers between devices: 1360 us -> none  [the longest x3 608 us: body(): amp_cols = lax.all_gather(amps_low, 'row', axis=0, tiled=True)]
    psum x1 -> x0, blocking collectives: 179 us -> none  [body(): square_list.append(lax.psum(local_square, ('row', 'col')))]
    all_to_all x0 -> x6, blocking collectives: none -> 155 us  [gather(): return lax.all_to_all(copies, axes, 0, 0, tiled=True)]
    ppermute x0 -> x6, starting transfers between devices: none -> 58.2 us  [the longest x3 41.4 us: swap(): return lax.ppermute(tile, axis, [(i, i ^ bit) for i in range(size)])]
    all_to_all x0 -> x3, starting transfers between devices: none -> 41.4 us  [gather(): return lax.all_to_all(copies, axes, 0, 0, tiled=True)]
    all_to_all x0 -> x3, waiting for transfers between devices: none -> 19.9 us  [gather(): return lax.all_to_all(copies, axes, 0, 0, tiled=True)]
  transfers between devices with their start and end apart: 8 -> 9, of which waited for: 8 -> 7; matrix products, arithmetic and copies ran while one was open for 0% -> 1% of each run, Pallas kernels for 0% -> 0%
where the time goes in v1:
time: 302 us
  blocking collectives  155 us (51%)
  starting transfers between devices  99.7 us (33%)
  waiting for transfers between devices  32.6 us (11%)
  other arithmetic  7.97 us (3%)
  local copies, waits for them, and re-layouts  4.44 us (1%)
    all_to_all x6, blocking collectives, gather(): return lax.all_to_all(copies, axes, 0, 0, tiled=True)  155 us
    all_to_all x3, starting transfers between devices, gather(): return lax.all_to_all(copies, axes, 0, 0, tiled=True)  41.4 us
    ppermute x3, starting transfers between devices, swap(): return lax.ppermute(tile, axis, [(i, i ^ bit) for i in range(size)])  41.4 us
    all_to_all x3, waiting for transfers between devices, gather(): return lax.all_to_all(copies, axes, 0, 0, tiled=True)  19.9 us
    ppermute x3, starting transfers between devices, transpose_tiles(): return lax.ppermute(tile, AXES, pairs)  16.9 us
    ppermute x3, waiting for transfers between devices, swap(): return lax.ppermute(tile, axis, [(i, i ^ bit) for i in range(size)])  6.76 us
  transfers between devices with their start and end apart: 9, of which 7 were waited for; matrix products, arithmetic and copies ran while one was open for 1% of the time, Pallas kernels for 0%

profile of v1, /device:TPU:1, one launch (start us, length us, event | category | flops | bytes accessed | tf_op | source)
XLA Modules:
  0.0 301.6 jit_solution(13423255931730705052)
XLA Ops:
  0.6 0.8 convert_element_type.9
  1.5 0.7 broadcast_in_dim.22
  2.2 13.2 %all-to-all-start = ((bf16[8,128,128]{2,1,0:T(8,128)(2,1)}), bf16[8,128,128]{2,1,0:T(8,128)(2,1)S(1)}, u32[]{:S(2)}, u32[]{:S(2)}) async-start(bf16[8,128,128]{2,1,0:T(8,128)(2,1)} %broadcast_in_dim.22), calls=%async_computation | async-start | bytes 524288 | tf_op jit(solution)/shard_map/all_to_all | solution.py:19
  15.5 21.2 %collective-permute-start = (bf16[128,128]{1,0:T(8,128)(2,1)S(1)}, bf16[128,128]{1,0:T(8,128)(2,1)S(1)}, u32[]{:S(2)}, u32[]{:S(2)}) collective-permute-start(bf16[128,128]{1,0:T(8,128)(2,1)S(1)} %bitcast.68), channel_id=1, source_target_pairs={{0,4},{2,6},{4,0},{6,2},{1,5},{3,7},{5,1},{7,3},{8,12},{10,14},{12... | collective-permute-start | bytes 98312 | tf_op jit(solution)/shard_map/ppermute | solution.py:23
  36.7 3.6 %collective-permute-done = bf16[128,128]{1,0:T(8,128)(2,1)S(1)} collective-permute-done((bf16[128,128]{1,0:T(8,128)(2,1)S(1)}, bf16[128,128]{1,0:T(8,128)(2,1)S(1)}, u32[]{:S(2)}, u32[]{:S(2)}) %collective-permute-start) | collective-permute-done | bytes 32800 | tf_op jit(solution)/shard_map/ppermute | solution.py:23
  40.4 1.2 broadcast_in_dim.23
  41.6 4.3 %all-to-all-start.1 = ((bf16[4,8,128,128]{3,2,1,0:T(8,128)(2,1)}), bf16[4,8,128,128]{3,2,1,0:T(8,128)(2,1)S(1)}, u32[]{:S(2)}, u32[]{:S(2)}) async-start(bf16[4,8,128,128]{3,2,1,0:T(8,128)(2,1)} %broadcast_in_dim.23), calls=%async_computation.1 | async-start | bytes 2097152 | tf_op jit(solution)/shard_map/all_to_all | solution.py:19
  45.9 13.5 %collective-permute-start.1 = (bf16[2,128,128]{2,1,0:T(8,128)(2,1)S(1)}, bf16[2,128,128]{2,1,0:T(8,128)(2,1)S(1)}, u32[]{:S(2)}, u32[]{:S(2)}) collective-permute-start(bf16[2,128,128]{2,1,0:T(8,128)(2,1)S(1)} %pad_maximum_fusion.2), channel_id=1, source_target_pairs={{0,2},{2,0},{4,6},{6,4},{1,3},{3,1},{5,7},{7,5},{8,10},{10,8},{12,... | collective-permute-start | bytes 196616 | tf_op jit(solution)/shard_map/ppermute | solution.py:23
  59.4 1.6 collective-permute-done.1
  61.2 10.7 %all_to_all.45 = bf16[4,4,128,128]{3,2,1,0:T(8,128)(2,1)S(1)} all-to-all(bf16[4,4,128,128]{3,2,1,0:T(8,128)(2,1)S(1)} %broadcast_in_dim.25), channel_id=1, replica_groups=mesh['y'=4,'l'=8,'x'=4,'h'=4,'c'=2] {'x'}, dimensions={0} | all-to-all | bytes 1048576 | tf_op jit(solution)/shard_map/all_to_all | solution.py:19
  72.0 6.7 %collective-permute-start.2 = (bf16[16,128,128]{2,1,0:T(8,128)(2,1)S(1)}, bf16[16,128,128]{2,1,0:T(8,128)(2,1)S(1)}, u32[]{:S(2)}, u32[]{:S(2)}) collective-permute-start(bf16[16,128,128]{2,1,0:T(8,128)(2,1)S(1)} %bitcast.66), channel_id=1, source_target_pairs={{0,1},{1,0},{2,3},{3,2},{4,5},{5,4},{6,7},{7,6},{8,9},{9,8},{10,11... | collective-permute-start | bytes 1572872 | tf_op jit(solution)/shard_map/ppermute | solution.py:23
  78.6 1.5 collective-permute-done.2
  81.0 4.0 %collective-permute-start.3 = (f32[128,128]{0,1:T(8,128)S(1)}, f32[128,128]{0,1:T(8,128)S(1)}, u32[]{:S(2)}, u32[]{:S(2)}) collective-permute-start(f32[128,128]{0,1:T(8,128)S(1)} %copy.24), channel_id=1, source_target_pairs={{0,0},{1,32},{2,64},{3,96},{4,128},{5,160},{6,192},{7,224},{8,256}... | collective-permute-start | bytes 196616 | tf_op jit(solution)/shard_map/ppermute | solution.py:33
  84.9 0.8 fusion.19
  85.8 1.1 collective-permute-done.3
  86.9 0.7 multiply_reduce_fusion.2
  87.7 50.7 %all_to_all.46 = bf16[8,128,128]{2,1,0:T(8,128)(2,1)S(1)} all-to-all(bf16[8,128,128]{2,1,0:T(8,128)(2,1)S(1)} %broadcast_in_dim.26), channel_id=1, replica_groups=mesh['y'=4,'l'=8,'x'=4,'h'=4,'c'=2] {'l'}, dimensions={0} | all-to-all | bytes 524288 | tf_op jit(solution)/shard_map/all_to_all | solution.py:19
  138.7 25.4 %all_to_all.47 = bf16[4,8,128,128]{3,2,1,0:T(8,128)(2,1)S(1)} all-to-all(bf16[4,8,128,128]{3,2,1,0:T(8,128)(2,1)S(1)} %broadcast_in_dim.27), channel_id=1, replica_groups=mesh['y'=4,'l'=8,'x'=4,'h'=4,'c'=2] {'y'}, dimensions={0} | all-to-all | bytes 2097152 | tf_op jit(solution)/shard_map/all_to_all | solution.py:19
  164.7 4.9 %collective-permute-start.4 = (f32[128,128]{0,1:T(8,128)S(1)}, f32[128,128]{0,1:T(8,128)S(1)}, u32[]{:S(2)}, u32[]{:S(2)}) collective-permute-start(f32[128,128]{0,1:T(8,128)S(1)} %copy.25), channel_id=1, source_target_pairs={{0,0},{1,32},{2,64},{3,96},{4,128},{5,160},{6,192},{7,224},{8,256}... | collective-permute-start | bytes 196616 | tf_op jit(solution)/shard_map/ppermute | solution.py:33
  169.6 3.3 %collective-permute-done.4 = f32[128,128]{0,1:T(8,128)S(1)} collective-permute-done((f32[128,128]{0,1:T(8,128)S(1)}, f32[128,128]{0,1:T(8,128)S(1)}, u32[]{:S(2)}, u32[]{:S(2)}) %collective-permute-start.4) | collective-permute-done | bytes 65568 | tf_op jit(solution)/shard_map/ppermute | solution.py:33
  172.9 0.7 multiply_reduce_fusion.1
  173.8 30.8 %all_to_all.48 = bf16[8,128,128]{2,1,0:T(8,128)(2,1)S(1)} all-to-all(bf16[8,128,128]{2,1,0:T(8,128)(2,1)S(1)} %broadcast_in_dim.28), channel_id=1, replica_groups=mesh['y'=4,'l'=8,'x'=4,'h'=4,'c'=2] {'l'}, dimensions={0} | all-to-all | bytes 524288 | tf_op jit(solution)/shard_map/all_to_all | solution.py:19
  204.8 23.9 %all_to_all.49 = bf16[4,8,128,128]{3,2,1,0:T(8,128)(2,1)S(1)} all-to-all(bf16[4,8,128,128]{3,2,1,0:T(8,128)(2,1)S(1)} %broadcast_in_dim.29), channel_id=1, replica_groups=mesh['y'=4,'l'=8,'x'=4,'h'=4,'c'=2] {'y'}, dimensions={0} | all-to-all | bytes 2097152 | tf_op jit(solution)/shard_map/all_to_all | solution.py:19
  229.3 8.0 %collective-permute-start.5 = (f32[128,128]{0,1:T(8,128)S(1)}, f32[128,128]{0,1:T(8,128)S(1)}, u32[]{:S(2)}, u32[]{:S(2)}) collective-permute-start(f32[128,128]{0,1:T(8,128)S(1)} %copy.26), channel_id=1, source_target_pairs={{0,0},{1,32},{2,64},{3,96},{4,128},{5,160},{6,192},{7,224},{8,256}... | collective-permute-start | bytes 196616 | tf_op jit(solution)/shard_map/ppermute | solution.py:33
  237.3 0.6 compare_reduce_fusion
  237.9 1.5 collective-permute-done.5
  239.4 0.8 multiply_reduce_fusion
  240.2 2.6 broadcast_select_fusion
  242.8 13.0 %all_to_all.50 = f32[32,1,128]{2,1,0:T(1,128)S(1)} all-to-all(f32[32,1,128]{2,1,0:T(1,128)S(1)} %broadcast_in_dim.31), channel_id=1, replica_groups=mesh['y'=4,'l'=8,'x'=4,'h'=4,'c'=2] {'y','x','c'}, dimensions={0} | all-to-all | bytes 32768 | tf_op jit(solution)/shard_map/all_to_all | solution.py:19
  256.4 24.0 %all-to-all-start.8 = ((f32[32,1,128]{2,1,0:T(1,128)}), f32[32,1,128]{2,1,0:T(1,128)S(1)}, u32[]{:S(2)}, u32[]{:S(2)}) async-start(f32[32,1,128]{2,1,0:T(1,128)} %broadcast_in_dim.32), calls=%async_computation.8 | async-start | bytes 32768 | tf_op jit(solution)/shard_map/all_to_all | solution.py:19
  280.4 0.7 fusion.11
  281.1 19.9 %all-to-all-done.8 = f32[32,1,128]{2,1,0:T(1,128)S(1)} async-done(((f32[32,1,128]{2,1,0:T(1,128)}), f32[32,1,128]{2,1,0:T(1,128)S(1)}, u32[]{:S(2)}, u32[]{:S(2)}) %all-to-all-start.8) | async-done | bytes 16416 | tf_op jit(solution)/shard_map/all_to_all | solution.py:19
  (34 shorter events, 4.1 us)
Async XLA Ops:
  2.2 13.2 %copy-start.2 = (bf16[128,128]{1,0:T(8,128)(2,1)S(1)}, bf16[128,128]{1,0:T(8,128)(2,1)}, u32[]{:S(2)}) copy-start(bf16[128,128]{1,0:T(8,128)(2,1)} %param.7) | copy-start | bytes 98308
  2.2 38.2 %all-to-all-start = ((bf16[8,128,128]{2,1,0:T(8,128)(2,1)}), bf16[8,128,128]{2,1,0:T(8,128)(2,1)S(1)}, u32[]{:S(2)}, u32[]{:S(2)}) async-start(bf16[8,128,128]{2,1,0:T(8,128)(2,1)} %broadcast_in_dim.22), calls=%async_computation | async-start | bytes 524288 | tf_op jit(solution)/shard_map/all_to_all | solution.py:19
  15.5 24.8 %collective-permute-start = (bf16[128,128]{1,0:T(8,128)(2,1)S(1)}, bf16[128,128]{1,0:T(8,128)(2,1)S(1)}, u32[]{:S(2)}, u32[]{:S(2)}) collective-permute-start(bf16[128,128]{1,0:T(8,128)(2,1)S(1)} %bitcast.68), channel_id=1, source_target_pairs={{0,4},{2,6},{4,0},{6,2},{1,5},{3,7},{5,1},{7,3},{8,12},{10,14},{12... | collective-permute-start | bytes 98312 | tf_op jit(solution)/shard_map/ppermute | solution.py:23
  41.6 19.5 %all-to-all-start.1 = ((bf16[4,8,128,128]{3,2,1,0:T(8,128)(2,1)}), bf16[4,8,128,128]{3,2,1,0:T(8,128)(2,1)S(1)}, u32[]{:S(2)}, u32[]{:S(2)}) async-start(bf16[4,8,128,128]{3,2,1,0:T(8,128)(2,1)} %broadcast_in_dim.23), calls=%async_computation.1 | async-start | bytes 2097152 | tf_op jit(solution)/shard_map/all_to_all | solution.py:19
  45.9 15.2 %collective-permute-start.1 = (bf16[2,128,128]{2,1,0:T(8,128)(2,1)S(1)}, bf16[2,128,128]{2,1,0:T(8,128)(2,1)S(1)}, u32[]{:S(2)}, u32[]{:S(2)}) collective-permute-start(bf16[2,128,128]{2,1,0:T(8,128)(2,1)S(1)} %pad_maximum_fusion.2), channel_id=1, source_target_pairs={{0,2},{2,0},{4,6},{6,4},{1,3},{3,1},{5,7},{7,5},{8,10},{10,8},{12,... | collective-permute-start | bytes 196616 | tf_op jit(solution)/shard_map/ppermute | solution.py:23
  72.0 8.2 %collective-permute-start.2 = (bf16[16,128,128]{2,1,0:T(8,128)(2,1)S(1)}, bf16[16,128,128]{2,1,0:T(8,128)(2,1)S(1)}, u32[]{:S(2)}, u32[]{:S(2)}) collective-permute-start(bf16[16,128,128]{2,1,0:T(8,128)(2,1)S(1)} %bitcast.66), channel_id=1, source_target_pairs={{0,1},{1,0},{2,3},{3,2},{4,5},{5,4},{6,7},{7,6},{8,9},{9,8},{10,11... | collective-permute-start | bytes 1572872 | tf_op jit(solution)/shard_map/ppermute | solution.py:23
  80.8 6.0 %copy-start = (f32[128,128]{1,0:T(8,128)S(1)}, f32[128,128]{1,0:T(8,128)}, u32[]{:S(2)}) copy-start(f32[128,128]{1,0:T(8,128)} %param.8) | copy-start | bytes 196612
  80.9 6.0 %copy-start.1 = (f32[128,128]{1,0:T(8,128)S(1)}, f32[128,128]{1,0:T(8,128)}, u32[]{:S(2)}) copy-start(f32[128,128]{1,0:T(8,128)} %param.6) | copy-start | bytes 196612
  81.0 5.9 %collective-permute-start.3 = (f32[128,128]{0,1:T(8,128)S(1)}, f32[128,128]{0,1:T(8,128)S(1)}, u32[]{:S(2)}, u32[]{:S(2)}) collective-permute-start(f32[128,128]{0,1:T(8,128)S(1)} %copy.24), channel_id=1, source_target_pairs={{0,0},{1,32},{2,64},{3,96},{4,128},{5,160},{6,192},{7,224},{8,256}... | collective-permute-start | bytes 196616 | tf_op jit(solution)/shard_map/ppermute | solution.py:33
  164.7 8.2 %collective-permute-start.4 = (f32[128,128]{0,1:T(8,128)S(1)}, f32[128,128]{0,1:T(8,128)S(1)}, u32[]{:S(2)}, u32[]{:S(2)}) collective-permute-start(f32[128,128]{0,1:T(8,128)S(1)} %copy.25), channel_id=1, source_target_pairs={{0,0},{1,32},{2,64},{3,96},{4,128},{5,160},{6,192},{7,224},{8,256}... | collective-permute-start | bytes 196616 | tf_op jit(solution)/shard_map/ppermute | solution.py:33
  229.3 10.2 %collective-permute-start.5 = (f32[128,128]{0,1:T(8,128)S(1)}, f32[128,128]{0,1:T(8,128)S(1)}, u32[]{:S(2)}, u32[]{:S(2)}) collective-permute-start(f32[128,128]{0,1:T(8,128)S(1)} %copy.26), channel_id=1, source_target_pairs={{0,0},{1,32},{2,64},{3,96},{4,128},{5,160},{6,192},{7,224},{8,256}... | collective-permute-start | bytes 196616 | tf_op jit(solution)/shard_map/ppermute | solution.py:33
  256.4 44.6 %all-to-all-start.8 = ((f32[32,1,128]{2,1,0:T(1,128)}), f32[32,1,128]{2,1,0:T(1,128)S(1)}, u32[]{:S(2)}, u32[]{:S(2)}) async-start(f32[32,1,128]{2,1,0:T(1,128)} %broadcast_in_dim.32), calls=%async_computation.8 | async-start | bytes 32768 | tf_op jit(solution)/shard_map/all_to_all | solution.py:19

commit v2 on v1

v2 whole, which is shorter than its diff:
```python
import jax
import jax.numpy as jnp
import numpy as np
from jax import lax
from jax.sharding import Mesh, PartitionSpec as P

NO = 16
NV = 256
ITERS = 3

AXES = ("y", "m", "p", "x", "h", "c")
SIZES = (4, 4, 2, 4, 4, 2)
ROW = ("y", "m", "p")
COL = ("x", "h", "c")
NEAR_ROW = ("y", "x", "p")
NEAR_COL = ("m", "h", "c")


def places():
    side = SIZES[0] * SIZES[1] * SIZES[2]
    grid = np.arange(side * side).reshape(SIZES)
    return grid.reshape(side, side), grid.transpose(0, 3, 2, 1, 4, 5).reshape(side, side)


def send(tile, source, target):
    pairs = list(zip(source.ravel().tolist(), target.ravel().tolist()))
    return lax.ppermute(tile, AXES, pairs)


def swap(tile, axis, bit):
    size = SIZES[AXES.index(axis)]
    return lax.ppermute(tile, axis, [(i, i ^ bit) for i in range(size)])


def gather(tiles, *axes):
    count = int(np.prod([SIZES[AXES.index(axis)] for axis in axes]))
    copies = jnp.broadcast_to(tiles[None], (count,) + tiles.shape)
    got = lax.all_to_all(copies, axes, 0, 0, tiled=True)
    return got.reshape((-1,) + tiles.shape[1:])


def ordered(own, other, bit):
    first = bit == 0
    return jnp.stack([jnp.where(first, own, other), jnp.where(first, other, own)])


def with_core(tiles):
    both = ordered(tiles, swap(tiles, "c", 1), lax.axis_index("c"))
    return jnp.swapaxes(both, 0, 1).reshape(-1, tiles.shape[-1])


def multiply(left, right):
    dims = (((0,), (0,)), ((), ()))
    return lax.dot_general(left, right, dims, preferred_element_type=jnp.float32)


def body(amplitudes, coupling, source, orbital_gaps):
    n = amplitudes.shape[0]
    start, near = places()
    h = lax.axis_index("h")

    turned = coupling.T
    far = swap(turned, "h", 2)
    low = amplitudes.astype(jnp.bfloat16)[None]
    by_m = gather(low, "m", "p")
    far, by_m = lax.optimization_barrier((far, by_m))
    pair = ordered(turned, far, h // 2)
    close = swap(pair, "h", 1)
    amp_cols = gather(by_m, "y").reshape(-1, n)
    state = send(jnp.stack([source, amplitudes]), start, near)
    close, amp_cols, state = lax.optimization_barrier((close, amp_cols, state))
    quad = jnp.swapaxes(ordered(pair, close, h % 2), 0, 1).reshape(-1, n, n)
    by_x = gather(quad, "x")
    product = multiply(with_core(by_x), amp_cols)
    later = send(by_x, start, near)
    own = send(product, start, near)
    mirror = send(product, start, near.T)
    later, own, mirror = lax.optimization_barrier((later, own, mirror))
    coupling_rows = with_core(later)
    source, amps = state[0], state[1]

    gap_rows = lax.dynamic_slice_in_dim(orbital_gaps, lax.axis_index(NEAR_ROW) * n, n)
    gap_cols = lax.dynamic_slice_in_dim(orbital_gaps, lax.axis_index(NEAR_COL) * n, n)
    delta = gap_rows[:, None] + gap_cols[None, :]
    squares = []
    for step in range(ITERS):
        if step:
            amp_cols = gather(amps.astype(jnp.bfloat16)[None], *NEAR_ROW).reshape(-1, n)
            own = multiply(coupling_rows, amp_cols)
            mirror = send(own, near, near.T)
        paired = own + mirror.T
        residual = source + delta * amps + paired + amps * paired
        squares.append(jnp.sum(residual * residual))
        amps = amps - residual / delta

    local = jnp.zeros((1, 128), jnp.float32)
    local = local.at[0, :ITERS].set(jnp.stack(squares))
    plane = jnp.sum(gather(local[None], "y", "x", "c"), axis=0)
    total = jnp.sum(gather(plane[None], "m", "p", "h"), axis=0)
    norms = jnp.sqrt(total[0, :ITERS]) / (NO * NV)
    return (send(amps, near, start), norms)


def solution(mesh):
    fine = Mesh(mesh.devices.reshape(SIZES), AXES)
    in_specs = (P(ROW, COL), P(ROW, COL), P(ROW, COL), P())
    out_specs = (P(ROW, COL), P())
    return jax.shard_map(body, mesh=fine, in_specs=in_specs, out_specs=out_specs, check_vma=False)
```

time: 302 us -> 344 us (1.14)
  starting transfers between devices: 99.7 us -> 166 us
  blocking collectives: 155 us -> 113 us
  waiting for transfers between devices: 32.6 us -> 46.7 us
    all_to_all x3 -> x4, starting transfers between devices: 41.4 us -> 112 us  [gather(): got = lax.all_to_all(copies, axes, 0, 0, tiled=True)]
    all_to_all x6 -> x3, blocking collectives: 155 us -> 113 us  [gather(): got = lax.all_to_all(copies, axes, 0, 0, tiled=True)]
    all_to_all x3 -> x4, waiting for transfers between devices: 19.9 us -> 31.6 us  [gather(): got = lax.all_to_all(copies, axes, 0, 0, tiled=True)]
    ppermute x3 -> x7, starting transfers between devices: 16.9 us -> 13.2 us  [send(): return lax.ppermute(tile, AXES, pairs)]
    ppermute x3 -> x7, waiting for transfers between devices: 5.91 us -> 7.2 us  [send(): return lax.ppermute(tile, AXES, pairs)]
    ppermute x3 -> x4, waiting for transfers between devices: 6.76 us -> 7.9 us  [swap(): return lax.ppermute(tile, axis, [(i, i ^ bit) for i in range(size)])]
    ppermute x3 -> x4, starting transfers between devices: 41.4 us -> 41.1 us  [swap(): return lax.ppermute(tile, axis, [(i, i ^ bit) for i in range(size)])]
  transfers between devices with their start and end apart: 9 -> 15, of which waited for: 7 -> 9; matrix products, arithmetic and copies ran while one was open for 1% -> 1% of each run, Pallas kernels for 0% -> 0%
where the time goes in v2:
time: 344 us; the launch traced here: 343 us
  starting transfers between devices  166 us (48%)
  blocking collectives  113 us (33%)
  waiting for transfers between devices  46.7 us (14%)
  other arithmetic  7.54 us (2%)
  local copies, waits for them, and re-layouts  7.35 us (2%)
    all_to_all x3, blocking collectives, gather(): got = lax.all_to_all(copies, axes, 0, 0, tiled=True)  113 us
    all_to_all x4, starting transfers between devices, gather(): got = lax.all_to_all(copies, axes, 0, 0, tiled=True)  112 us
    ppermute x4, starting transfers between devices, swap(): return lax.ppermute(tile, axis, [(i, i ^ bit) for i in range(size)])  41.1 us
    all_to_all x4, waiting for transfers between devices, gather(): got = lax.all_to_all(copies, axes, 0, 0, tiled=True)  31.6 us
    ppermute x7, starting transfers between devices, send(): return lax.ppermute(tile, AXES, pairs)  13.2 us
    ppermute x4, waiting for transfers between devices, swap(): return lax.ppermute(tile, axis, [(i, i ^ bit) for i in range(size)])  7.9 us
    ppermute x7, waiting for transfers between devices, send(): return lax.ppermute(tile, AXES, pairs)  7.2 us
  transfers between devices with their start and end apart: 15, of which 9 were waited for; matrix products, arithmetic and copies ran while one was open for 1% of the time, Pallas kernels for 0%

profile of v2, /device:TPU:1, one launch (start us, length us, event | category | flops | bytes accessed | tf_op | source)
XLA Modules:
  0.0 343.2 jit_solution(10980652511257210586)
XLA Ops:
  0.6 0.8 convert_element_type.9
  1.5 0.7 broadcast_in_dim.18
  2.2 13.2 %all-to-all-start = ((bf16[8,1,128,128]{3,2,1,0:T(8,128)(2,1)}), bf16[8,1,128,128]{3,2,1,0:T(8,128)(2,1)S(1)}, u32[]{:S(2)}, u32[]{:S(2)}) async-start(bf16[8,1,128,128]{3,2,1,0:T(8,128)(2,1)} %broadcast_in_dim.18), calls=%async_computation | async-start | bytes 524288 | tf_op jit(solution)/shard_map/all_to_all | solution.py:38
  15.5 21.2 %collective-permute-start = (bf16[128,128]{1,0:T(8,128)(2,1)S(1)}, bf16[128,128]{1,0:T(8,128)(2,1)S(1)}, u32[]{:S(2)}, u32[]{:S(2)}) collective-permute-start(bf16[128,128]{1,0:T(8,128)(2,1)S(1)} %bitcast.97), channel_id=1, source_target_pairs={{0,4},{2,6},{4,0},{6,2},{1,5},{3,7},{5,1},{7,3},{8,12},{10,14},{12... | collective-permute-start | bytes 98312 | tf_op jit(solution)/shard_map/ppermute | solution.py:32
  36.7 3.6 %collective-permute-done = bf16[128,128]{1,0:T(8,128)(2,1)S(1)} collective-permute-done((bf16[128,128]{1,0:T(8,128)(2,1)S(1)}, bf16[128,128]{1,0:T(8,128)(2,1)S(1)}, u32[]{:S(2)}, u32[]{:S(2)}) %collective-permute-start) | collective-permute-done | bytes 32800 | tf_op jit(solution)/shard_map/ppermute | solution.py:32
  40.4 1.2 broadcast_in_dim.19
  41.6 4.4 %all-to-all-start.1 = ((bf16[4,8,128,128]{3,2,1,0:T(8,128)(2,1)}), bf16[4,8,128,128]{3,2,1,0:T(8,128)(2,1)S(1)}, u32[]{:S(2)}, u32[]{:S(2)}) async-start(bf16[4,8,128,128]{3,2,1,0:T(8,128)(2,1)} %broadcast_in_dim.19), calls=%async_computation.1 | async-start | bytes 2097152 | tf_op jit(solution)/shard_map/all_to_all | solution.py:38
  46.1 0.7 copy-done.1
  47.7 13.5 %collective-permute-start.1 = (bf16[2,128,128]{2,1,0:T(8,128)(2,1)S(1)}, bf16[2,128,128]{2,1,0:T(8,128)(2,1)S(1)}, u32[]{:S(2)}, u32[]{:S(2)}) collective-permute-start(bf16[2,128,128]{2,1,0:T(8,128)(2,1)S(1)} %pad_maximum_fusion.3), channel_id=1, source_target_pairs={{0,2},{2,0},{4,6},{6,4},{1,3},{3,1},{5,7},{7,5},{8,10},{10,8},{12,... | collective-permute-start | bytes 196616 | tf_op jit(solution)/shard_map/ppermute | solution.py:32
  61.2 2.0 collective-permute-done.1
  63.4 33.8 %all_to_all.35 = bf16[4,4,128,128]{3,2,1,0:T(8,128)(2,1)S(1)} all-to-all(bf16[4,4,128,128]{3,2,1,0:T(8,128)(2,1)S(1)} %broadcast_in_dim.21), channel_id=1, replica_groups=mesh['y'=4,'m'=4,'p'=2,'x'=4,'h'=4,'c'=2] {'x'}, dimensions={0} | all-to-all | bytes 1048576 | tf_op jit(solution)/shard_map/all_to_all | solution.py:38
  97.2 3.8 %collective-permute-start.4 = (bf16[16,128,128]{2,1,0:T(8,128)(2,1)S(1)}, bf16[16,128,128]{2,1,0:T(8,128)(2,1)S(1)}, u32[]{:S(2)}, u32[]{:S(2)}) collective-permute-start(bf16[16,128,128]{2,1,0:T(8,128)(2,1)S(1)} %bitcast.91), channel_id=1, source_target_pairs={{0,1},{1,0},{2,3},{3,2},{4,5},{5,4},{6,7},{7,6},{8,9},{9,8},{10,11... | collective-permute-start | bytes 1572872 | tf_op jit(solution)/shard_map/ppermute | solution.py:32
  101.7 0.8 collective-permute-done.4
  103.3 1.9 collective-permute-start.6
  105.9 0.8 fusion.19
  106.8 2.2 collective-permute-done.6
  109.9 1.2 broadcast_in_dim.22
  111.1 84.2 %all-to-all-start.3 = ((bf16[32,1,128,128]{3,2,1,0:T(8,128)(2,1)}), bf16[32,1,128,128]{3,2,1,0:T(8,128)(2,1)S(1)}, u32[]{:S(2)}, u32[]{:S(2)}) async-start(bf16[32,1,128,128]{3,2,1,0:T(8,128)(2,1)} %broadcast_in_dim.22), calls=%async_computation.3 | async-start | bytes 2097152 | tf_op jit(solution)/shard_map/all_to_all | solution.py:38
  195.3 2.6 collective-permute-start.7
  197.9 1.5 collective-permute-done.7
  199.7 12.5 %all-to-all-done.3 = bf16[32,1,128,128]{3,2,1,0:T(8,128)(2,1)S(1)} async-done(((bf16[32,1,128,128]{3,2,1,0:T(8,128)(2,1)}), bf16[32,1,128,128]{3,2,1,0:T(8,128)(2,1)S(1)}, u32[]{:S(2)}, u32[]{:S(2)}) %all-to-all-start.3) | async-done | bytes 1048608 | tf_op jit(solution)/shard_map/all_to_all | solution.py:38
  212.7 3.9 %collective-permute-start.8 = (f32[128,128]{1,0:T(8,128)S(1)}, f32[128,128]{1,0:T(8,128)S(1)}, u32[]{:S(2)}, u32[]{:S(2)}) collective-permute-start(f32[128,128]{1,0:T(8,128)S(1)} %fusion.21), channel_id=1, source_target_pairs={{0,0},{1,32},{2,8},{3,40},{4,16},{5,48},{6,24},{7,56},{64,256},{65... | collective-permute-start | bytes 196616 | tf_op jit(solution)/shard_map/ppermute | solution.py:27
  216.8 2.9 collective-permute-done.8
  220.8 44.3 %all_to_all.36 = bf16[32,1,128,128]{3,2,1,0:T(8,128)(2,1)S(1)} all-to-all(bf16[32,1,128,128]{3,2,1,0:T(8,128)(2,1)S(1)} %broadcast_in_dim.23), channel_id=1, replica_groups=mesh['y'=4,'m'=4,'p'=2,'x'=4,'h'=4,'c'=2] {'y','x','p'}, dimensions={0} | all-to-all | bytes 2097152 | tf_op jit(solution)/shard_map/all_to_all | solution.py:38
  265.6 4.7 %collective-permute-start.9 = (f32[128,128]{1,0:T(8,128)S(1)}, f32[128,128]{1,0:T(8,128)S(1)}, u32[]{:S(2)}, u32[]{:S(2)}) collective-permute-start(f32[128,128]{1,0:T(8,128)S(1)} %fusion.22), channel_id=1, source_target_pairs={{0,0},{1,32},{2,8},{3,40},{4,16},{5,48},{6,24},{7,56},{64,256},{65... | collective-permute-start | bytes 196616 | tf_op jit(solution)/shard_map/ppermute | solution.py:27
  271.0 2.1 collective-permute-done.9
  273.2 0.7 multiply_reduce_fusion
  273.9 2.6 broadcast_select_fusion
  276.6 34.5 %all_to_all.37 = f32[32,1,1,128]{3,2,1,0:T(1,128)S(1)} all-to-all(f32[32,1,1,128]{3,2,1,0:T(1,128)S(1)} %broadcast_in_dim.50), channel_id=1, replica_groups=mesh['y'=4,'m'=4,'p'=2,'x'=4,'h'=4,'c'=2] {'y','x','c'}, dimensions={0} | all-to-all | bytes 32768 | tf_op jit(solution)/shard_map/all_to_all | solution.py:38
  311.7 10.3 %all-to-all-start.6 = ((f32[32,1,1,128]{3,2,1,0:T(1,128)}), f32[32,1,1,128]{3,2,1,0:T(1,128)S(1)}, u32[]{:S(2)}, u32[]{:S(2)}) async-start(f32[32,1,1,128]{3,2,1,0:T(1,128)} %broadcast_in_dim.51), calls=%async_computation.6 | async-start | bytes 32768 | tf_op jit(solution)/shard_map/all_to_all | solution.py:38
  322.8 0.7 copy.51
  323.5 19.1 %all-to-all-done.6 = f32[32,1,1,128]{3,2,1,0:T(1,128)S(1)} async-done(((f32[32,1,1,128]{3,2,1,0:T(1,128)}), f32[32,1,1,128]{3,2,1,0:T(1,128)S(1)}, u32[]{:S(2)}, u32[]{:S(2)}) %all-to-all-start.6) | async-done | bytes 16416 | tf_op jit(solution)/shard_map/all_to_all | solution.py:38
  (50 shorter events, 9.3 us)
Async XLA Ops:
  2.2 13.2 %copy-start.2 = (bf16[128,128]{1,0:T(8,128)(2,1)S(1)}, bf16[128,128]{1,0:T(8,128)(2,1)}, u32[]{:S(2)}) copy-start(bf16[128,128]{1,0:T(8,128)(2,1)} %param.7) | copy-start | bytes 98308
  2.2 38.2 %all-to-all-start = ((bf16[8,1,128,128]{3,2,1,0:T(8,128)(2,1)}), bf16[8,1,128,128]{3,2,1,0:T(8,128)(2,1)S(1)}, u32[]{:S(2)}, u32[]{:S(2)}) async-start(bf16[8,1,128,128]{3,2,1,0:T(8,128)(2,1)} %broadcast_in_dim.18), calls=%async_computation | async-start | bytes 524288 | tf_op jit(solution)/shard_map/all_to_all | solution.py:38
  15.5 24.8 %collective-permute-start = (bf16[128,128]{1,0:T(8,128)(2,1)S(1)}, bf16[128,128]{1,0:T(8,128)(2,1)S(1)}, u32[]{:S(2)}, u32[]{:S(2)}) collective-permute-start(bf16[128,128]{1,0:T(8,128)(2,1)S(1)} %bitcast.97), channel_id=1, source_target_pairs={{0,4},{2,6},{4,0},{6,2},{1,5},{3,7},{5,1},{7,3},{8,12},{10,14},{12... | collective-permute-start | bytes 98312 | tf_op jit(solution)/shard_map/ppermute | solution.py:32
  41.6 4.4 %copy-start = (f32[128,128]{1,0:T(8,128)S(1)}, f32[128,128]{1,0:T(8,128)}, u32[]{:S(2)}) copy-start(f32[128,128]{1,0:T(8,128)} %param.6) | copy-start | bytes 196612
  41.6 21.6 %all-to-all-start.1 = ((bf16[4,8,128,128]{3,2,1,0:T(8,128)(2,1)}), bf16[4,8,128,128]{3,2,1,0:T(8,128)(2,1)S(1)}, u32[]{:S(2)}, u32[]{:S(2)}) async-start(bf16[4,8,128,128]{3,2,1,0:T(8,128)(2,1)} %broadcast_in_dim.19), calls=%async_computation.1 | async-start | bytes 2097152 | tf_op jit(solution)/shard_map/all_to_all | solution.py:38
  46.0 0.8 copy-start.1
  47.0 14.3 %collective-permute-start.2 = (f32[2,128,128]{1,2,0:T(8,128)S(1)}, f32[2,128,128]{1,2,0:T(8,128)S(1)}, u32[]{:S(2)}, u32[]{:S(2)}) collective-permute-start(f32[2,128,128]{1,2,0:T(8,128)S(1)} %pad_maximum_fusion.1), channel_id=1, source_target_pairs={{0,0},{1,1},{2,2},{3,3},{4,4},{5,5},{6,6},{7,7},{8,64},{9,65},{10,... | collective-permute-start | bytes 393224 | tf_op jit(solution)/shard_map/ppermute | solution.py:27
  47.7 15.5 %collective-permute-start.1 = (bf16[2,128,128]{2,1,0:T(8,128)(2,1)S(1)}, bf16[2,128,128]{2,1,0:T(8,128)(2,1)S(1)}, u32[]{:S(2)}, u32[]{:S(2)}) collective-permute-start(bf16[2,128,128]{2,1,0:T(8,128)(2,1)S(1)} %pad_maximum_fusion.3), channel_id=1, source_target_pairs={{0,2},{2,0},{4,6},{6,4},{1,3},{3,1},{5,7},{7,5},{8,10},{10,8},{12,... | collective-permute-start | bytes 196616 | tf_op jit(solution)/shard_map/ppermute | solution.py:32
  97.2 5.4 %collective-permute-start.4 = (bf16[16,128,128]{2,1,0:T(8,128)(2,1)S(1)}, bf16[16,128,128]{2,1,0:T(8,128)(2,1)S(1)}, u32[]{:S(2)}, u32[]{:S(2)}) collective-permute-start(bf16[16,128,128]{2,1,0:T(8,128)(2,1)S(1)} %bitcast.91), channel_id=1, source_target_pairs={{0,1},{1,0},{2,3},{3,2},{4,5},{5,4},{6,7},{7,6},{8,9},{9,8},{10,11... | collective-permute-start | bytes 1572872 | tf_op jit(solution)/shard_map/ppermute | solution.py:32
  101.0 5.7 %collective-permute-start.3 = (bf16[16,128,128]{2,1,0:T(8,128)(2,1)S(1)}, bf16[16,128,128]{2,1,0:T(8,128)(2,1)S(1)}, u32[]{:S(2)}, u32[]{:S(2)}) collective-permute-start(bf16[16,128,128]{2,1,0:T(8,128)(2,1)S(1)} %bitcast.92), channel_id=1, source_target_pairs={{0,0},{1,1},{2,2},{3,3},{4,4},{5,5},{6,6},{7,7},{8,64},{9,65},{10,... | collective-permute-start | bytes 1572872 | tf_op jit(solution)/shard_map/ppermute | solution.py:27
  103.3 5.6 %collective-permute-start.6 = (f32[128,128]{1,0:T(8,128)S(1)}, f32[128,128]{1,0:T(8,128)S(1)}, u32[]{:S(2)}, u32[]{:S(2)}) collective-permute-start(f32[128,128]{1,0:T(8,128)S(1)} %fusion.20), channel_id=1, source_target_pairs={{0,0},{1,32},{2,8},{3,40},{4,16},{5,48},{6,24},{7,56},{8,256},{9,2... | collective-permute-start | bytes 196616 | tf_op jit(solution)/shard_map/ppermute | solution.py:27
  105.3 1.5 collective-permute-start.5
  111.1 101.1 %all-to-all-start.3 = ((bf16[32,1,128,128]{3,2,1,0:T(8,128)(2,1)}), bf16[32,1,128,128]{3,2,1,0:T(8,128)(2,1)S(1)}, u32[]{:S(2)}, u32[]{:S(2)}) async-start(bf16[32,1,128,128]{3,2,1,0:T(8,128)(2,1)} %broadcast_in_dim.22), calls=%async_computation.3 | async-start | bytes 2097152 | tf_op jit(solution)/shard_map/all_to_all | solution.py:38
  195.3 4.1 %collective-permute-start.7 = (bf16[16,128,128]{2,1,0:T(8,128)(2,1)S(1)}, bf16[16,128,128]{2,1,0:T(8,128)(2,1)S(1)}, u32[]{:S(2)}, u32[]{:S(2)}) collective-permute-start(bf16[16,128,128]{2,1,0:T(8,128)(2,1)S(1)} %collective-permute-done.3), channel_id=1, source_target_pairs={{0,1},{1,0},{2,3},{3,2},{4,5},{5,4},{6,7},{7,6},{8,9},{9,8},{10,11... | collective-permute-start | bytes 1572872 | tf_op jit(solution)/shard_map/ppermute | solution.py:32
  212.7 6.9 %collective-permute-start.8 = (f32[128,128]{1,0:T(8,128)S(1)}, f32[128,128]{1,0:T(8,128)S(1)}, u32[]{:S(2)}, u32[]{:S(2)}) collective-permute-start(f32[128,128]{1,0:T(8,128)S(1)} %fusion.21), channel_id=1, source_target_pairs={{0,0},{1,32},{2,8},{3,40},{4,16},{5,48},{6,24},{7,56},{64,256},{65... | collective-permute-start | bytes 196616 | tf_op jit(solution)/shard_map/ppermute | solution.py:27
  265.6 7.6 %collective-permute-start.9 = (f32[128,128]{1,0:T(8,128)S(1)}, f32[128,128]{1,0:T(8,128)S(1)}, u32[]{:S(2)}, u32[]{:S(2)}) collective-permute-start(f32[128,128]{1,0:T(8,128)S(1)} %fusion.22), channel_id=1, source_target_pairs={{0,0},{1,32},{2,8},{3,40},{4,16},{5,48},{6,24},{7,56},{64,256},{65... | collective-permute-start | bytes 196616 | tf_op jit(solution)/shard_map/ppermute | solution.py:27
  311.7 30.9 %all-to-all-start.6 = ((f32[32,1,1,128]{3,2,1,0:T(1,128)}), f32[32,1,1,128]{3,2,1,0:T(1,128)S(1)}, u32[]{:S(2)}, u32[]{:S(2)}) async-start(f32[32,1,1,128]{3,2,1,0:T(1,128)} %broadcast_in_dim.51), calls=%async_computation.6 | async-start | bytes 32768 | tf_op jit(solution)/shard_map/all_to_all | solution.py:38
  322.1 0.7 collective-permute-start.10

commit v3 on v1

--- a/solution.py
+++ b/solution.py
@@ -33,12 +33,6 @@
     return lax.ppermute(tile, AXES, pairs)
 
 
-def gather_amps(low):
-    by_l = gather(low, "l", 8)
-    by_y = gather(by_l, "y", 4)
-    return by_y.reshape(-1, low.shape[1])
-
-
 def body(amplitudes, coupling, source, orbital_gaps):
     n = amplitudes.shape[0]
     h = lax.axis_index("h")
@@ -67,14 +61,22 @@
     squares = []
     for step in range(ITERS):
         if step:
-            amp_cols = gather_amps(amps.astype(jnp.bfloat16))
-        product = lax.dot_general(
-            coupling_rows,
-            amp_cols,
-            (((0,), (0,)), ((), ())),
-            preferred_element_type=jnp.float32,
-        )
-        paired = product + transpose_tiles(product).T
+            by_l = gather(amps.astype(jnp.bfloat16), "l", 8).reshape(-1, n)
+            shares = jnp.einsum("ykr,kc->yrc", coupling_part, by_l, preferred_element_type=jnp.float32)
+            product = jnp.sum(lax.all_to_all(shares, "y", 0, 0, tiled=True), axis=0)
+            mirror = transpose_tiles(product)
+        else:
+            product = lax.dot_general(
+                coupling_rows,
+                amp_cols,
+                (((0,), (0,)), ((), ())),
+                preferred_element_type=jnp.float32,
+            )
+            mirror = transpose_tiles(product)
+            parts = coupling_rows.reshape(4, -1, n)
+            coupling_part = lax.all_to_all(parts, "y", 0, 0, tiled=True)
+            mirror, coupling_part = lax.optimization_barrier((mirror, coupling_part))
+        paired = product + mirror.T
         residual = source + delta * amps + paired + amps * paired
         squares.append(jnp.sum(residual * residual))
         amps = amps - residual / delta

time: 302 us -> 291 us (0.964)
  blocking collectives: 155 us -> 125 us
  starting transfers between devices: 99.7 us -> 109 us
  waiting for transfers between devices: 32.6 us -> 40.2 us
    all_to_all x6 -> x4, blocking collectives: 155 us -> 95.8 us  [gather(): return lax.all_to_all(copies, axes, 0, 0, tiled=True)]
    all_to_all x0 -> x2, blocking collectives: none -> 29.2 us  [body(): product = jnp.sum(lax.all_to_all(shares, 'y', 0, 0, tiled=True), axis=0)]
    all_to_all x0 -> x1, waiting for transfers between devices: none -> 6.79 us  [body(): coupling_part = lax.all_to_all(parts, 'y', 0, 0, tiled=True)]
    all_to_all x0 -> x1, starting transfers between devices: none -> 5.22 us  [body(): coupling_part = lax.all_to_all(parts, 'y', 0, 0, tiled=True)]
    ppermute x3, starting transfers between devices: 16.9 us -> 21.3 us  [transpose_tiles(): return lax.ppermute(tile, AXES, pairs)]
  transfers between devices with their start and end apart: 9 -> 10, of which waited for: 7 -> 8; matrix products, arithmetic and copies ran while one was open for 1% -> 1% of each run, Pallas kernels for 0% -> 0%
where the time goes in v3:
time: 291 us; the launch traced here: 290 us
  blocking collectives  125 us (43%)
  starting transfers between devices  109 us (37%)
  waiting for transfers between devices  40.2 us (14%)
  other arithmetic  8.97 us (3%)
  local copies, waits for them, and re-layouts  3.97 us (1%)
    all_to_all x4, blocking collectives, gather(): return lax.all_to_all(copies, axes, 0, 0, tiled=True)  95.8 us
    ppermute x3, starting transfers between devices, swap(): return lax.ppermute(tile, axis, [(i, i ^ bit) for i in range(size)])  41.4 us
    all_to_all x3, starting transfers between devices, gather(): return lax.all_to_all(copies, axes, 0, 0, tiled=True)  40.8 us
    all_to_all x2, blocking collectives, body(): product = jnp.sum(lax.all_to_all(shares, 'y', 0, 0, tiled=True), axis=0)  29.2 us
    ppermute x3, starting transfers between devices, transpose_tiles(): return lax.ppermute(tile, AXES, pairs)  21.3 us
    all_to_all x3, waiting for transfers between devices, gather(): return lax.all_to_all(copies, axes, 0, 0, tiled=True)  19.9 us
    all_to_all x1, waiting for transfers between devices, body(): coupling_part = lax.all_to_all(parts, 'y', 0, 0, tiled=True)  6.79 us
    ppermute x3, waiting for transfers between devices, swap(): return lax.ppermute(tile, axis, [(i, i ^ bit) for i in range(size)])  6.77 us
  transfers between devices with their start and end apart: 10, of which 8 were waited for; matrix products, arithmetic and copies ran while one was open for 1% of the time, Pallas kernels for 0%

profile of v3, /device:TPU:1, one launch (start us, length us, event | category | flops | bytes accessed | tf_op | source)
XLA Modules:
  0.0 290.4 jit_solution(12496813040264532293)
XLA Ops:
  0.6 0.8 convert_element_type.9
  2.2 13.2 %all-to-all-start = ((bf16[8,128,128]{2,1,0:T(8,128)(2,1)}), bf16[8,128,128]{2,1,0:T(8,128)(2,1)S(1)}, u32[]{:S(2)}, u32[]{:S(2)}) async-start(bf16[8,128,128]{2,1,0:T(8,128)(2,1)} %broadcast_in_dim.18), calls=%async_computation | async-start | bytes 524288 | tf_op jit(solution)/shard_map/all_to_all | solution.py:19
  15.5 21.2 %collective-permute-start = (bf16[128,128]{1,0:T(8,128)(2,1)S(1)}, bf16[128,128]{1,0:T(8,128)(2,1)S(1)}, u32[]{:S(2)}, u32[]{:S(2)}) collective-permute-start(bf16[128,128]{1,0:T(8,128)(2,1)S(1)} %bitcast.71), channel_id=1, source_target_pairs={{0,4},{2,6},{4,0},{6,2},{1,5},{3,7},{5,1},{7,3},{8,12},{10,14},{12... | collective-permute-start | bytes 98312 | tf_op jit(solution)/shard_map/ppermute | solution.py:23
  36.7 3.6 %collective-permute-done = bf16[128,128]{1,0:T(8,128)(2,1)S(1)} collective-permute-done((bf16[128,128]{1,0:T(8,128)(2,1)S(1)}, bf16[128,128]{1,0:T(8,128)(2,1)S(1)}, u32[]{:S(2)}, u32[]{:S(2)}) %collective-permute-start) | collective-permute-done | bytes 32800 | tf_op jit(solution)/shard_map/ppermute | solution.py:23
  40.4 1.2 broadcast_in_dim.19
  41.6 4.3 %all-to-all-start.1 = ((bf16[4,8,128,128]{3,2,1,0:T(8,128)(2,1)}), bf16[4,8,128,128]{3,2,1,0:T(8,128)(2,1)S(1)}, u32[]{:S(2)}, u32[]{:S(2)}) async-start(bf16[4,8,128,128]{3,2,1,0:T(8,128)(2,1)} %broadcast_in_dim.19), calls=%async_computation.1 | async-start | bytes 2097152 | tf_op jit(solution)/shard_map/all_to_all | solution.py:19
  45.9 13.5 %collective-permute-start.1 = (bf16[2,128,128]{2,1,0:T(8,128)(2,1)S(1)}, bf16[2,128,128]{2,1,0:T(8,128)(2,1)S(1)}, u32[]{:S(2)}, u32[]{:S(2)}) collective-permute-start(bf16[2,128,128]{2,1,0:T(8,128)(2,1)S(1)} %pad_maximum_fusion.2), channel_id=1, source_target_pairs={{0,2},{2,0},{4,6},{6,4},{1,3},{3,1},{5,7},{7,5},{8,10},{10,8},{12,... | collective-permute-start | bytes 196616 | tf_op jit(solution)/shard_map/ppermute | solution.py:23
  59.4 1.6 collective-permute-done.1
  61.2 10.7 %all_to_all.50 = bf16[4,4,128,128]{3,2,1,0:T(8,128)(2,1)S(1)} all-to-all(bf16[4,4,128,128]{3,2,1,0:T(8,128)(2,1)S(1)} %broadcast_in_dim.21), channel_id=1, replica_groups=mesh['y'=4,'l'=8,'x'=4,'h'=4,'c'=2] {'x'}, dimensions={0} | all-to-all | bytes 1048576 | tf_op jit(solution)/shard_map/all_to_all | solution.py:19
  71.9 6.7 %collective-permute-start.2 = (bf16[16,128,128]{2,1,0:T(8,128)(2,1)S(1)}, bf16[16,128,128]{2,1,0:T(8,128)(2,1)S(1)}, u32[]{:S(2)}, u32[]{:S(2)}) collective-permute-start(bf16[16,128,128]{2,1,0:T(8,128)(2,1)S(1)} %bitcast.67), channel_id=1, source_target_pairs={{0,1},{1,0},{2,3},{3,2},{4,5},{5,4},{6,7},{7,6},{8,9},{9,8},{10,11... | collective-permute-start | bytes 1572872 | tf_op jit(solution)/shard_map/ppermute | solution.py:23
  78.6 1.5 collective-permute-done.2
  80.2 1.1 pad_maximum_fusion
  81.3 5.2 %all-to-all-start.3 = ((bf16[4,1024,128]{2,1,0:T(8,128)(2,1)}), bf16[4,1024,128]{2,1,0:T(8,128)(2,1)S(1)}, u32[]{:S(2)}, u32[]{:S(2)}) async-start(bf16[4,1024,128]{2,1,0:T(8,128)(2,1)} %bitcast.15), calls=%async_computation.3 | async-start | bytes 2097152 | tf_op jit(solution)/shard_map/all_to_all | solution.py:77
  86.5 1.7 fusion.20
  88.4 3.5 %collective-permute-start.3 = (f32[128,128]{0,1:T(8,128)S(1)}, f32[128,128]{0,1:T(8,128)S(1)}, u32[]{:S(2)}, u32[]{:S(2)}) collective-permute-start(f32[128,128]{0,1:T(8,128)S(1)} %copy.36), channel_id=1, source_target_pairs={{0,0},{1,32},{2,64},{3,96},{4,128},{5,160},{6,192},{7,224},{8,256}... | collective-permute-start | bytes 196616 | tf_op jit(solution)/shard_map/ppermute | solution.py:33
  91.9 0.8 fusion.19
  92.8 1.5 collective-permute-done.3
  94.3 6.8 %all-to-all-done.3 = bf16[4,1024,128]{2,1,0:T(8,128)(2,1)S(1)} async-done(((bf16[4,1024,128]{2,1,0:T(8,128)(2,1)}), bf16[4,1024,128]{2,1,0:T(8,128)(2,1)S(1)}, u32[]{:S(2)}, u32[]{:S(2)}) %all-to-all-start.3) | async-done | bytes 1048608 | tf_op jit(solution)/shard_map/all_to_all | solution.py:77
  101.9 41.5 %all_to_all.51 = bf16[8,128,128]{2,1,0:T(8,128)(2,1)S(1)} all-to-all(bf16[8,128,128]{2,1,0:T(8,128)(2,1)S(1)} %broadcast_in_dim.22), channel_id=1, replica_groups=mesh['y'=4,'l'=8,'x'=4,'h'=4,'c'=2] {'l'}, dimensions={0} | all-to-all | bytes 524288 | tf_op jit(solution)/shard_map/all_to_all | solution.py:19
  143.9 17.4 %all_to_all.52 = f32[4,128,128]{2,1,0:T(8,128)S(1)} all-to-all(f32[4,128,128]{2,1,0:T(8,128)S(1)} %fusion.21), channel_id=1, replica_groups=mesh['y'=4,'l'=8,'x'=4,'h'=4,'c'=2] {'y'}, dimensions={0} | all-to-all | bytes 524288 | tf_op jit(solution)/shard_map/all_to_all | solution.py:66
  161.4 7.5 %collective-permute-start.4 = (f32[128,128]{0,1:T(8,128)S(1)}, f32[128,128]{0,1:T(8,128)S(1)}, u32[]{:S(2)}, u32[]{:S(2)}) collective-permute-start(f32[128,128]{0,1:T(8,128)S(1)} %copy.38), channel_id=1, source_target_pairs={{0,0},{1,32},{2,64},{3,96},{4,128},{5,160},{6,192},{7,224},{8,256}... | collective-permute-start | bytes 196616 | tf_op jit(solution)/shard_map/ppermute | solution.py:33
  168.9 3.3 %collective-permute-done.4 = f32[128,128]{0,1:T(8,128)S(1)} collective-permute-done((f32[128,128]{0,1:T(8,128)S(1)}, f32[128,128]{0,1:T(8,128)S(1)}, u32[]{:S(2)}, u32[]{:S(2)}) %collective-permute-start.4) | collective-permute-done | bytes 65568 | tf_op jit(solution)/shard_map/ppermute | solution.py:33
  173.1 29.5 %all_to_all.53 = bf16[8,128,128]{2,1,0:T(8,128)(2,1)S(1)} all-to-all(bf16[8,128,128]{2,1,0:T(8,128)(2,1)S(1)} %broadcast_in_dim.23), channel_id=1, replica_groups=mesh['y'=4,'l'=8,'x'=4,'h'=4,'c'=2] {'l'}, dimensions={0} | all-to-all | bytes 524288 | tf_op jit(solution)/shard_map/all_to_all | solution.py:19
  203.1 11.8 %all_to_all.54 = f32[4,128,128]{2,1,0:T(8,128)S(1)} all-to-all(f32[4,128,128]{2,1,0:T(8,128)S(1)} %fusion.22), channel_id=1, replica_groups=mesh['y'=4,'l'=8,'x'=4,'h'=4,'c'=2] {'y'}, dimensions={0} | all-to-all | bytes 524288 | tf_op jit(solution)/shard_map/all_to_all | solution.py:66
  215.0 10.3 %collective-permute-start.5 = (f32[128,128]{0,1:T(8,128)S(1)}, f32[128,128]{0,1:T(8,128)S(1)}, u32[]{:S(2)}, u32[]{:S(2)}) collective-permute-start(f32[128,128]{0,1:T(8,128)S(1)} %copy.40), channel_id=1, source_target_pairs={{0,0},{1,32},{2,64},{3,96},{4,128},{5,160},{6,192},{7,224},{8,256}... | collective-permute-start | bytes 196616 | tf_op jit(solution)/shard_map/ppermute | solution.py:33
  225.9 2.0 collective-permute-done.5
  227.9 0.8 multiply_reduce_fusion
  228.7 2.6 broadcast_select_fusion
  231.3 14.0 %all_to_all.55 = f32[32,1,128]{2,1,0:T(1,128)S(1)} all-to-all(f32[32,1,128]{2,1,0:T(1,128)S(1)} %broadcast_in_dim.25), channel_id=1, replica_groups=mesh['y'=4,'l'=8,'x'=4,'h'=4,'c'=2] {'y','x','c'}, dimensions={0} | all-to-all | bytes 32768 | tf_op jit(solution)/shard_map/all_to_all | solution.py:19
  245.9 23.3 %all-to-all-start.9 = ((f32[32,1,128]{2,1,0:T(1,128)}), f32[32,1,128]{2,1,0:T(1,128)S(1)}, u32[]{:S(2)}, u32[]{:S(2)}) async-start(f32[32,1,128]{2,1,0:T(1,128)} %broadcast_in_dim.26), calls=%async_computation.9 | async-start | bytes 32768 | tf_op jit(solution)/shard_map/all_to_all | solution.py:19
  269.2 0.7 fusion.11
  269.9 19.9 %all-to-all-done.9 = f32[32,1,128]{2,1,0:T(1,128)S(1)} async-done(((f32[32,1,128]{2,1,0:T(1,128)}), f32[32,1,128]{2,1,0:T(1,128)S(1)}, u32[]{:S(2)}, u32[]{:S(2)}) %all-to-all-start.9) | async-done | bytes 16416 | tf_op jit(solution)/shard_map/all_to_all | solution.py:19
  (36 shorter events, 5.8 us)
Async XLA Ops:
  2.2 13.2 %copy-start.2 = (bf16[128,128]{1,0:T(8,128)(2,1)S(1)}, bf16[128,128]{1,0:T(8,128)(2,1)}, u32[]{:S(2)}) copy-start(bf16[128,128]{1,0:T(8,128)(2,1)} %param.7) | copy-start | bytes 98308
  2.2 38.2 %all-to-all-start = ((bf16[8,128,128]{2,1,0:T(8,128)(2,1)}), bf16[8,128,128]{2,1,0:T(8,128)(2,1)S(1)}, u32[]{:S(2)}, u32[]{:S(2)}) async-start(bf16[8,128,128]{2,1,0:T(8,128)(2,1)} %broadcast_in_dim.18), calls=%async_computation | async-start | bytes 524288 | tf_op jit(solution)/shard_map/all_to_all | solution.py:19
  15.5 24.8 %collective-permute-start = (bf16[128,128]{1,0:T(8,128)(2,1)S(1)}, bf16[128,128]{1,0:T(8,128)(2,1)S(1)}, u32[]{:S(2)}, u32[]{:S(2)}) collective-permute-start(bf16[128,128]{1,0:T(8,128)(2,1)S(1)} %bitcast.71), channel_id=1, source_target_pairs={{0,4},{2,6},{4,0},{6,2},{1,5},{3,7},{5,1},{7,3},{8,12},{10,14},{12... | collective-permute-start | bytes 98312 | tf_op jit(solution)/shard_map/ppermute | solution.py:23
  41.6 19.5 %all-to-all-start.1 = ((bf16[4,8,128,128]{3,2,1,0:T(8,128)(2,1)}), bf16[4,8,128,128]{3,2,1,0:T(8,128)(2,1)S(1)}, u32[]{:S(2)}, u32[]{:S(2)}) async-start(bf16[4,8,128,128]{3,2,1,0:T(8,128)(2,1)} %broadcast_in_dim.19), calls=%async_computation.1 | async-start | bytes 2097152 | tf_op jit(solution)/shard_map/all_to_all | solution.py:19
  45.9 15.2 %collective-permute-start.1 = (bf16[2,128,128]{2,1,0:T(8,128)(2,1)S(1)}, bf16[2,128,128]{2,1,0:T(8,128)(2,1)S(1)}, u32[]{:S(2)}, u32[]{:S(2)}) collective-permute-start(bf16[2,128,128]{2,1,0:T(8,128)(2,1)S(1)} %pad_maximum_fusion.2), channel_id=1, source_target_pairs={{0,2},{2,0},{4,6},{6,4},{1,3},{3,1},{5,7},{7,5},{8,10},{10,8},{12,... | collective-permute-start | bytes 196616 | tf_op jit(solution)/shard_map/ppermute | solution.py:23
  71.9 8.2 %collective-permute-start.2 = (bf16[16,128,128]{2,1,0:T(8,128)(2,1)S(1)}, bf16[16,128,128]{2,1,0:T(8,128)(2,1)S(1)}, u32[]{:S(2)}, u32[]{:S(2)}) collective-permute-start(bf16[16,128,128]{2,1,0:T(8,128)(2,1)S(1)} %bitcast.67), channel_id=1, source_target_pairs={{0,1},{1,0},{2,3},{3,2},{4,5},{5,4},{6,7},{7,6},{8,9},{9,8},{10,11... | collective-permute-start | bytes 1572872 | tf_op jit(solution)/shard_map/ppermute | solution.py:23
  81.3 19.7 %all-to-all-start.3 = ((bf16[4,1024,128]{2,1,0:T(8,128)(2,1)}), bf16[4,1024,128]{2,1,0:T(8,128)(2,1)S(1)}, u32[]{:S(2)}, u32[]{:S(2)}) async-start(bf16[4,1024,128]{2,1,0:T(8,128)(2,1)} %bitcast.15), calls=%async_computation.3 | async-start | bytes 2097152 | tf_op jit(solution)/shard_map/all_to_all | solution.py:77
  88.3 12.8 %copy-start = (f32[128,128]{1,0:T(8,128)S(1)}, f32[128,128]{1,0:T(8,128)}, u32[]{:S(2)}) copy-start(f32[128,128]{1,0:T(8,128)} %param.8) | copy-start | bytes 196612
  88.3 12.8 %copy-start.1 = (f32[128,128]{1,0:T(8,128)S(1)}, f32[128,128]{1,0:T(8,128)}, u32[]{:S(2)}) copy-start(f32[128,128]{1,0:T(8,128)} %param.6) | copy-start | bytes 196612
  88.4 5.9 %collective-permute-start.3 = (f32[128,128]{0,1:T(8,128)S(1)}, f32[128,128]{0,1:T(8,128)S(1)}, u32[]{:S(2)}, u32[]{:S(2)}) collective-permute-start(f32[128,128]{0,1:T(8,128)S(1)} %copy.36), channel_id=1, source_target_pairs={{0,0},{1,32},{2,64},{3,96},{4,128},{5,160},{6,192},{7,224},{8,256}... | collective-permute-start | bytes 196616 | tf_op jit(solution)/shard_map/ppermute | solution.py:33
  161.4 10.8 %collective-permute-start.4 = (f32[128,128]{0,1:T(8,128)S(1)}, f32[128,128]{0,1:T(8,128)S(1)}, u32[]{:S(2)}, u32[]{:S(2)}) collective-permute-start(f32[128,128]{0,1:T(8,128)S(1)} %copy.38), channel_id=1, source_target_pairs={{0,0},{1,32},{2,64},{3,96},{4,128},{5,160},{6,192},{7,224},{8,256}... | collective-permute-start | bytes 196616 | tf_op jit(solution)/shard_map/ppermute | solution.py:33
  215.0 12.9 %collective-permute-start.5 = (f32[128,128]{0,1:T(8,128)S(1)}, f32[128,128]{0,1:T(8,128)S(1)}, u32[]{:S(2)}, u32[]{:S(2)}) collective-permute-start(f32[128,128]{0,1:T(8,128)S(1)} %copy.40), channel_id=1, source_target_pairs={{0,0},{1,32},{2,64},{3,96},{4,128},{5,160},{6,192},{7,224},{8,256}... | collective-permute-start | bytes 196616 | tf_op jit(solution)/shard_map/ppermute | solution.py:33
  245.9 43.9 %all-to-all-start.9 = ((f32[32,1,128]{2,1,0:T(1,128)}), f32[32,1,128]{2,1,0:T(1,128)S(1)}, u32[]{:S(2)}, u32[]{:S(2)}) async-start(f32[32,1,128]{2,1,0:T(1,128)} %broadcast_in_dim.26), calls=%async_computation.9 | async-start | bytes 32768 | tf_op jit(solution)/shard_map/all_to_all | solution.py:19

commit v4 on v3

--- a/solution.py
+++ b/solution.py
@@ -72,6 +72,7 @@
                 (((0,), (0,)), ((), ())),
                 preferred_element_type=jnp.float32,
             )
+            product, coupling_rows = lax.optimization_barrier((product, coupling_rows))
             mirror = transpose_tiles(product)
             parts = coupling_rows.reshape(4, -1, n)
             coupling_part = lax.all_to_all(parts, "y", 0, 0, tiled=True)
@@ -81,8 +82,11 @@
         squares.append(jnp.sum(residual * residual))
         amps = amps - residual / delta
 
+    amps, squares = lax.optimization_barrier((amps, squares))
+    lane = lax.broadcasted_iota(jnp.int32, (1, 128), 1)
     local = jnp.zeros((1, 128), jnp.float32)
-    local = local.at[0, :ITERS].set(jnp.stack(squares))
+    for step, square in enumerate(squares):
+        local = jnp.where(lane == step, square, local)
     plane = jnp.sum(gather(local, ("y", "x", "c"), 32), axis=0)
     total = jnp.sum(gather(plane, ("l", "h"), 32), axis=0)
     norms = jnp.sqrt(total[0, :ITERS]) / (NO * NV)

time: 291 us -> 291 us (level)
  blocking collectives: 125 us -> 167 us
  starting transfers between devices: 109 us -> 84.4 us
  waiting for transfers between devices: 40.2 us -> 24.1 us
    all_to_all x4 -> x5, blocking collectives: 95.8 us -> 140 us  [gather(): return lax.all_to_all(copies, axes, 0, 0, tiled=True)]
    all_to_all x3 -> x2, starting transfers between devices: 40.8 us -> 17.5 us  [gather(): return lax.all_to_all(copies, axes, 0, 0, tiled=True)]
    all_to_all x3 -> x2, waiting for transfers between devices: 19.9 us -> 0.01 us  [gather(): return lax.all_to_all(copies, axes, 0, 0, tiled=True)]
  transfers between devices with their start and end apart: 10 -> 9, of which waited for: 8 -> 7; matrix products, arithmetic and copies ran while one was open for 1% -> 0% of each run, Pallas kernels for 0% -> 0%
where the time goes in v4:
time: 291 us; the launch traced here: 290 us
  blocking collectives  167 us (57%)
  starting transfers between devices  84.4 us (29%)
  waiting for transfers between devices  24.1 us (8%)
  other arithmetic  7.54 us (3%)
  local copies, waits for them, and re-layouts  3.35 us (1%)
    all_to_all x5, blocking collectives, gather(): return lax.all_to_all(copies, axes, 0, 0, tiled=True)  140 us
    ppermute x3, starting transfers between devices, swap(): return lax.ppermute(tile, axis, [(i, i ^ bit) for i in range(size)])  41.4 us
    all_to_all x2, blocking collectives, body(): product = jnp.sum(lax.all_to_all(shares, 'y', 0, 0, tiled=True), axis=0)  26.8 us
    ppermute x3, starting transfers between devices, transpose_tiles(): return lax.ppermute(tile, AXES, pairs)  20.3 us
    all_to_all x2, starting transfers between devices, gather(): return lax.all_to_all(copies, axes, 0, 0, tiled=True)  17.5 us
    ppermute x3, waiting for transfers between devices, transpose_tiles(): return lax.ppermute(tile, AXES, pairs)  8.78 us
    all_to_all x1, waiting for transfers between devices, body(): coupling_part = lax.all_to_all(parts, 'y', 0, 0, tiled=True)  8.54 us
    ppermute x3, waiting for transfers between devices, swap(): return lax.ppermute(tile, axis, [(i, i ^ bit) for i in range(size)])  6.77 us
  transfers between devices with their start and end apart: 9, of which 7 were waited for; matrix products, arithmetic and copies ran while one was open for 0% of the time, Pallas kernels for 0%

profile of v4, /device:TPU:1, one launch (start us, length us, event | category | flops | bytes accessed | tf_op | source)
XLA Modules:
  0.0 289.7 jit_solution(1940493592539979134)
XLA Ops:
  0.6 0.8 convert_element_type.9
  1.5 0.7 broadcast_in_dim.28
  2.2 13.2 %all-to-all-start = ((bf16[8,128,128]{2,1,0:T(8,128)(2,1)}), bf16[8,128,128]{2,1,0:T(8,128)(2,1)S(1)}, u32[]{:S(2)}, u32[]{:S(2)}) async-start(bf16[8,128,128]{2,1,0:T(8,128)(2,1)} %broadcast_in_dim.28), calls=%async_computation | async-start | bytes 524288 | tf_op jit(solution)/shard_map/all_to_all | solution.py:19
  15.5 21.2 %collective-permute-start = (bf16[128,128]{1,0:T(8,128)(2,1)S(1)}, bf16[128,128]{1,0:T(8,128)(2,1)S(1)}, u32[]{:S(2)}, u32[]{:S(2)}) collective-permute-start(bf16[128,128]{1,0:T(8,128)(2,1)S(1)} %bitcast.67), channel_id=1, source_target_pairs={{0,4},{2,6},{4,0},{6,2},{1,5},{3,7},{5,1},{7,3},{8,12},{10,14},{12... | collective-permute-start | bytes 98312 | tf_op jit(solution)/shard_map/ppermute | solution.py:23
  36.7 3.6 %collective-permute-done = bf16[128,128]{1,0:T(8,128)(2,1)S(1)} collective-permute-done((bf16[128,128]{1,0:T(8,128)(2,1)S(1)}, bf16[128,128]{1,0:T(8,128)(2,1)S(1)}, u32[]{:S(2)}, u32[]{:S(2)}) %collective-permute-start) | collective-permute-done | bytes 32800 | tf_op jit(solution)/shard_map/ppermute | solution.py:23
  40.4 1.2 broadcast_in_dim.29
  41.6 4.3 %all-to-all-start.1 = ((bf16[4,8,128,128]{3,2,1,0:T(8,128)(2,1)}), bf16[4,8,128,128]{3,2,1,0:T(8,128)(2,1)S(1)}, u32[]{:S(2)}, u32[]{:S(2)}) async-start(bf16[4,8,128,128]{3,2,1,0:T(8,128)(2,1)} %broadcast_in_dim.29), calls=%async_computation.1 | async-start | bytes 2097152 | tf_op jit(solution)/shard_map/all_to_all | solution.py:19
  45.9 13.5 %collective-permute-start.1 = (bf16[2,128,128]{2,1,0:T(8,128)(2,1)S(1)}, bf16[2,128,128]{2,1,0:T(8,128)(2,1)S(1)}, u32[]{:S(2)}, u32[]{:S(2)}) collective-permute-start(bf16[2,128,128]{2,1,0:T(8,128)(2,1)S(1)} %pad_maximum_fusion.2), channel_id=1, source_target_pairs={{0,2},{2,0},{4,6},{6,4},{1,3},{3,1},{5,7},{7,5},{8,10},{10,8},{12,... | collective-permute-start | bytes 196616 | tf_op jit(solution)/shard_map/ppermute | solution.py:23
  59.4 1.6 collective-permute-done.1
  61.2 10.7 %all_to_all.50 = bf16[4,4,128,128]{3,2,1,0:T(8,128)(2,1)S(1)} all-to-all(bf16[4,4,128,128]{3,2,1,0:T(8,128)(2,1)S(1)} %broadcast_in_dim.31), channel_id=1, replica_groups=mesh['y'=4,'l'=8,'x'=4,'h'=4,'c'=2] {'x'}, dimensions={0} | all-to-all | bytes 1048576 | tf_op jit(solution)/shard_map/all_to_all | solution.py:19
  71.9 6.7 %collective-permute-start.2 = (bf16[16,128,128]{2,1,0:T(8,128)(2,1)S(1)}, bf16[16,128,128]{2,1,0:T(8,128)(2,1)S(1)}, u32[]{:S(2)}, u32[]{:S(2)}) collective-permute-start(bf16[16,128,128]{2,1,0:T(8,128)(2,1)S(1)} %bitcast.63), channel_id=1, source_target_pairs={{0,1},{1,0},{2,3},{3,2},{4,5},{5,4},{6,7},{7,6},{8,9},{9,8},{10,11... | collective-permute-start | bytes 1572872 | tf_op jit(solution)/shard_map/ppermute | solution.py:23
  78.6 1.5 collective-permute-done.2
  80.2 1.1 pad_maximum_fusion
  81.3 1.7 fusion.20
  83.0 5.2 %all-to-all-start.3 = ((bf16[4,1024,128]{2,1,0:T(8,128)(2,1)}), bf16[4,1024,128]{2,1,0:T(8,128)(2,1)S(1)}, u32[]{:S(2)}, u32[]{:S(2)}) async-start(bf16[4,1024,128]{2,1,0:T(8,128)(2,1)} %bitcast.15), calls=%async_computation.3 | async-start | bytes 2097152 | tf_op jit(solution)/shard_map/all_to_all | solution.py:78
  88.3 3.5 %collective-permute-start.3 = (f32[128,128]{0,1:T(8,128)S(1)}, f32[128,128]{0,1:T(8,128)S(1)}, u32[]{:S(2)}, u32[]{:S(2)}) collective-permute-start(f32[128,128]{0,1:T(8,128)S(1)} %copy.36), channel_id=1, source_target_pairs={{0,0},{1,32},{2,64},{3,96},{4,128},{5,160},{6,192},{7,224},{8,256}... | collective-permute-start | bytes 196616 | tf_op jit(solution)/shard_map/ppermute | solution.py:33
  91.9 0.8 fusion.19
  92.7 1.5 collective-permute-done.3
  94.2 8.5 %all-to-all-done.3 = bf16[4,1024,128]{2,1,0:T(8,128)(2,1)S(1)} async-done(((bf16[4,1024,128]{2,1,0:T(8,128)(2,1)}), bf16[4,1024,128]{2,1,0:T(8,128)(2,1)S(1)}, u32[]{:S(2)}, u32[]{:S(2)}) %all-to-all-start.3) | async-done | bytes 1048608 | tf_op jit(solution)/shard_map/all_to_all | solution.py:78
  103.6 39.7 %all_to_all.51 = bf16[8,128,128]{2,1,0:T(8,128)(2,1)S(1)} all-to-all(bf16[8,128,128]{2,1,0:T(8,128)(2,1)S(1)} %broadcast_in_dim.62), channel_id=1, replica_groups=mesh['y'=4,'l'=8,'x'=4,'h'=4,'c'=2] {'l'}, dimensions={0} | all-to-all | bytes 524288 | tf_op jit(solution)/shard_map/all_to_all | solution.py:19
  143.8 17.4 %all_to_all.52 = f32[4,128,128]{2,1,0:T(8,128)S(1)} all-to-all(f32[4,128,128]{2,1,0:T(8,128)S(1)} %fusion.21), channel_id=1, replica_groups=mesh['y'=4,'l'=8,'x'=4,'h'=4,'c'=2] {'y'}, dimensions={0} | all-to-all | bytes 524288 | tf_op jit(solution)/shard_map/all_to_all | solution.py:66
  161.4 7.5 %collective-permute-start.4 = (f32[128,128]{0,1:T(8,128)S(1)}, f32[128,128]{0,1:T(8,128)S(1)}, u32[]{:S(2)}, u32[]{:S(2)}) collective-permute-start(f32[128,128]{0,1:T(8,128)S(1)} %copy.38), channel_id=1, source_target_pairs={{0,0},{1,32},{2,64},{3,96},{4,128},{5,160},{6,192},{7,224},{8,256}... | collective-permute-start | bytes 196616 | tf_op jit(solution)/shard_map/ppermute | solution.py:33
  168.9 4.7 %collective-permute-done.4 = f32[128,128]{0,1:T(8,128)S(1)} collective-permute-done((f32[128,128]{0,1:T(8,128)S(1)}, f32[128,128]{0,1:T(8,128)S(1)}, u32[]{:S(2)}, u32[]{:S(2)}) %collective-permute-start.4) | collective-permute-done | bytes 65568 | tf_op jit(solution)/shard_map/ppermute | solution.py:33
  173.5 0.7 multiply_reduce_fusion.1
  174.4 32.5 %all_to_all.53 = bf16[8,128,128]{2,1,0:T(8,128)(2,1)S(1)} all-to-all(bf16[8,128,128]{2,1,0:T(8,128)(2,1)S(1)} %broadcast_in_dim.63), channel_id=1, replica_groups=mesh['y'=4,'l'=8,'x'=4,'h'=4,'c'=2] {'l'}, dimensions={0} | all-to-all | bytes 524288 | tf_op jit(solution)/shard_map/all_to_all | solution.py:19
  207.4 9.3 %all_to_all.54 = f32[4,128,128]{2,1,0:T(8,128)S(1)} all-to-all(f32[4,128,128]{2,1,0:T(8,128)S(1)} %fusion.22), channel_id=1, replica_groups=mesh['y'=4,'l'=8,'x'=4,'h'=4,'c'=2] {'y'}, dimensions={0} | all-to-all | bytes 524288 | tf_op jit(solution)/shard_map/all_to_all | solution.py:66
  216.9 9.2 %collective-permute-start.5 = (f32[128,128]{0,1:T(8,128)S(1)}, f32[128,128]{0,1:T(8,128)S(1)}, u32[]{:S(2)}, u32[]{:S(2)}) collective-permute-start(f32[128,128]{0,1:T(8,128)S(1)} %copy.40), channel_id=1, source_target_pairs={{0,0},{1,32},{2,64},{3,96},{4,128},{5,160},{6,192},{7,224},{8,256}... | collective-permute-start | bytes 196616 | tf_op jit(solution)/shard_map/ppermute | solution.py:33
  226.1 2.6 collective-permute-done.5
  229.4 0.7 fusion.11
  230.2 1.9 compare_select_fusion.2
  232.1 13.7 %all_to_all.55 = f32[32,1,128]{2,1,0:T(1,128)S(1)} all-to-all(f32[32,1,128]{2,1,0:T(1,128)S(1)} %broadcast_in_dim.68), channel_id=1, replica_groups=mesh['y'=4,'l'=8,'x'=4,'h'=4,'c'=2] {'y','x','c'}, dimensions={0} | all-to-all | bytes 32768 | tf_op jit(solution)/shard_map/all_to_all | solution.py:19
  245.8 43.4 %all_to_all.56 = f32[32,1,128]{2,1,0:T(1,128)S(1)} all-to-all(f32[32,1,128]{2,1,0:T(1,128)S(1)} %broadcast_in_dim.69), channel_id=1, replica_groups=mesh['y'=4,'l'=8,'x'=4,'h'=4,'c'=2] {'l','h'}, dimensions={0} | all-to-all | bytes 32768 | tf_op jit(solution)/shard_map/all_to_all | solution.py:19
  (33 shorter events, 3.8 us)
Async XLA Ops:
  2.2 13.2 %copy-start.2 = (bf16[128,128]{1,0:T(8,128)(2,1)S(1)}, bf16[128,128]{1,0:T(8,128)(2,1)}, u32[]{:S(2)}) copy-start(bf16[128,128]{1,0:T(8,128)(2,1)} %param.5) | copy-start | bytes 98308
  2.2 38.2 %all-to-all-start = ((bf16[8,128,128]{2,1,0:T(8,128)(2,1)}), bf16[8,128,128]{2,1,0:T(8,128)(2,1)S(1)}, u32[]{:S(2)}, u32[]{:S(2)}) async-start(bf16[8,128,128]{2,1,0:T(8,128)(2,1)} %broadcast_in_dim.28), calls=%async_computation | async-start | bytes 524288 | tf_op jit(solution)/shard_map/all_to_all | solution.py:19
  15.5 24.8 %collective-permute-start = (bf16[128,128]{1,0:T(8,128)(2,1)S(1)}, bf16[128,128]{1,0:T(8,128)(2,1)S(1)}, u32[]{:S(2)}, u32[]{:S(2)}) collective-permute-start(bf16[128,128]{1,0:T(8,128)(2,1)S(1)} %bitcast.67), channel_id=1, source_target_pairs={{0,4},{2,6},{4,0},{6,2},{1,5},{3,7},{5,1},{7,3},{8,12},{10,14},{12... | collective-permute-start | bytes 98312 | tf_op jit(solution)/shard_map/ppermute | solution.py:23
  41.6 19.5 %all-to-all-start.1 = ((bf16[4,8,128,128]{3,2,1,0:T(8,128)(2,1)}), bf16[4,8,128,128]{3,2,1,0:T(8,128)(2,1)S(1)}, u32[]{:S(2)}, u32[]{:S(2)}) async-start(bf16[4,8,128,128]{3,2,1,0:T(8,128)(2,1)} %broadcast_in_dim.29), calls=%async_computation.1 | async-start | bytes 2097152 | tf_op jit(solution)/shard_map/all_to_all | solution.py:19
  45.9 15.2 %collective-permute-start.1 = (bf16[2,128,128]{2,1,0:T(8,128)(2,1)S(1)}, bf16[2,128,128]{2,1,0:T(8,128)(2,1)S(1)}, u32[]{:S(2)}, u32[]{:S(2)}) collective-permute-start(bf16[2,128,128]{2,1,0:T(8,128)(2,1)S(1)} %pad_maximum_fusion.2), channel_id=1, source_target_pairs={{0,2},{2,0},{4,6},{6,4},{1,3},{3,1},{5,7},{7,5},{8,10},{10,8},{12,... | collective-permute-start | bytes 196616 | tf_op jit(solution)/shard_map/ppermute | solution.py:23
  71.9 8.2 %collective-permute-start.2 = (bf16[16,128,128]{2,1,0:T(8,128)(2,1)S(1)}, bf16[16,128,128]{2,1,0:T(8,128)(2,1)S(1)}, u32[]{:S(2)}, u32[]{:S(2)}) collective-permute-start(bf16[16,128,128]{2,1,0:T(8,128)(2,1)S(1)} %bitcast.63), channel_id=1, source_target_pairs={{0,1},{1,0},{2,3},{3,2},{4,5},{5,4},{6,7},{7,6},{8,9},{9,8},{10,11... | collective-permute-start | bytes 1572872 | tf_op jit(solution)/shard_map/ppermute | solution.py:23
  83.0 19.8 %all-to-all-start.3 = ((bf16[4,1024,128]{2,1,0:T(8,128)(2,1)}), bf16[4,1024,128]{2,1,0:T(8,128)(2,1)S(1)}, u32[]{:S(2)}, u32[]{:S(2)}) async-start(bf16[4,1024,128]{2,1,0:T(8,128)(2,1)} %bitcast.15), calls=%async_computation.3 | async-start | bytes 2097152 | tf_op jit(solution)/shard_map/all_to_all | solution.py:78
  88.2 14.5 %copy-start = (f32[128,128]{1,0:T(8,128)S(1)}, f32[128,128]{1,0:T(8,128)}, u32[]{:S(2)}) copy-start(f32[128,128]{1,0:T(8,128)} %param.6) | copy-start | bytes 196612
  88.2 14.5 %copy-start.1 = (f32[128,128]{1,0:T(8,128)S(1)}, f32[128,128]{1,0:T(8,128)}, u32[]{:S(2)}) copy-start(f32[128,128]{1,0:T(8,128)} %param.4) | copy-start | bytes 196612
  88.3 5.9 %collective-permute-start.3 = (f32[128,128]{0,1:T(8,128)S(1)}, f32[128,128]{0,1:T(8,128)S(1)}, u32[]{:S(2)}, u32[]{:S(2)}) collective-permute-start(f32[128,128]{0,1:T(8,128)S(1)} %copy.36), channel_id=1, source_target_pairs={{0,0},{1,32},{2,64},{3,96},{4,128},{5,160},{6,192},{7,224},{8,256}... | collective-permute-start | bytes 196616 | tf_op jit(solution)/shard_map/ppermute | solution.py:33
  161.4 12.2 %collective-permute-start.4 = (f32[128,128]{0,1:T(8,128)S(1)}, f32[128,128]{0,1:T(8,128)S(1)}, u32[]{:S(2)}, u32[]{:S(2)}) collective-permute-start(f32[128,128]{0,1:T(8,128)S(1)} %copy.38), channel_id=1, source_target_pairs={{0,0},{1,32},{2,64},{3,96},{4,128},{5,160},{6,192},{7,224},{8,256}... | collective-permute-start | bytes 196616 | tf_op jit(solution)/shard_map/ppermute | solution.py:33
  216.9 11.9 %collective-permute-start.5 = (f32[128,128]{0,1:T(8,128)S(1)}, f32[128,128]{0,1:T(8,128)S(1)}, u32[]{:S(2)}, u32[]{:S(2)}) collective-permute-start(f32[128,128]{0,1:T(8,128)S(1)} %copy.40), channel_id=1, source_target_pairs={{0,0},{1,32},{2,64},{3,96},{4,128},{5,160},{6,192},{7,224},{8,256}... | collective-permute-start | bytes 196616 | tf_op jit(solution)/shard_map/ppermute | solution.py:33

commit v5 on v4

v5 whole, which is shorter than its diff:
```python
import jax
import jax.numpy as jnp
import numpy as np
from jax import lax
from jax.sharding import Mesh, PartitionSpec as P

NO = 16
NV = 256
ITERS = 3

AXES = ("y", "l", "x", "h", "c")
SIZES = (4, 8, 4, 4, 2)
SIDE = 32
ROW = ("y", "l")
COL = ("x", "h", "c")


def gather(tile, axes, count):
    copies = jnp.broadcast_to(tile[None], (count,) + tile.shape)
    return lax.all_to_all(copies, axes, 0, 0, tiled=True)


def swap(tile, axis, size, bit):
    return lax.ppermute(tile, axis, [(i, i ^ bit) for i in range(size)])


def ordered(own, other, bit):
    first = bit == 0
    return jnp.stack([jnp.where(first, own, other), jnp.where(first, other, own)])


def places():
    grid = np.arange(SIDE * SIDE).reshape(SIZES)
    return grid.reshape(SIDE, SIDE), grid.transpose(2, 1, 0, 3, 4).reshape(SIDE, SIDE)


def send(tile, source, target):
    return lax.ppermute(tile, AXES, list(zip(source.ravel().tolist(), target.ravel().tolist())))


def body(amplitudes, coupling, source, orbital_gaps):
    n = amplitudes.shape[0]
    h = lax.axis_index("h")
    start, turned = places()

    block = coupling.T
    far = swap(block, "h", 4, 2)
    low = send(amplitudes.astype(jnp.bfloat16), start, turned)
    far, low = lax.optimization_barrier((far, low))
    pair = ordered(block, far, h // 2)
    near = swap(pair, "h", 4, 1)
    by_l = gather(low, "l", 8).reshape(-1, n)
    near, by_l = lax.optimization_barrier((near, by_l))
    state = send(jnp.stack([source, amplitudes]), start, turned)
    quad = jnp.swapaxes(ordered(pair, near, h % 2), 0, 1).reshape(4, n, n)
    by_y = gather(quad, "y", 4).reshape(16, n, n)
    other = swap(by_y, "c", 2, 1)
    both = ordered(by_y, other, lax.axis_index("c"))
    part = jnp.swapaxes(both, 0, 1).reshape(4, -1, n)

    source, amps = state[0], state[1]
    gap_rows = lax.dynamic_slice_in_dim(orbital_gaps, lax.axis_index(("x", "l")) * n, n)
    gap_cols = lax.dynamic_slice_in_dim(orbital_gaps, lax.axis_index(("y", "h", "c")) * n, n)
    delta = gap_rows[:, None] + gap_cols[None, :]
    squares = []
    for step in range(ITERS):
        if step:
            by_l = gather(amps.astype(jnp.bfloat16), "l", 8).reshape(-1, n)
        shares = jnp.einsum("ykr,kc->yrc", part, by_l, preferred_element_type=jnp.float32)
        product = jnp.sum(lax.all_to_all(shares, "x", 0, 0, tiled=True), axis=0)
        paired = product + send(product, turned, turned.T).T
        residual = source + delta * amps + paired + amps * paired
        squares.append(jnp.sum(residual * residual))
        amps = amps - residual / delta

    lane = lax.broadcasted_iota(jnp.int32, (1, 128), 1)
    local = jnp.zeros((1, 128), jnp.float32)
    for step, square in enumerate(squares):
        local = jnp.where(lane == step, square, local)
    plane = jnp.sum(gather(local, ("y", "x", "c"), 32), axis=0)
    total = jnp.sum(gather(plane, ("l", "h"), 32), axis=0)
    norms = jnp.sqrt(total[0, :ITERS]) / (NO * NV)
    return (send(amps, turned, start), norms)


def solution(mesh):
    fine = Mesh(mesh.devices.reshape(SIZES), AXES)
    in_specs = (P(ROW, COL), P(ROW, COL), P(ROW, COL), P())
    out_specs = (P(ROW, COL), P())
    return jax.shard_map(body, mesh=fine, in_specs=in_specs, out_specs=out_specs, check_vma=False)
```

time: 291 us -> 290 us (level)
  blocking collectives: 167 us -> 125 us
  starting transfers between devices: 84.4 us -> 118 us
  waiting for transfers between devices: 24.1 us -> 34.2 us
    all_to_all x5 -> x4, blocking collectives: 140 us -> 101 us  [gather(): return lax.all_to_all(copies, axes, 0, 0, tiled=True)]
    all_to_all x2, waiting for transfers between devices: 0.01 us -> 19.8 us  [gather(): return lax.all_to_all(copies, axes, 0, 0, tiled=True)]
    ppermute x3, starting transfers between devices: 41.4 us -> 58.6 us  [swap(): return lax.ppermute(tile, axis, [(i, i ^ bit) for i in range(size)])]
    all_to_all x2, starting transfers between devices: 17.5 us -> 27.5 us  [gather(): return lax.all_to_all(copies, axes, 0, 0, tiled=True)]
    ppermute x3 -> x6, starting transfers between devices: 20.3 us -> 28.5 us  [send(): lax.ppermute(tile, AXES, list(zip(source.ravel().tolist(), target.ravel()...]
    ppermute x3 -> x6, waiting for transfers between devices: 8.78 us -> 4.96 us  [send(): lax.ppermute(tile, AXES, list(zip(source.ravel().tolist(), target.ravel()...]
    all_to_all x2, blocking collectives: 26.8 us -> 23.5 us  [body(): product = jnp.sum(lax.all_to_all(shares, 'x', 0, 0, tiled=True), axis=0)]
    all_to_all x1, waiting for transfers between devices: 8.54 us -> 5.37 us  [body(): product = jnp.sum(lax.all_to_all(shares, 'x', 0, 0, tiled=True), axis=0)]
  transfers between devices with their start and end apart: 9 -> 12, of which waited for: 7 -> 8; matrix products, arithmetic and copies ran while one was open for 0% -> 0% of each run, Pallas kernels for 0% -> 0%
where the time goes in v5:
time: 290 us; the launch traced here: 289 us
  blocking collectives  125 us (43%)
  starting transfers between devices  118 us (41%)
  waiting for transfers between devices  34.2 us (12%)
  other arithmetic  5.21 us (2%)
  local copies, waits for them, and re-layouts  4.15 us (1%)
    all_to_all x4, blocking collectives, gather(): return lax.all_to_all(copies, axes, 0, 0, tiled=True)  101 us
    ppermute x3, starting transfers between devices, swap(): return lax.ppermute(tile, axis, [(i, i ^ bit) for i in range(size)])  58.6 us
    ppermute x6, starting transfers between devices, send(): lax.ppermute(tile, AXES, list(zip(source.ravel().tolist(), target.ravel()...  28.5 us
    all_to_all x2, starting transfers between devices, gather(): return lax.all_to_all(copies, axes, 0, 0, tiled=True)  27.5 us
    all_to_all x2, blocking collectives, body(): product = jnp.sum(lax.all_to_all(shares, 'x', 0, 0, tiled=True), axis=0)  23.5 us
    all_to_all x2, waiting for transfers between devices, gather(): return lax.all_to_all(copies, axes, 0, 0, tiled=True)  19.8 us
  transfers between devices with their start and end apart: 12, of which 8 were waited for; matrix products, arithmetic and copies ran while one was open for 0% of the time, Pallas kernels for 0%

profile of v5, /device:TPU:1, one launch (start us, length us, event | category | flops | bytes accessed | tf_op | source)
XLA Modules:
  0.0 289.3 jit_solution(11913006430035818796)
XLA Ops:
  0.6 0.9 copy.36
  1.5 29.5 %collective-permute-start.1 = (bf16[128,128]{1,0:T(8,128)(2,1)S(1)}, bf16[128,128]{1,0:T(8,128)(2,1)S(1)}, u32[]{:S(2)}, u32[]{:S(2)}) collective-permute-start(bf16[128,128]{1,0:T(8,128)(2,1)S(1)} %bitcast.93), channel_id=1, source_target_pairs={{0,4},{2,6},{4,0},{6,2},{1,5},{3,7},{5,1},{7,3},{8,12},{10,14},{12... | collective-permute-start | bytes 98312 | tf_op jit(solution)/shard_map/ppermute | solution.py:24
  31.8 0.8 collective-permute-done.1
  32.6 0.7 broadcast_in_dim.26
  33.3 5.0 %all-to-all-start = ((bf16[8,128,128]{2,1,0:T(8,128)(2,1)}), bf16[8,128,128]{2,1,0:T(8,128)(2,1)S(1)}, u32[]{:S(2)}, u32[]{:S(2)}) async-start(bf16[8,128,128]{2,1,0:T(8,128)(2,1)} %broadcast_in_dim.26), calls=%async_computation | async-start | bytes 524288 | tf_op jit(solution)/shard_map/all_to_all | solution.py:20
  38.4 16.1 %collective-permute-start.3 = (bf16[2,128,128]{2,1,0:T(8,128)(2,1)S(1)}, bf16[2,128,128]{2,1,0:T(8,128)(2,1)S(1)}, u32[]{:S(2)}, u32[]{:S(2)}) collective-permute-start(bf16[2,128,128]{2,1,0:T(8,128)(2,1)S(1)} %pad_maximum_fusion.3), channel_id=1, source_target_pairs={{0,2},{2,0},{4,6},{6,4},{1,3},{3,1},{5,7},{7,5},{8,10},{10,8},{12,... | collective-permute-start | bytes 196616 | tf_op jit(solution)/shard_map/ppermute | solution.py:24
  54.5 1.8 collective-permute-done.3
  56.4 13.7 %all_to_all.45 = bf16[4,4,128,128]{3,2,1,0:T(8,128)(2,1)S(1)} all-to-all(bf16[4,4,128,128]{3,2,1,0:T(8,128)(2,1)S(1)} %broadcast_in_dim.54), channel_id=1, replica_groups=mesh['y'=4,'l'=8,'x'=4,'h'=4,'c'=2] {'y'}, dimensions={0} | all-to-all | bytes 1048576 | tf_op jit(solution)/shard_map/all_to_all | solution.py:20
  70.2 12.9 %collective-permute-start.4 = (bf16[16,128,128]{2,1,0:T(8,128)(2,1)S(1)}, bf16[16,128,128]{2,1,0:T(8,128)(2,1)S(1)}, u32[]{:S(2)}, u32[]{:S(2)}) collective-permute-start(bf16[16,128,128]{2,1,0:T(8,128)(2,1)S(1)} %bitcast.87), channel_id=1, source_target_pairs={{0,1},{1,0},{2,3},{3,2},{4,5},{5,4},{6,7},{7,6},{8,9},{9,8},{10,11... | collective-permute-start | bytes 1572872 | tf_op jit(solution)/shard_map/ppermute | solution.py:24
  83.1 1.5 collective-permute-done.4
  84.8 1.2 fusion
  86.0 3.5 %all-to-all-start.2 = ((f32[4,128,128]{2,1,0:T(8,128)}), f32[4,128,128]{2,1,0:T(8,128)S(1)}, u32[]{:S(2)}, u32[]{:S(2)}) async-start(f32[4,128,128]{2,1,0:T(8,128)} %fusion), calls=%async_computation.2 | async-start | bytes 524288 | tf_op jit(solution)/shard_map/all_to_all | solution.py:70
  89.5 0.7 collective-permute-start
  90.2 5.4 %all-to-all-done.2 = f32[4,128,128]{2,1,0:T(8,128)S(1)} async-done(((f32[4,128,128]{2,1,0:T(8,128)}), f32[4,128,128]{2,1,0:T(8,128)S(1)}, u32[]{:S(2)}, u32[]{:S(2)}) %all-to-all-start.2) | async-done | bytes 262176 | tf_op jit(solution)/shard_map/all_to_all | solution.py:70
  95.7 5.7 %collective-permute-start.5 = (f32[128,128]{0,1:T(8,128)S(1)}, f32[128,128]{0,1:T(8,128)S(1)}, u32[]{:S(2)}, u32[]{:S(2)}) collective-permute-start(f32[128,128]{0,1:T(8,128)S(1)} %copy.40), channel_id=1, source_target_pairs={{0,0},{1,32},{2,64},{3,96},{4,128},{5,160},{6,192},{7,224},{256,8}... | collective-permute-start | bytes 196616 | tf_op jit(solution)/shard_map/ppermute | solution.py:38
  101.4 0.8 fusion.21
  102.2 1.1 collective-permute-done.5
  103.3 0.7 multiply_reduce_fusion
  104.2 34.8 %all_to_all.46 = bf16[8,128,128]{2,1,0:T(8,128)(2,1)S(1)} all-to-all(bf16[8,128,128]{2,1,0:T(8,128)(2,1)S(1)} %broadcast_in_dim.55), channel_id=1, replica_groups=mesh['y'=4,'l'=8,'x'=4,'h'=4,'c'=2] {'l'}, dimensions={0} | all-to-all | bytes 524288 | tf_op jit(solution)/shard_map/all_to_all | solution.py:20
  139.4 11.5 %all_to_all.47 = f32[4,128,128]{2,1,0:T(8,128)S(1)} all-to-all(f32[4,128,128]{2,1,0:T(8,128)S(1)} %fusion.22), channel_id=1, replica_groups=mesh['y'=4,'l'=8,'x'=4,'h'=4,'c'=2] {'x'}, dimensions={0} | all-to-all | bytes 524288 | tf_op jit(solution)/shard_map/all_to_all | solution.py:70
  151.0 10.2 %collective-permute-start.6 = (f32[128,128]{0,1:T(8,128)S(1)}, f32[128,128]{0,1:T(8,128)S(1)}, u32[]{:S(2)}, u32[]{:S(2)}) collective-permute-start(f32[128,128]{0,1:T(8,128)S(1)} %copy.42), channel_id=1, source_target_pairs={{0,0},{1,32},{2,64},{3,96},{4,128},{5,160},{6,192},{7,224},{256,8}... | collective-permute-start | bytes 196616 | tf_op jit(solution)/shard_map/ppermute | solution.py:38
  161.3 1.9 collective-permute-done.6
  163.2 0.7 multiply_reduce_fusion.1
  164.0 28.9 %all_to_all.48 = bf16[8,128,128]{2,1,0:T(8,128)(2,1)S(1)} all-to-all(bf16[8,128,128]{2,1,0:T(8,128)(2,1)S(1)} %broadcast_in_dim.56), channel_id=1, replica_groups=mesh['y'=4,'l'=8,'x'=4,'h'=4,'c'=2] {'l'}, dimensions={0} | all-to-all | bytes 524288 | tf_op jit(solution)/shard_map/all_to_all | solution.py:20
  193.4 11.9 %all_to_all.49 = f32[4,128,128]{2,1,0:T(8,128)S(1)} all-to-all(f32[4,128,128]{2,1,0:T(8,128)S(1)} %fusion.23), channel_id=1, replica_groups=mesh['y'=4,'l'=8,'x'=4,'h'=4,'c'=2] {'x'}, dimensions={0} | all-to-all | bytes 524288 | tf_op jit(solution)/shard_map/all_to_all | solution.py:70
  205.4 10.6 %collective-permute-start.7 = (f32[128,128]{0,1:T(8,128)S(1)}, f32[128,128]{0,1:T(8,128)S(1)}, u32[]{:S(2)}, u32[]{:S(2)}) collective-permute-start(f32[128,128]{0,1:T(8,128)S(1)} %copy.44), channel_id=1, source_target_pairs={{0,0},{1,32},{2,64},{3,96},{4,128},{5,160},{6,192},{7,224},{256,8}... | collective-permute-start | bytes 196616 | tf_op jit(solution)/shard_map/ppermute | solution.py:38
  216.0 1.9 collective-permute-done.7
  218.0 0.8 multiply_reduce_fusion.2
  218.7 1.9 compare_select_fusion.2
  220.7 23.8 %all_to_all.50 = f32[32,1,128]{2,1,0:T(1,128)S(1)} all-to-all(f32[32,1,128]{2,1,0:T(1,128)S(1)} %broadcast_in_dim.61), channel_id=1, replica_groups=mesh['y'=4,'l'=8,'x'=4,'h'=4,'c'=2] {'y','x','c'}, dimensions={0} | all-to-all | bytes 32768 | tf_op jit(solution)/shard_map/all_to_all | solution.py:20
  245.1 22.5 %all-to-all-start.8 = ((f32[32,1,128]{2,1,0:T(1,128)}), f32[32,1,128]{2,1,0:T(1,128)S(1)}, u32[]{:S(2)}, u32[]{:S(2)}) async-start(f32[32,1,128]{2,1,0:T(1,128)} %broadcast_in_dim.62), calls=%async_computation.8 | async-start | bytes 32768 | tf_op jit(solution)/shard_map/all_to_all | solution.py:20
  268.3 19.8 %all-to-all-done.8 = f32[32,1,128]{2,1,0:T(1,128)S(1)} async-done(((f32[32,1,128]{2,1,0:T(1,128)}), f32[32,1,128]{2,1,0:T(1,128)S(1)}, u32[]{:S(2)}, u32[]{:S(2)}) %all-to-all-start.8) | async-done | bytes 16416 | tf_op jit(solution)/shard_map/all_to_all | solution.py:20
  (38 shorter events, 5.1 us)
Async XLA Ops:
  0.6 30.4 %copy-start = (f32[128,128]{1,0:T(8,128)S(1)}, f32[128,128]{1,0:T(8,128)}, u32[]{:S(2)}) copy-start(f32[128,128]{1,0:T(8,128)} %param.4) | copy-start | bytes 196612
  1.5 31.0 %collective-permute-start.1 = (bf16[128,128]{1,0:T(8,128)(2,1)S(1)}, bf16[128,128]{1,0:T(8,128)(2,1)S(1)}, u32[]{:S(2)}, u32[]{:S(2)}) collective-permute-start(bf16[128,128]{1,0:T(8,128)(2,1)S(1)} %bitcast.93), channel_id=1, source_target_pairs={{0,4},{2,6},{4,0},{6,2},{1,5},{3,7},{5,1},{7,3},{8,12},{10,14},{12... | collective-permute-start | bytes 98312 | tf_op jit(solution)/shard_map/ppermute | solution.py:24
  31.1 1.5 collective-permute-start.2
  33.3 23.0 %all-to-all-start = ((bf16[8,128,128]{2,1,0:T(8,128)(2,1)}), bf16[8,128,128]{2,1,0:T(8,128)(2,1)S(1)}, u32[]{:S(2)}, u32[]{:S(2)}) async-start(bf16[8,128,128]{2,1,0:T(8,128)(2,1)} %broadcast_in_dim.26), calls=%async_computation | async-start | bytes 524288 | tf_op jit(solution)/shard_map/all_to_all | solution.py:20
  38.4 17.9 %collective-permute-start.3 = (bf16[2,128,128]{2,1,0:T(8,128)(2,1)S(1)}, bf16[2,128,128]{2,1,0:T(8,128)(2,1)S(1)}, u32[]{:S(2)}, u32[]{:S(2)}) collective-permute-start(bf16[2,128,128]{2,1,0:T(8,128)(2,1)S(1)} %pad_maximum_fusion.3), channel_id=1, source_target_pairs={{0,2},{2,0},{4,6},{6,4},{1,3},{3,1},{5,7},{7,5},{8,10},{10,8},{12,... | collective-permute-start | bytes 196616 | tf_op jit(solution)/shard_map/ppermute | solution.py:24
  70.2 14.4 %collective-permute-start.4 = (bf16[16,128,128]{2,1,0:T(8,128)(2,1)S(1)}, bf16[16,128,128]{2,1,0:T(8,128)(2,1)S(1)}, u32[]{:S(2)}, u32[]{:S(2)}) collective-permute-start(bf16[16,128,128]{2,1,0:T(8,128)(2,1)S(1)} %bitcast.87), channel_id=1, source_target_pairs={{0,1},{1,0},{2,3},{3,2},{4,5},{5,4},{6,7},{7,6},{8,9},{9,8},{10,11... | collective-permute-start | bytes 1572872 | tf_op jit(solution)/shard_map/ppermute | solution.py:24
  86.0 3.5 %copy-start.1 = (f32[128,128]{1,0:T(8,128)S(1)}, f32[128,128]{1,0:T(8,128)}, u32[]{:S(2)}) copy-start(f32[128,128]{1,0:T(8,128)} %param.6) | copy-start | bytes 196612
  86.0 9.6 %all-to-all-start.2 = ((f32[4,128,128]{2,1,0:T(8,128)}), f32[4,128,128]{2,1,0:T(8,128)S(1)}, u32[]{:S(2)}, u32[]{:S(2)}) async-start(f32[4,128,128]{2,1,0:T(8,128)} %fusion), calls=%async_computation.2 | async-start | bytes 524288 | tf_op jit(solution)/shard_map/all_to_all | solution.py:70
  89.5 12.7 %collective-permute-start = (f32[2,128,128]{2,1,0:T(8,128)S(1)}, f32[2,128,128]{2,1,0:T(8,128)S(1)}, u32[]{:S(2)}, u32[]{:S(2)}) collective-permute-start(f32[2,128,128]{2,1,0:T(8,128)S(1)} %pad_maximum_fusion.1), channel_id=1, source_target_pairs={{0,0},{1,1},{2,2},{3,3},{4,4},{5,5},{6,6},{7,7},{8,256},{9,257},{1... | collective-permute-start | bytes 393224 | tf_op jit(solution)/shard_map/ppermute | solution.py:38
  95.7 7.6 %collective-permute-start.5 = (f32[128,128]{0,1:T(8,128)S(1)}, f32[128,128]{0,1:T(8,128)S(1)}, u32[]{:S(2)}, u32[]{:S(2)}) collective-permute-start(f32[128,128]{0,1:T(8,128)S(1)} %copy.40), channel_id=1, source_target_pairs={{0,0},{1,32},{2,64},{3,96},{4,128},{5,160},{6,192},{7,224},{256,8}... | collective-permute-start | bytes 196616 | tf_op jit(solution)/shard_map/ppermute | solution.py:38
  151.0 12.2 %collective-permute-start.6 = (f32[128,128]{0,1:T(8,128)S(1)}, f32[128,128]{0,1:T(8,128)S(1)}, u32[]{:S(2)}, u32[]{:S(2)}) collective-permute-start(f32[128,128]{0,1:T(8,128)S(1)} %copy.42), channel_id=1, source_target_pairs={{0,0},{1,32},{2,64},{3,96},{4,128},{5,160},{6,192},{7,224},{256,8}... | collective-permute-start | bytes 196616 | tf_op jit(solution)/shard_map/ppermute | solution.py:38
  205.4 12.5 %collective-permute-start.7 = (f32[128,128]{0,1:T(8,128)S(1)}, f32[128,128]{0,1:T(8,128)S(1)}, u32[]{:S(2)}, u32[]{:S(2)}) collective-permute-start(f32[128,128]{0,1:T(8,128)S(1)} %copy.44), channel_id=1, source_target_pairs={{0,0},{1,32},{2,64},{3,96},{4,128},{5,160},{6,192},{7,224},{256,8}... | collective-permute-start | bytes 196616 | tf_op jit(solution)/shard_map/ppermute | solution.py:38
  245.1 43.1 %all-to-all-start.8 = ((f32[32,1,128]{2,1,0:T(1,128)}), f32[32,1,128]{2,1,0:T(1,128)S(1)}, u32[]{:S(2)}, u32[]{:S(2)}) async-start(f32[32,1,128]{2,1,0:T(1,128)} %broadcast_in_dim.62), calls=%async_computation.8 | async-start | bytes 32768 | tf_op jit(solution)/shard_map/all_to_all | solution.py:20
  267.7 0.7 collective-permute-start.8

commit v6 on v5

--- a/solution.py
+++ b/solution.py
@@ -13,6 +13,7 @@
 SIDE = 32
 ROW = ("y", "l")
 COL = ("x", "h", "c")
+SHIFT = (0, 0, 0, 2)
 
 
 def gather(tile, axes, count):
@@ -31,7 +32,10 @@
 
 def places():
     grid = np.arange(SIDE * SIDE).reshape(SIZES)
-    return grid.reshape(SIDE, SIDE), grid.transpose(2, 1, 0, 3, 4).reshape(SIDE, SIDE)
+    later = np.zeros(SIZES, np.int64)
+    for y, l, x, h, c in np.ndindex(SIZES):
+        later[y, l, x, h, c] = grid[(x + SHIFT[h]) % SIZES[0], l, y, h, c]
+    return grid.reshape(SIDE, SIDE), later.reshape(SIDE, SIDE)
 
 
 def send(tile, source, target):
@@ -44,23 +48,22 @@
     start, turned = places()
 
     block = coupling.T
-    far = swap(block, "h", 4, 2)
     low = send(amplitudes.astype(jnp.bfloat16), start, turned)
-    far, low = lax.optimization_barrier((far, low))
-    pair = ordered(block, far, h // 2)
-    near = swap(pair, "h", 4, 1)
+    quad = gather(block, "h", 4)
+    low, quad = lax.optimization_barrier((low, quad))
+    by_y = gather(quad.reshape(4, n, n), "y", 4).reshape(16, n, n)
+    by_y, low = lax.optimization_barrier((by_y, low))
     by_l = gather(low, "l", 8).reshape(-1, n)
-    near, by_l = lax.optimization_barrier((near, by_l))
     state = send(jnp.stack([source, amplitudes]), start, turned)
-    quad = jnp.swapaxes(ordered(pair, near, h % 2), 0, 1).reshape(4, n, n)
-    by_y = gather(quad, "y", 4).reshape(16, n, n)
     other = swap(by_y, "c", 2, 1)
     both = ordered(by_y, other, lax.axis_index("c"))
     part = jnp.swapaxes(both, 0, 1).reshape(4, -1, n)
 
     source, amps = state[0], state[1]
     gap_rows = lax.dynamic_slice_in_dim(orbital_gaps, lax.axis_index(("x", "l")) * n, n)
-    gap_cols = lax.dynamic_slice_in_dim(orbital_gaps, lax.axis_index(("y", "h", "c")) * n, n)
+    shift = sum(jnp.where(h == i, SHIFT[i], 0) for i in range(SIZES[3]))
+    col = (lax.axis_index("y") - shift + 4) % 4 * 8 + lax.axis_index(("h", "c"))
+    gap_cols = lax.dynamic_slice_in_dim(orbital_gaps, col * n, n)
     delta = gap_rows[:, None] + gap_cols[None, :]
     squares = []
     for step in range(ITERS):

time: 290 us -> 279 us (0.962)
  blocking collectives: 125 us -> 95.7 us
  waiting for transfers between devices: 34.2 us -> 55.3 us
  starting transfers between devices: 118 us -> 114 us
    ppermute x3 -> x1, starting transfers between devices: 58.6 us -> 7.69 us  [swap(): return lax.ppermute(tile, axis, [(i, i ^ bit) for i in range(size)])]
    all_to_all x2 -> x3, starting transfers between devices: 27.5 us -> 59.3 us  [gather(): return lax.all_to_all(copies, axes, 0, 0, tiled=True)]
    all_to_all x2 -> x3, waiting for transfers between devices: 19.8 us -> 44 us  [gather(): return lax.all_to_all(copies, axes, 0, 0, tiled=True)]
    all_to_all x4, blocking collectives: 101 us -> 78.3 us  [gather(): return lax.all_to_all(copies, axes, 0, 0, tiled=True)]
    ppermute x6, starting transfers between devices: 28.5 us -> 42.7 us  [send(): lax.ppermute(tile, AXES, list(zip(source.ravel().tolist(), target.ravel()...]
    all_to_all x2, blocking collectives: 23.5 us -> 17.3 us  [body(): product = jnp.sum(lax.all_to_all(shares, 'x', 0, 0, tiled=True), axis=0)]
  transfers between devices with their start and end apart: 12 -> 11, of which waited for: 8 -> 8; matrix products, arithmetic and copies ran while one was open for 0% -> 0% of each run, Pallas kernels for 0% -> 0%
where the time goes in v6:
time: 279 us; the launch traced here: 278 us
  starting transfers between devices  114 us (41%)
  blocking collectives  95.7 us (34%)
  waiting for transfers between devices  55.3 us (20%)
  other arithmetic  4.99 us (2%)
  local copies, waits for them, and re-layouts  4.81 us (2%)
    all_to_all x4, blocking collectives, gather(): return lax.all_to_all(copies, axes, 0, 0, tiled=True)  78.3 us
    all_to_all x3, starting transfers between devices, gather(): return lax.all_to_all(copies, axes, 0, 0, tiled=True)  59.3 us
    all_to_all x3, waiting for transfers between devices, gather(): return lax.all_to_all(copies, axes, 0, 0, tiled=True)  44 us
    ppermute x6, starting transfers between devices, send(): lax.ppermute(tile, AXES, list(zip(source.ravel().tolist(), target.ravel()...  42.7 us
    all_to_all x2, blocking collectives, body(): product = jnp.sum(lax.all_to_all(shares, 'x', 0, 0, tiled=True), axis=0)  17.3 us
    ppermute x1, starting transfers between devices, swap(): return lax.ppermute(tile, axis, [(i, i ^ bit) for i in range(size)])  7.69 us
  transfers between devices with their start and end apart: 11, of which 8 were waited for; matrix products, arithmetic and copies ran while one was open for 0% of the time, Pallas kernels for 0%

profile of v6, /device:TPU:1, one launch (start us, length us, event | category | flops | bytes accessed | tf_op | source)
XLA Modules:
  0.0 277.6 jit_solution(3076635386544160058)
XLA Ops:
  0.6 0.9 copy.34
  1.5 0.7 broadcast_in_dim.26
  2.2 29.0 %all-to-all-start = ((bf16[4,128,128]{2,1,0:T(8,128)(2,1)}), bf16[4,128,128]{2,1,0:T(8,128)(2,1)S(1)}, u32[]{:S(2)}, u32[]{:S(2)}) async-start(bf16[4,128,128]{2,1,0:T(8,128)(2,1)} %broadcast_in_dim.26), calls=%async_computation | async-start | bytes 262144 | tf_op jit(solution)/shard_map/all_to_all | solution.py:21
  31.9 21.7 %all-to-all-done = bf16[4,128,128]{2,1,0:T(8,128)(2,1)S(1)} async-done(((bf16[4,128,128]{2,1,0:T(8,128)(2,1)}), bf16[4,128,128]{2,1,0:T(8,128)(2,1)S(1)}, u32[]{:S(2)}, u32[]{:S(2)}) %all-to-all-start) | async-done | bytes 131104 | tf_op jit(solution)/shard_map/all_to_all | solution.py:21
  53.7 10.9 %all_to_all.50 = bf16[4,4,128,128]{3,2,1,0:T(8,128)(2,1)S(1)} all-to-all(bf16[4,4,128,128]{3,2,1,0:T(8,128)(2,1)S(1)} %broadcast_in_dim.27), channel_id=1, replica_groups=mesh['y'=4,'l'=8,'x'=4,'h'=4,'c'=2] {'y'}, dimensions={0} | all-to-all | bytes 1048576 | tf_op jit(solution)/shard_map/all_to_all | solution.py:21
  64.6 0.7 broadcast_in_dim.28
  65.3 7.5 %all-to-all-start.2 = ((bf16[8,128,128]{2,1,0:T(8,128)(2,1)}), bf16[8,128,128]{2,1,0:T(8,128)(2,1)S(1)}, u32[]{:S(2)}, u32[]{:S(2)}) async-start(bf16[8,128,128]{2,1,0:T(8,128)(2,1)} %broadcast_in_dim.28), calls=%async_computation.2 | async-start | bytes 524288 | tf_op jit(solution)/shard_map/all_to_all | solution.py:21
  72.9 7.7 %collective-permute-start.2 = (bf16[16,128,128]{2,1,0:T(8,128)(2,1)S(1)}, bf16[16,128,128]{2,1,0:T(8,128)(2,1)S(1)}, u32[]{:S(2)}, u32[]{:S(2)}) collective-permute-start(bf16[16,128,128]{2,1,0:T(8,128)(2,1)S(1)} %bitcast.70), channel_id=1, source_target_pairs={{0,1},{1,0},{2,3},{3,2},{4,5},{5,4},{6,7},{7,6},{8,9},{9,8},{10,11... | collective-permute-start | bytes 1572872 | tf_op jit(solution)/shard_map/ppermute | solution.py:25
  80.6 1.5 collective-permute-done.2
  82.3 2.5 all-to-all-done.2
  84.8 1.2 fusion.20
  86.0 4.1 %all-to-all-start.3 = ((f32[4,128,128]{2,1,0:T(8,128)}), f32[4,128,128]{2,1,0:T(8,128)S(1)}, u32[]{:S(2)}, u32[]{:S(2)}) async-start(f32[4,128,128]{2,1,0:T(8,128)} %fusion.20), calls=%async_computation.3 | async-start | bytes 524288 | tf_op jit(solution)/shard_map/all_to_all | solution.py:73
  90.1 0.7 collective-permute-start
  90.8 4.8 %all-to-all-done.3 = f32[4,128,128]{2,1,0:T(8,128)S(1)} async-done(((f32[4,128,128]{2,1,0:T(8,128)}), f32[4,128,128]{2,1,0:T(8,128)S(1)}, u32[]{:S(2)}, u32[]{:S(2)}) %all-to-all-start.3) | async-done | bytes 262176 | tf_op jit(solution)/shard_map/all_to_all | solution.py:73
  95.7 11.4 %collective-permute-start.3 = (f32[128,128]{0,1:T(8,128)S(1)}, f32[128,128]{0,1:T(8,128)S(1)}, u32[]{:S(2)}, u32[]{:S(2)}) collective-permute-start(f32[128,128]{0,1:T(8,128)S(1)} %copy.37), channel_id=1, source_target_pairs={{0,0},{1,32},{2,64},{3,96},{4,128},{5,160},{518,192},{519,224},{25... | collective-permute-start | bytes 196616 | tf_op jit(solution)/shard_map/ppermute | solution.py:42
  107.1 0.8 fusion.19
  108.0 1.1 collective-permute-done.3
  109.1 0.7 multiply_reduce_fusion
  109.9 28.7 %all_to_all.51 = bf16[8,128,128]{2,1,0:T(8,128)(2,1)S(1)} all-to-all(bf16[8,128,128]{2,1,0:T(8,128)(2,1)S(1)} %broadcast_in_dim.29), channel_id=1, replica_groups=mesh['y'=4,'l'=8,'x'=4,'h'=4,'c'=2] {'l'}, dimensions={0} | all-to-all | bytes 524288 | tf_op jit(solution)/shard_map/all_to_all | solution.py:21
  139.1 8.2 %all_to_all.52 = f32[4,128,128]{2,1,0:T(8,128)S(1)} all-to-all(f32[4,128,128]{2,1,0:T(8,128)S(1)} %fusion.21), channel_id=1, replica_groups=mesh['y'=4,'l'=8,'x'=4,'h'=4,'c'=2] {'x'}, dimensions={0} | all-to-all | bytes 524288 | tf_op jit(solution)/shard_map/all_to_all | solution.py:73
  147.4 13.3 %collective-permute-start.4 = (f32[128,128]{0,1:T(8,128)S(1)}, f32[128,128]{0,1:T(8,128)S(1)}, u32[]{:S(2)}, u32[]{:S(2)}) collective-permute-start(f32[128,128]{0,1:T(8,128)S(1)} %copy.39), channel_id=1, source_target_pairs={{0,0},{1,32},{2,64},{3,96},{4,128},{5,160},{518,192},{519,224},{25... | collective-permute-start | bytes 196616 | tf_op jit(solution)/shard_map/ppermute | solution.py:42
  160.7 1.9 collective-permute-done.4
  162.7 0.7 multiply_reduce_fusion.1
  163.5 23.7 %all_to_all.53 = bf16[8,128,128]{2,1,0:T(8,128)(2,1)S(1)} all-to-all(bf16[8,128,128]{2,1,0:T(8,128)(2,1)S(1)} %broadcast_in_dim.30), channel_id=1, replica_groups=mesh['y'=4,'l'=8,'x'=4,'h'=4,'c'=2] {'l'}, dimensions={0} | all-to-all | bytes 524288 | tf_op jit(solution)/shard_map/all_to_all | solution.py:21
  187.7 9.1 %all_to_all.54 = f32[4,128,128]{2,1,0:T(8,128)S(1)} all-to-all(f32[4,128,128]{2,1,0:T(8,128)S(1)} %fusion.22), channel_id=1, replica_groups=mesh['y'=4,'l'=8,'x'=4,'h'=4,'c'=2] {'x'}, dimensions={0} | all-to-all | bytes 524288 | tf_op jit(solution)/shard_map/all_to_all | solution.py:73
  196.9 16.0 %collective-permute-start.5 = (f32[128,128]{0,1:T(8,128)S(1)}, f32[128,128]{0,1:T(8,128)S(1)}, u32[]{:S(2)}, u32[]{:S(2)}) collective-permute-start(f32[128,128]{0,1:T(8,128)S(1)} %copy.41), channel_id=1, source_target_pairs={{0,0},{1,32},{2,64},{3,96},{4,128},{5,160},{518,192},{519,224},{25... | collective-permute-start | bytes 196616 | tf_op jit(solution)/shard_map/ppermute | solution.py:42
  213.0 1.9 collective-permute-done.5
  214.9 0.7 multiply_reduce_fusion.2
  215.6 1.9 compare_select_fusion.2
  217.5 15.0 %all_to_all.55 = f32[32,1,128]{2,1,0:T(1,128)S(1)} all-to-all(f32[32,1,128]{2,1,0:T(1,128)S(1)} %broadcast_in_dim.66), channel_id=1, replica_groups=mesh['y'=4,'l'=8,'x'=4,'h'=4,'c'=2] {'y','x','c'}, dimensions={0} | all-to-all | bytes 32768 | tf_op jit(solution)/shard_map/all_to_all | solution.py:21
  233.1 22.8 %all-to-all-start.9 = ((f32[32,1,128]{2,1,0:T(1,128)}), f32[32,1,128]{2,1,0:T(1,128)S(1)}, u32[]{:S(2)}, u32[]{:S(2)}) async-start(f32[32,1,128]{2,1,0:T(1,128)} %broadcast_in_dim.67), calls=%async_computation.9 | async-start | bytes 32768 | tf_op jit(solution)/shard_map/all_to_all | solution.py:21
  256.7 19.8 %all-to-all-done.9 = f32[32,1,128]{2,1,0:T(1,128)S(1)} async-done(((f32[32,1,128]{2,1,0:T(1,128)}), f32[32,1,128]{2,1,0:T(1,128)S(1)}, u32[]{:S(2)}, u32[]{:S(2)}) %all-to-all-start.9) | async-done | bytes 16416 | tf_op jit(solution)/shard_map/all_to_all | solution.py:21
  (33 shorter events, 5.1 us)
Async XLA Ops:
  2.2 29.0 %copy-start = (f32[128,128]{1,0:T(8,128)S(1)}, f32[128,128]{1,0:T(8,128)}, u32[]{:S(2)}) copy-start(f32[128,128]{1,0:T(8,128)} %param.4) | copy-start | bytes 196612
  2.2 51.4 %all-to-all-start = ((bf16[4,128,128]{2,1,0:T(8,128)(2,1)}), bf16[4,128,128]{2,1,0:T(8,128)(2,1)S(1)}, u32[]{:S(2)}, u32[]{:S(2)}) async-start(bf16[4,128,128]{2,1,0:T(8,128)(2,1)} %broadcast_in_dim.26), calls=%async_computation | async-start | bytes 262144 | tf_op jit(solution)/shard_map/all_to_all | solution.py:21
  31.2 0.7 collective-permute-start.1
  65.3 19.4 %all-to-all-start.2 = ((bf16[8,128,128]{2,1,0:T(8,128)(2,1)}), bf16[8,128,128]{2,1,0:T(8,128)(2,1)S(1)}, u32[]{:S(2)}, u32[]{:S(2)}) async-start(bf16[8,128,128]{2,1,0:T(8,128)(2,1)} %broadcast_in_dim.28), calls=%async_computation.2 | async-start | bytes 524288 | tf_op jit(solution)/shard_map/all_to_all | solution.py:21
  72.9 9.2 %collective-permute-start.2 = (bf16[16,128,128]{2,1,0:T(8,128)(2,1)S(1)}, bf16[16,128,128]{2,1,0:T(8,128)(2,1)S(1)}, u32[]{:S(2)}, u32[]{:S(2)}) collective-permute-start(bf16[16,128,128]{2,1,0:T(8,128)(2,1)S(1)} %bitcast.70), channel_id=1, source_target_pairs={{0,1},{1,0},{2,3},{3,2},{4,5},{5,4},{6,7},{7,6},{8,9},{9,8},{10,11... | collective-permute-start | bytes 1572872 | tf_op jit(solution)/shard_map/ppermute | solution.py:25
  86.0 4.1 %copy-start.1 = (f32[128,128]{1,0:T(8,128)S(1)}, f32[128,128]{1,0:T(8,128)}, u32[]{:S(2)}) copy-start(f32[128,128]{1,0:T(8,128)} %param.6) | copy-start | bytes 196612
  86.0 9.7 %all-to-all-start.3 = ((f32[4,128,128]{2,1,0:T(8,128)}), f32[4,128,128]{2,1,0:T(8,128)S(1)}, u32[]{:S(2)}, u32[]{:S(2)}) async-start(f32[4,128,128]{2,1,0:T(8,128)} %fusion.20), calls=%async_computation.3 | async-start | bytes 524288 | tf_op jit(solution)/shard_map/all_to_all | solution.py:73
  90.1 17.9 %collective-permute-start = (f32[2,128,128]{2,1,0:T(8,128)S(1)}, f32[2,128,128]{2,1,0:T(8,128)S(1)}, u32[]{:S(2)}, u32[]{:S(2)}) collective-permute-start(f32[2,128,128]{2,1,0:T(8,128)S(1)} %pad_maximum_fusion.1), channel_id=1, source_target_pairs={{0,0},{1,1},{2,2},{3,3},{4,4},{5,5},{6,518},{7,519},{8,256},{9,257... | collective-permute-start | bytes 393224 | tf_op jit(solution)/shard_map/ppermute | solution.py:42
  95.7 13.3 %collective-permute-start.3 = (f32[128,128]{0,1:T(8,128)S(1)}, f32[128,128]{0,1:T(8,128)S(1)}, u32[]{:S(2)}, u32[]{:S(2)}) collective-permute-start(f32[128,128]{0,1:T(8,128)S(1)} %copy.37), channel_id=1, source_target_pairs={{0,0},{1,32},{2,64},{3,96},{4,128},{5,160},{518,192},{519,224},{25... | collective-permute-start | bytes 196616 | tf_op jit(solution)/shard_map/ppermute | solution.py:42
  147.4 15.3 %collective-permute-start.4 = (f32[128,128]{0,1:T(8,128)S(1)}, f32[128,128]{0,1:T(8,128)S(1)}, u32[]{:S(2)}, u32[]{:S(2)}) collective-permute-start(f32[128,128]{0,1:T(8,128)S(1)} %copy.39), channel_id=1, source_target_pairs={{0,0},{1,32},{2,64},{3,96},{4,128},{5,160},{518,192},{519,224},{25... | collective-permute-start | bytes 196616 | tf_op jit(solution)/shard_map/ppermute | solution.py:42
  196.9 18.0 %collective-permute-start.5 = (f32[128,128]{0,1:T(8,128)S(1)}, f32[128,128]{0,1:T(8,128)S(1)}, u32[]{:S(2)}, u32[]{:S(2)}) collective-permute-start(f32[128,128]{0,1:T(8,128)S(1)} %copy.41), channel_id=1, source_target_pairs={{0,0},{1,32},{2,64},{3,96},{4,128},{5,160},{518,192},{519,224},{25... | collective-permute-start | bytes 196616 | tf_op jit(solution)/shard_map/ppermute | solution.py:42
  233.1 43.4 %all-to-all-start.9 = ((f32[32,1,128]{2,1,0:T(1,128)}), f32[32,1,128]{2,1,0:T(1,128)S(1)}, u32[]{:S(2)}, u32[]{:S(2)}) async-start(f32[32,1,128]{2,1,0:T(1,128)} %broadcast_in_dim.67), calls=%async_computation.9 | async-start | bytes 32768 | tf_op jit(solution)/shard_map/all_to_all | solution.py:21
  256.0 0.7 collective-permute-start.6

commit v7 on v6

--- a/solution.py
+++ b/solution.py
@@ -48,12 +48,19 @@
     start, turned = places()
 
     block = coupling.T
-    low = send(amplitudes.astype(jnp.bfloat16), start, turned)
-    quad = gather(block, "h", 4)
-    low, quad = lax.optimization_barrier((low, quad))
-    by_y = gather(quad.reshape(4, n, n), "y", 4).reshape(16, n, n)
-    by_y, low = lax.optimization_barrier((by_y, low))
-    by_l = gather(low, "l", 8).reshape(-1, n)
+    l = lax.axis_index("l")
+    low = amplitudes.astype(jnp.bfloat16)
+    across = turned[np.arange(SIDE) ^ 4]
+    own, other = send(low, start, turned), send(low, start, across)
+    quad = lax.all_gather(block, "h")
+    own, other, quad = lax.optimization_barrier((own, other, quad))
+    two = ordered(own, other, l // 4)
+    other = swap(two, "l", 8, 2)
+    by_y = lax.all_gather(quad, "y").reshape(16, n, n)
+    other, by_y = lax.optimization_barrier((other, by_y))
+    four = jnp.swapaxes(ordered(two, other, l // 2 % 2), 0, 1).reshape(4, n, n)
+    eight = ordered(four, swap(four, "l", 8, 1), l % 2)
+    by_l = jnp.swapaxes(eight, 0, 1).reshape(-1, n)
     state = send(jnp.stack([source, amplitudes]), start, turned)
     other = swap(by_y, "c", 2, 1)
     both = ordered(by_y, other, lax.axis_index("c"))

time: 279 us -> 291 us (1.043)
  blocking collectives: 95.7 us -> 168 us
  starting transfers between devices: 114 us -> 76 us
  waiting for transfers between devices: 55.3 us -> 33.5 us
    all_gather x0 -> x2, blocking collectives: none -> 59.7 us  [the longest x1 43.4 us: body(): quad = lax.all_gather(block, 'h')]
    all_to_all x3 -> x1, starting transfers between devices: 59.3 us -> 20.2 us  [gather(): return lax.all_to_all(copies, axes, 0, 0, tiled=True)]
    all_to_all x3 -> x1, waiting for transfers between devices: 44 us -> 19.8 us  [gather(): return lax.all_to_all(copies, axes, 0, 0, tiled=True)]
    ppermute x1 -> x3, starting transfers between devices: 7.69 us -> 18 us  [swap(): return lax.ppermute(tile, axis, [(i, i ^ bit) for i in range(size)])]
    ppermute x6 -> x7, starting transfers between devices: 42.7 us -> 34.3 us  [send(): lax.ppermute(tile, AXES, list(zip(source.ravel().tolist(), target.ravel()...]
    all_to_all x4 -> x3, blocking collectives: 78.3 us -> 85.2 us  [gather(): return lax.all_to_all(copies, axes, 0, 0, tiled=True)]
    all_to_all x2, blocking collectives: 17.3 us -> 23.6 us  [body(): product = jnp.sum(lax.all_to_all(shares, 'x', 0, 0, tiled=True), axis=0)]
  transfers between devices with their start and end apart: 11 -> 12, of which waited for: 8 -> 6; matrix products, arithmetic and copies ran while one was open for 0% -> 0% of each run, Pallas kernels for 0% -> 0%
where the time goes in v7:
time: 291 us; the launch traced here: 290 us
  blocking collectives  168 us (58%)
  starting transfers between devices  76 us (26%)
  waiting for transfers between devices  33.5 us (12%)
  other arithmetic  6.03 us (2%)
    all_to_all x3, blocking collectives, gather(): return lax.all_to_all(copies, axes, 0, 0, tiled=True)  85.2 us
    all_gather x1, blocking collectives, body(): quad = lax.all_gather(block, 'h')  43.4 us
    ppermute x7, starting transfers between devices, send(): lax.ppermute(tile, AXES, list(zip(source.ravel().tolist(), target.ravel()...  34.3 us
    all_to_all x2, blocking collectives, body(): product = jnp.sum(lax.all_to_all(shares, 'x', 0, 0, tiled=True), axis=0)  23.6 us
    all_to_all x1, starting transfers between devices, gather(): return lax.all_to_all(copies, axes, 0, 0, tiled=True)  20.2 us
    all_to_all x1, waiting for transfers between devices, gather(): return lax.all_to_all(copies, axes, 0, 0, tiled=True)  19.8 us
    ppermute x3, starting transfers between devices, swap(): return lax.ppermute(tile, axis, [(i, i ^ bit) for i in range(size)])  18 us
    all_gather x1, blocking collectives, body(): by_y = lax.all_gather(quad, 'y').reshape(16, n, n)  16.3 us
  transfers between devices with their start and end apart: 12, of which 6 were waited for; matrix products, arithmetic and copies ran while one was open for 0% of the time, Pallas kernels for 0%

profile of v7, /device:TPU:1, one launch (start us, length us, event | category | flops | bytes accessed | tf_op | source)
XLA Modules:
  0.0 289.7 jit_solution(9149897246462669648)
XLA Ops:
  0.6 0.8 convert_element_type.9
  1.5 0.8 collective-permute-start.1
  2.3 9.6 %collective-permute-start.2 = (bf16[128,128]{1,0:T(8,128)(2,1)S(1)}, bf16[128,128]{1,0:T(8,128)(2,1)S(1)}, u32[]{:S(2)}, u32[]{:S(2)}) collective-permute-start(bf16[128,128]{1,0:T(8,128)(2,1)S(1)} %convert_element_type.9), channel_id=1, source_target_pairs={{0,128},{1,129},{2,130},{3,131},{4,132},{5,133},{6,646},{7,647},{8... | collective-permute-start | bytes 98312 | tf_op jit(solution)/shard_map/ppermute | solution.py:42
  12.0 43.4 %all-gather = bf16[512,128]{0,1:T(8,128)(2,1)S(1)} all-gather(bf16[128,128]{0,1:T(8,128)(2,1)S(1)} %bitcast.100), channel_id=2, replica_groups=mesh['y'=4,'l'=8,'x'=4,'h'=4,'c'=2] {'h'}, dimensions={0}, use_global_device_ids=true | all-gather | bytes 163840 | tf_op jit(solution)/shard_map/all_gather | solution.py:55
  55.6 1.9 collective-permute-start.3
  57.5 16.3 %all-gather.1 = bf16[16,128,128]{2,1,0:T(8,128)(2,1)S(1)} all-gather(bf16[4,128,128]{2,1,0:T(8,128)(2,1)S(1)} %bitcast.94), channel_id=3, replica_groups=mesh['y'=4,'l'=8,'x'=4,'h'=4,'c'=2] {'y'}, dimensions={0}, use_global_device_ids=true | all-gather | bytes 655360 | tf_op jit(solution)/shard_map/all_gather | solution.py:59
  73.8 12.8 %collective-permute-start.4 = (bf16[16,128,128]{2,1,0:T(8,128)(2,1)S(1)}, bf16[16,128,128]{2,1,0:T(8,128)(2,1)S(1)}, u32[]{:S(2)}, u32[]{:S(2)}) collective-permute-start(bf16[16,128,128]{2,1,0:T(8,128)(2,1)S(1)} %all-gather.1), channel_id=1, source_target_pairs={{0,1},{1,0},{2,3},{3,2},{4,5},{5,4},{6,7},{7,6},{8,9},{9,8},{10,11... | collective-permute-start | bytes 1572872 | tf_op jit(solution)/shard_map/ppermute | solution.py:25
  86.6 3.3 %collective-permute-start.5 = (bf16[4,128,128]{2,1,0:T(8,128)(2,1)S(1)}, bf16[4,128,128]{2,1,0:T(8,128)(2,1)S(1)}, u32[]{:S(2)}, u32[]{:S(2)}) collective-permute-start(bf16[4,128,128]{2,1,0:T(8,128)(2,1)S(1)} %bitcast.95), channel_id=1, source_target_pairs={{0,32},{32,0},{64,96},{96,64},{128,160},{160,128},{192,224},{224,1... | collective-permute-start | bytes 393224 | tf_op jit(solution)/shard_map/ppermute | solution.py:25
  90.0 3.6 %collective-permute-done.5 = bf16[4,128,128]{2,1,0:T(8,128)(2,1)S(1)} collective-permute-done((bf16[4,128,128]{2,1,0:T(8,128)(2,1)S(1)}, bf16[4,128,128]{2,1,0:T(8,128)(2,1)S(1)}, u32[]{:S(2)}, u32[]{:S(2)}) %collective-permute-start.5) | collective-permute-done | bytes 131104 | tf_op jit(solution)/shard_map/ppermute | solution.py:25
  93.9 1.2 fusion.20
  95.1 3.5 %all-to-all-start = ((f32[4,128,128]{2,1,0:T(8,128)}), f32[4,128,128]{2,1,0:T(8,128)S(1)}, u32[]{:S(2)}, u32[]{:S(2)}) async-start(f32[4,128,128]{2,1,0:T(8,128)} %fusion.20), calls=%async_computation | async-start | bytes 524288 | tf_op jit(solution)/shard_map/all_to_all | solution.py:80
  98.7 0.7 collective-permute-start
  99.4 4.9 %all-to-all-done = f32[4,128,128]{2,1,0:T(8,128)S(1)} async-done(((f32[4,128,128]{2,1,0:T(8,128)}), f32[4,128,128]{2,1,0:T(8,128)S(1)}, u32[]{:S(2)}, u32[]{:S(2)}) %all-to-all-start) | async-done | bytes 262176 | tf_op jit(solution)/shard_map/all_to_all | solution.py:80
  104.3 5.3 %collective-permute-start.6 = (f32[128,128]{0,1:T(8,128)S(1)}, f32[128,128]{0,1:T(8,128)S(1)}, u32[]{:S(2)}, u32[]{:S(2)}) collective-permute-start(f32[128,128]{0,1:T(8,128)S(1)} %copy.45), channel_id=1, source_target_pairs={{0,0},{1,32},{2,64},{3,96},{4,128},{5,160},{518,192},{519,224},{25... | collective-permute-start | bytes 196616 | tf_op jit(solution)/shard_map/ppermute | solution.py:42
  109.7 0.8 fusion.19
  110.5 1.1 collective-permute-done.6
  111.6 0.7 multiply_reduce_fusion
  112.4 37.7 %all_to_all.35 = bf16[8,128,128]{2,1,0:T(8,128)(2,1)S(1)} all-to-all(bf16[8,128,128]{2,1,0:T(8,128)(2,1)S(1)} %broadcast_in_dim.20), channel_id=1, replica_groups=mesh['y'=4,'l'=8,'x'=4,'h'=4,'c'=2] {'l'}, dimensions={0} | all-to-all | bytes 524288 | tf_op jit(solution)/shard_map/all_to_all | solution.py:21
  150.6 15.2 %all_to_all.36 = f32[4,128,128]{2,1,0:T(8,128)S(1)} all-to-all(f32[4,128,128]{2,1,0:T(8,128)S(1)} %fusion.21), channel_id=1, replica_groups=mesh['y'=4,'l'=8,'x'=4,'h'=4,'c'=2] {'x'}, dimensions={0} | all-to-all | bytes 524288 | tf_op jit(solution)/shard_map/all_to_all | solution.py:80
  165.9 6.9 %collective-permute-start.7 = (f32[128,128]{0,1:T(8,128)S(1)}, f32[128,128]{0,1:T(8,128)S(1)}, u32[]{:S(2)}, u32[]{:S(2)}) collective-permute-start(f32[128,128]{0,1:T(8,128)S(1)} %copy.47), channel_id=1, source_target_pairs={{0,0},{1,32},{2,64},{3,96},{4,128},{5,160},{518,192},{519,224},{25... | collective-permute-start | bytes 196616 | tf_op jit(solution)/shard_map/ppermute | solution.py:42
  172.9 2.2 collective-permute-done.7
  175.1 0.7 multiply_reduce_fusion.1
  175.9 32.2 %all_to_all.37 = bf16[8,128,128]{2,1,0:T(8,128)(2,1)S(1)} all-to-all(bf16[8,128,128]{2,1,0:T(8,128)(2,1)S(1)} %broadcast_in_dim.40), channel_id=1, replica_groups=mesh['y'=4,'l'=8,'x'=4,'h'=4,'c'=2] {'l'}, dimensions={0} | all-to-all | bytes 524288 | tf_op jit(solution)/shard_map/all_to_all | solution.py:21
  208.6 8.3 %all_to_all.38 = f32[4,128,128]{2,1,0:T(8,128)S(1)} all-to-all(f32[4,128,128]{2,1,0:T(8,128)S(1)} %fusion.22), channel_id=1, replica_groups=mesh['y'=4,'l'=8,'x'=4,'h'=4,'c'=2] {'x'}, dimensions={0} | all-to-all | bytes 524288 | tf_op jit(solution)/shard_map/all_to_all | solution.py:80
  217.1 10.3 %collective-permute-start.8 = (f32[128,128]{0,1:T(8,128)S(1)}, f32[128,128]{0,1:T(8,128)S(1)}, u32[]{:S(2)}, u32[]{:S(2)}) collective-permute-start(f32[128,128]{0,1:T(8,128)S(1)} %copy.49), channel_id=1, source_target_pairs={{0,0},{1,32},{2,64},{3,96},{4,128},{5,160},{518,192},{519,224},{25... | collective-permute-start | bytes 196616 | tf_op jit(solution)/shard_map/ppermute | solution.py:42
  227.3 1.9 collective-permute-done.8
  229.3 0.7 multiply_reduce_fusion.2
  230.0 1.9 compare_select_fusion.2
  231.9 15.2 %all_to_all.39 = f32[32,1,128]{2,1,0:T(1,128)S(1)} all-to-all(f32[32,1,128]{2,1,0:T(1,128)S(1)} %broadcast_in_dim.45), channel_id=1, replica_groups=mesh['y'=4,'l'=8,'x'=4,'h'=4,'c'=2] {'y','x','c'}, dimensions={0} | all-to-all | bytes 32768 | tf_op jit(solution)/shard_map/all_to_all | solution.py:21
  247.8 20.2 %all-to-all-start.6 = ((f32[32,1,128]{2,1,0:T(1,128)}), f32[32,1,128]{2,1,0:T(1,128)S(1)}, u32[]{:S(2)}, u32[]{:S(2)}) async-start(f32[32,1,128]{2,1,0:T(1,128)} %broadcast_in_dim.46), calls=%async_computation.6 | async-start | bytes 32768 | tf_op jit(solution)/shard_map/all_to_all | solution.py:21
  268.1 0.7 collective-permute-start.9
  268.8 19.8 %all-to-all-done.6 = f32[32,1,128]{2,1,0:T(1,128)S(1)} async-done(((f32[32,1,128]{2,1,0:T(1,128)}), f32[32,1,128]{2,1,0:T(1,128)S(1)}, u32[]{:S(2)}, u32[]{:S(2)}) %all-to-all-start.6) | async-done | bytes 16416 | tf_op jit(solution)/shard_map/all_to_all | solution.py:21
  (42 shorter events, 3.9 us)
Async XLA Ops:
  1.5 10.5 %copy-start.2 = (bf16[128,128]{1,0:T(8,128)(2,1)S(1)}, bf16[128,128]{1,0:T(8,128)(2,1)}, u32[]{:S(2)}) copy-start(bf16[128,128]{1,0:T(8,128)(2,1)} %param.5) | copy-start | bytes 98308
  1.5 54.0 %collective-permute-start.1 = (bf16[128,128]{1,0:T(8,128)(2,1)S(1)}, bf16[128,128]{1,0:T(8,128)(2,1)S(1)}, u32[]{:S(2)}, u32[]{:S(2)}) collective-permute-start(bf16[128,128]{1,0:T(8,128)(2,1)S(1)} %convert_element_type.9), channel_id=1, source_target_pairs={{0,0},{1,1},{2,2},{3,3},{4,4},{5,5},{6,518},{7,519},{8,256},{9,257... | collective-permute-start | bytes 98312 | tf_op jit(solution)/shard_map/ppermute | solution.py:42
  2.3 53.3 %collective-permute-start.2 = (bf16[128,128]{1,0:T(8,128)(2,1)S(1)}, bf16[128,128]{1,0:T(8,128)(2,1)S(1)}, u32[]{:S(2)}, u32[]{:S(2)}) collective-permute-start(bf16[128,128]{1,0:T(8,128)(2,1)S(1)} %convert_element_type.9), channel_id=1, source_target_pairs={{0,128},{1,129},{2,130},{3,131},{4,132},{5,133},{6,646},{7,647},{8... | collective-permute-start | bytes 98312 | tf_op jit(solution)/shard_map/ppermute | solution.py:42
  55.6 18.2 %collective-permute-start.3 = (bf16[2,128,128]{2,1,0:T(8,128)(2,1)S(1)}, bf16[2,128,128]{2,1,0:T(8,128)(2,1)S(1)}, u32[]{:S(2)}, u32[]{:S(2)}) collective-permute-start(bf16[2,128,128]{2,1,0:T(8,128)(2,1)S(1)} %pad_maximum_fusion.3), channel_id=1, source_target_pairs={{0,64},{32,96},{64,0},{96,32},{128,192},{160,224},{192,128},{224,1... | collective-permute-start | bytes 196616 | tf_op jit(solution)/shard_map/ppermute | solution.py:25
  73.8 19.9 %collective-permute-start.4 = (bf16[16,128,128]{2,1,0:T(8,128)(2,1)S(1)}, bf16[16,128,128]{2,1,0:T(8,128)(2,1)S(1)}, u32[]{:S(2)}, u32[]{:S(2)}) collective-permute-start(bf16[16,128,128]{2,1,0:T(8,128)(2,1)S(1)} %all-gather.1), channel_id=1, source_target_pairs={{0,1},{1,0},{2,3},{3,2},{4,5},{5,4},{6,7},{7,6},{8,9},{9,8},{10,11... | collective-permute-start | bytes 1572872 | tf_op jit(solution)/shard_map/ppermute | solution.py:25
  86.6 7.0 %collective-permute-start.5 = (bf16[4,128,128]{2,1,0:T(8,128)(2,1)S(1)}, bf16[4,128,128]{2,1,0:T(8,128)(2,1)S(1)}, u32[]{:S(2)}, u32[]{:S(2)}) collective-permute-start(bf16[4,128,128]{2,1,0:T(8,128)(2,1)S(1)} %bitcast.95), channel_id=1, source_target_pairs={{0,32},{32,0},{64,96},{96,64},{128,160},{160,128},{192,224},{224,1... | collective-permute-start | bytes 393224 | tf_op jit(solution)/shard_map/ppermute | solution.py:25
  95.1 3.5 %copy-start = (f32[128,128]{1,0:T(8,128)S(1)}, f32[128,128]{1,0:T(8,128)}, u32[]{:S(2)}) copy-start(f32[128,128]{1,0:T(8,128)} %param.4) | copy-start | bytes 196612
  95.1 3.6 %copy-start.1 = (f32[128,128]{1,0:T(8,128)S(1)}, f32[128,128]{1,0:T(8,128)}, u32[]{:S(2)}) copy-start(f32[128,128]{1,0:T(8,128)} %param.6) | copy-start | bytes 196612
  95.1 9.2 %all-to-all-start = ((f32[4,128,128]{2,1,0:T(8,128)}), f32[4,128,128]{2,1,0:T(8,128)S(1)}, u32[]{:S(2)}, u32[]{:S(2)}) async-start(f32[4,128,128]{2,1,0:T(8,128)} %fusion.20), calls=%async_computation | async-start | bytes 524288 | tf_op jit(solution)/shard_map/all_to_all | solution.py:80
  98.7 11.8 %collective-permute-start = (f32[2,128,128]{2,1,0:T(8,128)S(1)}, f32[2,128,128]{2,1,0:T(8,128)S(1)}, u32[]{:S(2)}, u32[]{:S(2)}) collective-permute-start(f32[2,128,128]{2,1,0:T(8,128)S(1)} %pad_maximum_fusion.1), channel_id=1, source_target_pairs={{0,0},{1,1},{2,2},{3,3},{4,4},{5,5},{6,518},{7,519},{8,256},{9,257... | collective-permute-start | bytes 393224 | tf_op jit(solution)/shard_map/ppermute | solution.py:42
  104.3 7.2 %collective-permute-start.6 = (f32[128,128]{0,1:T(8,128)S(1)}, f32[128,128]{0,1:T(8,128)S(1)}, u32[]{:S(2)}, u32[]{:S(2)}) collective-permute-start(f32[128,128]{0,1:T(8,128)S(1)} %copy.45), channel_id=1, source_target_pairs={{0,0},{1,32},{2,64},{3,96},{4,128},{5,160},{518,192},{519,224},{25... | collective-permute-start | bytes 196616 | tf_op jit(solution)/shard_map/ppermute | solution.py:42
  165.9 9.1 %collective-permute-start.7 = (f32[128,128]{0,1:T(8,128)S(1)}, f32[128,128]{0,1:T(8,128)S(1)}, u32[]{:S(2)}, u32[]{:S(2)}) collective-permute-start(f32[128,128]{0,1:T(8,128)S(1)} %copy.47), channel_id=1, source_target_pairs={{0,0},{1,32},{2,64},{3,96},{4,128},{5,160},{518,192},{519,224},{25... | collective-permute-start | bytes 196616 | tf_op jit(solution)/shard_map/ppermute | solution.py:42
  217.1 12.2 %collective-permute-start.8 = (f32[128,128]{0,1:T(8,128)S(1)}, f32[128,128]{0,1:T(8,128)S(1)}, u32[]{:S(2)}, u32[]{:S(2)}) collective-permute-start(f32[128,128]{0,1:T(8,128)S(1)} %copy.49), channel_id=1, source_target_pairs={{0,0},{1,32},{2,64},{3,96},{4,128},{5,160},{518,192},{519,224},{25... | collective-permute-start | bytes 196616 | tf_op jit(solution)/shard_map/ppermute | solution.py:42
  247.8 40.8 %all-to-all-start.6 = ((f32[32,1,128]{2,1,0:T(1,128)}), f32[32,1,128]{2,1,0:T(1,128)S(1)}, u32[]{:S(2)}, u32[]{:S(2)}) async-start(f32[32,1,128]{2,1,0:T(1,128)} %broadcast_in_dim.46), calls=%async_computation.6 | async-start | bytes 32768 | tf_op jit(solution)/shard_map/all_to_all | solution.py:21
  268.1 0.7 collective-permute-start.9

commit v8 on v7

--- a/solution.py
+++ b/solution.py
@@ -52,16 +52,17 @@
     low = amplitudes.astype(jnp.bfloat16)
     across = turned[np.arange(SIDE) ^ 4]
     own, other = send(low, start, turned), send(low, start, across)
-    quad = lax.all_gather(block, "h")
-    own, other, quad = lax.optimization_barrier((own, other, quad))
     two = ordered(own, other, l // 4)
     other = swap(two, "l", 8, 2)
-    by_y = lax.all_gather(quad, "y").reshape(16, n, n)
-    other, by_y = lax.optimization_barrier((other, by_y))
+    quad = gather(block, "h", 4).reshape(4, n, n)
+    two, other, quad = lax.optimization_barrier((two, other, quad))
     four = jnp.swapaxes(ordered(two, other, l // 2 % 2), 0, 1).reshape(4, n, n)
-    eight = ordered(four, swap(four, "l", 8, 1), l % 2)
+    other = swap(four, "l", 8, 1)
+    by_y = gather(quad, "y", 4).reshape(16, n, n)
+    state = send(jnp.stack([source, amplitudes]), start, turned)
+    four, other, by_y, state = lax.optimization_barrier((four, other, by_y, state))
+    eight = ordered(four, other, l % 2)
     by_l = jnp.swapaxes(eight, 0, 1).reshape(-1, n)
-    state = send(jnp.stack([source, amplitudes]), start, turned)
     other = swap(by_y, "c", 2, 1)
     both = ordered(by_y, other, lax.axis_index("c"))
     part = jnp.swapaxes(both, 0, 1).reshape(4, -1, n)

time: 291 us -> 278 us (0.955)
  blocking collectives: 168 us -> 106 us
  starting transfers between devices: 76 us -> 109 us
  waiting for transfers between devices: 33.5 us -> 48.7 us
    all_gather x2 -> x0, blocking collectives: 59.7 us -> none  [the longest x1 43.4 us: body(): quad = lax.all_gather(block, 'h')]
    all_to_all x1 -> x3, starting transfers between devices: 20.2 us -> 61.5 us  [gather(): return lax.all_to_all(copies, axes, 0, 0, tiled=True)]
    all_to_all x2, blocking collectives: 23.6 us -> 15.9 us  [body(): product = jnp.sum(lax.all_to_all(shares, 'x', 0, 0, tiled=True), axis=0)]
    all_to_all x1 -> x3, waiting for transfers between devices: 19.8 us -> 25.7 us  [gather(): return lax.all_to_all(copies, axes, 0, 0, tiled=True)]
    all_to_all x3, blocking collectives: 85.2 us -> 90.4 us  [gather(): return lax.all_to_all(copies, axes, 0, 0, tiled=True)]
    ppermute x7, starting transfers between devices: 34.3 us -> 29.6 us  [send(): lax.ppermute(tile, AXES, list(zip(source.ravel().tolist(), target.ravel()...]
    ppermute x3, waiting for transfers between devices: 3.65 us -> 8 us  [swap(): return lax.ppermute(tile, axis, [(i, i ^ bit) for i in range(size)])]
    ppermute x3, starting transfers between devices: 18 us -> 13.9 us  [swap(): return lax.ppermute(tile, axis, [(i, i ^ bit) for i in range(size)])]
  transfers between devices with their start and end apart: 12 -> 14, of which waited for: 6 -> 10; matrix products, arithmetic and copies ran while one was open for 0% -> 1% of each run, Pallas kernels for 0% -> 0%
where the time goes in v8:
time: 278 us; the launch traced here: 277 us
  starting transfers between devices  109 us (39%)
  blocking collectives  106 us (38%)
  waiting for transfers between devices  48.7 us (18%)
  other arithmetic  5.31 us (2%)
  local copies, waits for them, and re-layouts  4.9 us (2%)
    all_to_all x3, blocking collectives, gather(): return lax.all_to_all(copies, axes, 0, 0, tiled=True)  90.4 us
    all_to_all x3, starting transfers between devices, gather(): return lax.all_to_all(copies, axes, 0, 0, tiled=True)  61.5 us
    ppermute x7, starting transfers between devices, send(): lax.ppermute(tile, AXES, list(zip(source.ravel().tolist(), target.ravel()...  29.6 us
    all_to_all x3, waiting for transfers between devices, gather(): return lax.all_to_all(copies, axes, 0, 0, tiled=True)  25.7 us
    all_to_all x2, blocking collectives, body(): product = jnp.sum(lax.all_to_all(shares, 'x', 0, 0, tiled=True), axis=0)  15.9 us
    ppermute x3, starting transfers between devices, swap(): return lax.ppermute(tile, axis, [(i, i ^ bit) for i in range(size)])  13.9 us
    ppermute x7, waiting for transfers between devices, send(): lax.ppermute(tile, AXES, list(zip(source.ravel().tolist(), target.ravel()...  9.19 us
    ppermute x3, waiting for transfers between devices, swap(): return lax.ppermute(tile, axis, [(i, i ^ bit) for i in range(size)])  8 us
  transfers between devices with their start and end apart: 14, of which 10 were waited for; matrix products, arithmetic and copies ran while one was open for 1% of the time, Pallas kernels for 0%

profile of v8, /device:TPU:1, one launch (start us, length us, event | category | flops | bytes accessed | tf_op | source)
XLA Modules:
  0.0 276.9 jit_solution(9587998951272855900)
XLA Ops:
  0.6 0.9 copy.41
  2.2 29.0 %all-to-all-start = ((bf16[4,128,128]{2,1,0:T(8,128)(2,1)}), bf16[4,128,128]{2,1,0:T(8,128)(2,1)S(1)}, u32[]{:S(2)}, u32[]{:S(2)}) async-start(bf16[4,128,128]{2,1,0:T(8,128)(2,1)} %broadcast_in_dim.24), calls=%async_computation | async-start | bytes 262144 | tf_op jit(solution)/shard_map/all_to_all | solution.py:21
  31.2 4.0 %collective-permute-start.1 = (bf16[128,128]{1,0:T(8,128)(2,1)S(1)}, bf16[128,128]{1,0:T(8,128)(2,1)S(1)}, u32[]{:S(2)}, u32[]{:S(2)}) collective-permute-start(bf16[128,128]{1,0:T(8,128)(2,1)S(1)} %convert_element_type.9), channel_id=1, source_target_pairs={{0,128},{1,129},{2,130},{3,131},{4,132},{5,133},{6,646},{7,647},{8... | collective-permute-start | bytes 98312 | tf_op jit(solution)/shard_map/ppermute | solution.py:42
  35.9 4.1 %collective-permute-done.1 = bf16[128,128]{1,0:T(8,128)(2,1)S(1)} collective-permute-done((bf16[128,128]{1,0:T(8,128)(2,1)S(1)}, bf16[128,128]{1,0:T(8,128)(2,1)S(1)}, u32[]{:S(2)}, u32[]{:S(2)}) %collective-permute-start.1) | collective-permute-done | bytes 32800 | tf_op jit(solution)/shard_map/ppermute | solution.py:42
  40.0 2.9 %collective-permute-start.2 = (bf16[2,128,128]{2,1,0:T(8,128)(2,1)S(1)}, bf16[2,128,128]{2,1,0:T(8,128)(2,1)S(1)}, u32[]{:S(2)}, u32[]{:S(2)}) collective-permute-start(bf16[2,128,128]{2,1,0:T(8,128)(2,1)S(1)} %pad_maximum_fusion.3), channel_id=1, source_target_pairs={{0,64},{32,96},{64,0},{96,32},{128,192},{160,224},{192,128},{224,1... | collective-permute-start | bytes 196616 | tf_op jit(solution)/shard_map/ppermute | solution.py:25
  43.7 4.0 %collective-permute-done.2 = bf16[2,128,128]{2,1,0:T(8,128)(2,1)S(1)} collective-permute-done((bf16[2,128,128]{2,1,0:T(8,128)(2,1)S(1)}, bf16[2,128,128]{2,1,0:T(8,128)(2,1)S(1)}, u32[]{:S(2)}, u32[]{:S(2)}) %collective-permute-start.2) | collective-permute-done | bytes 65568 | tf_op jit(solution)/shard_map/ppermute | solution.py:25
  47.6 6.0 %all-to-all-done = bf16[4,128,128]{2,1,0:T(8,128)(2,1)S(1)} async-done(((bf16[4,128,128]{2,1,0:T(8,128)(2,1)}), bf16[4,128,128]{2,1,0:T(8,128)(2,1)S(1)}, u32[]{:S(2)}, u32[]{:S(2)}) %all-to-all-start) | async-done | bytes 131104 | tf_op jit(solution)/shard_map/all_to_all | solution.py:21
  53.6 0.9 broadcast_in_dim.25
  54.5 7.4 %all-to-all-start.1 = ((bf16[4,4,128,128]{3,2,1,0:T(8,128)(2,1)}), bf16[4,4,128,128]{3,2,1,0:T(8,128)(2,1)S(1)}, u32[]{:S(2)}, u32[]{:S(2)}) async-start(bf16[4,4,128,128]{3,2,1,0:T(8,128)(2,1)} %broadcast_in_dim.25), calls=%async_computation.1 | async-start | bytes 1048576 | tf_op jit(solution)/shard_map/all_to_all | solution.py:21
  61.9 5.1 %collective-permute-start.3 = (bf16[4,128,128]{2,1,0:T(8,128)(2,1)S(1)}, bf16[4,128,128]{2,1,0:T(8,128)(2,1)S(1)}, u32[]{:S(2)}, u32[]{:S(2)}) collective-permute-start(bf16[4,128,128]{2,1,0:T(8,128)(2,1)S(1)} %bitcast.90), channel_id=1, source_target_pairs={{0,32},{32,0},{64,96},{96,64},{128,160},{160,128},{192,224},{224,1... | collective-permute-start | bytes 393224 | tf_op jit(solution)/shard_map/ppermute | solution.py:25
  67.0 2.6 collective-permute-done.3
  69.6 5.9 %collective-permute-start.5 = (bf16[16,128,128]{2,1,0:T(8,128)(2,1)S(1)}, bf16[16,128,128]{2,1,0:T(8,128)(2,1)S(1)}, u32[]{:S(2)}, u32[]{:S(2)}) collective-permute-start(bf16[16,128,128]{2,1,0:T(8,128)(2,1)S(1)} %bitcast.85), channel_id=1, source_target_pairs={{0,1},{1,0},{2,3},{3,2},{4,5},{5,4},{6,7},{7,6},{8,9},{9,8},{10,11... | collective-permute-start | bytes 1572872 | tf_op jit(solution)/shard_map/ppermute | solution.py:25
  75.7 1.4 collective-permute-done.5
  77.2 1.2 fusion.20
  78.4 3.5 %all-to-all-start.2 = ((f32[4,128,128]{2,1,0:T(8,128)}), f32[4,128,128]{2,1,0:T(8,128)S(1)}, u32[]{:S(2)}, u32[]{:S(2)}) async-start(f32[4,128,128]{2,1,0:T(8,128)} %fusion.20), calls=%async_computation.2 | async-start | bytes 524288 | tf_op jit(solution)/shard_map/all_to_all | solution.py:81
  82.0 5.8 %all-to-all-done.2 = f32[4,128,128]{2,1,0:T(8,128)S(1)} async-done(((f32[4,128,128]{2,1,0:T(8,128)}), f32[4,128,128]{2,1,0:T(8,128)S(1)}, u32[]{:S(2)}, u32[]{:S(2)}) %all-to-all-start.2) | async-done | bytes 262176 | tf_op jit(solution)/shard_map/all_to_all | solution.py:81
  87.9 6.5 %collective-permute-start.6 = (f32[128,128]{0,1:T(8,128)S(1)}, f32[128,128]{0,1:T(8,128)S(1)}, u32[]{:S(2)}, u32[]{:S(2)}) collective-permute-start(f32[128,128]{0,1:T(8,128)S(1)} %copy.46), channel_id=1, source_target_pairs={{0,0},{1,32},{2,64},{3,96},{4,128},{5,160},{518,192},{519,224},{25... | collective-permute-start | bytes 196616 | tf_op jit(solution)/shard_map/ppermute | solution.py:42
  94.4 0.8 fusion.19
  95.2 1.1 collective-permute-done.6
  97.1 40.7 %all_to_all.45 = bf16[8,128,128]{2,1,0:T(8,128)(2,1)S(1)} all-to-all(bf16[8,128,128]{2,1,0:T(8,128)(2,1)S(1)} %broadcast_in_dim.26), channel_id=1, replica_groups=mesh['y'=4,'l'=8,'x'=4,'h'=4,'c'=2] {'l'}, dimensions={0} | all-to-all | bytes 524288 | tf_op jit(solution)/shard_map/all_to_all | solution.py:21
  138.3 7.9 %all_to_all.46 = f32[4,128,128]{2,1,0:T(8,128)S(1)} all-to-all(f32[4,128,128]{2,1,0:T(8,128)S(1)} %fusion.21), channel_id=1, replica_groups=mesh['y'=4,'l'=8,'x'=4,'h'=4,'c'=2] {'x'}, dimensions={0} | all-to-all | bytes 524288 | tf_op jit(solution)/shard_map/all_to_all | solution.py:81
  146.3 6.7 %collective-permute-start.7 = (f32[128,128]{0,1:T(8,128)S(1)}, f32[128,128]{0,1:T(8,128)S(1)}, u32[]{:S(2)}, u32[]{:S(2)}) collective-permute-start(f32[128,128]{0,1:T(8,128)S(1)} %copy.48), channel_id=1, source_target_pairs={{0,0},{1,32},{2,64},{3,96},{4,128},{5,160},{518,192},{519,224},{25... | collective-permute-start | bytes 196616 | tf_op jit(solution)/shard_map/ppermute | solution.py:42
  153.0 1.9 collective-permute-done.7
  155.8 33.5 %all_to_all.47 = bf16[8,128,128]{2,1,0:T(8,128)(2,1)S(1)} all-to-all(bf16[8,128,128]{2,1,0:T(8,128)(2,1)S(1)} %broadcast_in_dim.27), channel_id=1, replica_groups=mesh['y'=4,'l'=8,'x'=4,'h'=4,'c'=2] {'l'}, dimensions={0} | all-to-all | bytes 524288 | tf_op jit(solution)/shard_map/all_to_all | solution.py:21
  189.7 7.9 %all_to_all.48 = f32[4,128,128]{2,1,0:T(8,128)S(1)} all-to-all(f32[4,128,128]{2,1,0:T(8,128)S(1)} %fusion.22), channel_id=1, replica_groups=mesh['y'=4,'l'=8,'x'=4,'h'=4,'c'=2] {'x'}, dimensions={0} | all-to-all | bytes 524288 | tf_op jit(solution)/shard_map/all_to_all | solution.py:81
  197.8 10.3 %collective-permute-start.8 = (f32[128,128]{0,1:T(8,128)S(1)}, f32[128,128]{0,1:T(8,128)S(1)}, u32[]{:S(2)}, u32[]{:S(2)}) collective-permute-start(f32[128,128]{0,1:T(8,128)S(1)} %copy.50), channel_id=1, source_target_pairs={{0,0},{1,32},{2,64},{3,96},{4,128},{5,160},{518,192},{519,224},{25... | collective-permute-start | bytes 196616 | tf_op jit(solution)/shard_map/ppermute | solution.py:42
  208.1 2.1 collective-permute-done.8
  210.2 0.8 multiply_reduce_fusion.2
  211.0 2.0 compare_select_fusion.2
  213.0 16.3 %all_to_all.49 = f32[32,1,128]{2,1,0:T(1,128)S(1)} all-to-all(f32[32,1,128]{2,1,0:T(1,128)S(1)} %broadcast_in_dim.59), channel_id=1, replica_groups=mesh['y'=4,'l'=8,'x'=4,'h'=4,'c'=2] {'y','x','c'}, dimensions={0} | all-to-all | bytes 32768 | tf_op jit(solution)/shard_map/all_to_all | solution.py:21
  230.0 25.2 %all-to-all-start.8 = ((f32[32,1,128]{2,1,0:T(1,128)}), f32[32,1,128]{2,1,0:T(1,128)S(1)}, u32[]{:S(2)}, u32[]{:S(2)}) async-start(f32[32,1,128]{2,1,0:T(1,128)} %broadcast_in_dim.60), calls=%async_computation.8 | async-start | bytes 32768 | tf_op jit(solution)/shard_map/all_to_all | solution.py:21
  255.9 19.8 %all-to-all-done.8 = f32[32,1,128]{2,1,0:T(1,128)S(1)} async-done(((f32[32,1,128]{2,1,0:T(1,128)}), f32[32,1,128]{2,1,0:T(1,128)S(1)}, u32[]{:S(2)}, u32[]{:S(2)}) %all-to-all-start.8) | async-done | bytes 16416 | tf_op jit(solution)/shard_map/all_to_all | solution.py:21
  (44 shorter events, 7.8 us)
Async XLA Ops:
  2.2 29.0 %copy-start = (f32[128,128]{1,0:T(8,128)S(1)}, f32[128,128]{1,0:T(8,128)}, u32[]{:S(2)}) copy-start(f32[128,128]{1,0:T(8,128)} %param.4) | copy-start | bytes 196612
  2.2 51.4 %all-to-all-start = ((bf16[4,128,128]{2,1,0:T(8,128)(2,1)}), bf16[4,128,128]{2,1,0:T(8,128)(2,1)S(1)}, u32[]{:S(2)}, u32[]{:S(2)}) async-start(bf16[4,128,128]{2,1,0:T(8,128)(2,1)} %broadcast_in_dim.24), calls=%async_computation | async-start | bytes 262144 | tf_op jit(solution)/shard_map/all_to_all | solution.py:21
  31.2 8.8 %collective-permute-start.1 = (bf16[128,128]{1,0:T(8,128)(2,1)S(1)}, bf16[128,128]{1,0:T(8,128)(2,1)S(1)}, u32[]{:S(2)}, u32[]{:S(2)}) collective-permute-start(bf16[128,128]{1,0:T(8,128)(2,1)S(1)} %convert_element_type.9), channel_id=1, source_target_pairs={{0,128},{1,129},{2,130},{3,131},{4,132},{5,133},{6,646},{7,647},{8... | collective-permute-start | bytes 98312 | tf_op jit(solution)/shard_map/ppermute | solution.py:42
  35.2 4.8 %collective-permute-start = (bf16[128,128]{1,0:T(8,128)(2,1)S(1)}, bf16[128,128]{1,0:T(8,128)(2,1)S(1)}, u32[]{:S(2)}, u32[]{:S(2)}) collective-permute-start(bf16[128,128]{1,0:T(8,128)(2,1)S(1)} %convert_element_type.9), channel_id=1, source_target_pairs={{0,0},{1,1},{2,2},{3,3},{4,4},{5,5},{6,518},{7,519},{8,256},{9,257... | collective-permute-start | bytes 98312 | tf_op jit(solution)/shard_map/ppermute | solution.py:42
  40.0 2.9 %copy-start.1 = (f32[128,128]{1,0:T(8,128)S(1)}, f32[128,128]{1,0:T(8,128)}, u32[]{:S(2)}) copy-start(f32[128,128]{1,0:T(8,128)} %param.6) | copy-start | bytes 196612
  40.0 7.6 %collective-permute-start.2 = (bf16[2,128,128]{2,1,0:T(8,128)(2,1)S(1)}, bf16[2,128,128]{2,1,0:T(8,128)(2,1)S(1)}, u32[]{:S(2)}, u32[]{:S(2)}) collective-permute-start(bf16[2,128,128]{2,1,0:T(8,128)(2,1)S(1)} %pad_maximum_fusion.3), channel_id=1, source_target_pairs={{0,64},{32,96},{64,0},{96,32},{128,192},{160,224},{192,128},{224,1... | collective-permute-start | bytes 196616 | tf_op jit(solution)/shard_map/ppermute | solution.py:25
  43.0 24.0 %collective-permute-start.4 = (f32[2,128,128]{2,1,0:T(8,128)S(1)}, f32[2,128,128]{2,1,0:T(8,128)S(1)}, u32[]{:S(2)}, u32[]{:S(2)}) collective-permute-start(f32[2,128,128]{2,1,0:T(8,128)S(1)} %pad_maximum_fusion.2), channel_id=1, source_target_pairs={{0,0},{1,1},{2,2},{3,3},{4,4},{5,5},{6,518},{7,519},{8,256},{9,257... | collective-permute-start | bytes 393224 | tf_op jit(solution)/shard_map/ppermute | solution.py:42
  54.5 15.1 %all-to-all-start.1 = ((bf16[4,4,128,128]{3,2,1,0:T(8,128)(2,1)}), bf16[4,4,128,128]{3,2,1,0:T(8,128)(2,1)S(1)}, u32[]{:S(2)}, u32[]{:S(2)}) async-start(bf16[4,4,128,128]{3,2,1,0:T(8,128)(2,1)} %broadcast_in_dim.25), calls=%async_computation.1 | async-start | bytes 1048576 | tf_op jit(solution)/shard_map/all_to_all | solution.py:21
  61.9 7.7 %collective-permute-start.3 = (bf16[4,128,128]{2,1,0:T(8,128)(2,1)S(1)}, bf16[4,128,128]{2,1,0:T(8,128)(2,1)S(1)}, u32[]{:S(2)}, u32[]{:S(2)}) collective-permute-start(bf16[4,128,128]{2,1,0:T(8,128)(2,1)S(1)} %bitcast.90), channel_id=1, source_target_pairs={{0,32},{32,0},{64,96},{96,64},{128,160},{160,128},{192,224},{224,1... | collective-permute-start | bytes 393224 | tf_op jit(solution)/shard_map/ppermute | solution.py:25
  69.6 7.5 %collective-permute-start.5 = (bf16[16,128,128]{2,1,0:T(8,128)(2,1)S(1)}, bf16[16,128,128]{2,1,0:T(8,128)(2,1)S(1)}, u32[]{:S(2)}, u32[]{:S(2)}) collective-permute-start(bf16[16,128,128]{2,1,0:T(8,128)(2,1)S(1)} %bitcast.85), channel_id=1, source_target_pairs={{0,1},{1,0},{2,3},{3,2},{4,5},{5,4},{6,7},{7,6},{8,9},{9,8},{10,11... | collective-permute-start | bytes 1572872 | tf_op jit(solution)/shard_map/ppermute | solution.py:25
  78.4 9.3 %all-to-all-start.2 = ((f32[4,128,128]{2,1,0:T(8,128)}), f32[4,128,128]{2,1,0:T(8,128)S(1)}, u32[]{:S(2)}, u32[]{:S(2)}) async-start(f32[4,128,128]{2,1,0:T(8,128)} %fusion.20), calls=%async_computation.2 | async-start | bytes 524288 | tf_op jit(solution)/shard_map/all_to_all | solution.py:81
  87.9 8.4 %collective-permute-start.6 = (f32[128,128]{0,1:T(8,128)S(1)}, f32[128,128]{0,1:T(8,128)S(1)}, u32[]{:S(2)}, u32[]{:S(2)}) collective-permute-start(f32[128,128]{0,1:T(8,128)S(1)} %copy.46), channel_id=1, source_target_pairs={{0,0},{1,32},{2,64},{3,96},{4,128},{5,160},{518,192},{519,224},{25... | collective-permute-start | bytes 196616 | tf_op jit(solution)/shard_map/ppermute | solution.py:42
  146.3 8.7 %collective-permute-start.7 = (f32[128,128]{0,1:T(8,128)S(1)}, f32[128,128]{0,1:T(8,128)S(1)}, u32[]{:S(2)}, u32[]{:S(2)}) collective-permute-start(f32[128,128]{0,1:T(8,128)S(1)} %copy.48), channel_id=1, source_target_pairs={{0,0},{1,32},{2,64},{3,96},{4,128},{5,160},{518,192},{519,224},{25... | collective-permute-start | bytes 196616 | tf_op jit(solution)/shard_map/ppermute | solution.py:42
  197.8 12.4 %collective-permute-start.8 = (f32[128,128]{0,1:T(8,128)S(1)}, f32[128,128]{0,1:T(8,128)S(1)}, u32[]{:S(2)}, u32[]{:S(2)}) collective-permute-start(f32[128,128]{0,1:T(8,128)S(1)} %copy.50), channel_id=1, source_target_pairs={{0,0},{1,32},{2,64},{3,96},{4,128},{5,160},{518,192},{519,224},{25... | collective-permute-start | bytes 196616 | tf_op jit(solution)/shard_map/ppermute | solution.py:42
  230.0 45.7 %all-to-all-start.8 = ((f32[32,1,128]{2,1,0:T(1,128)}), f32[32,1,128]{2,1,0:T(1,128)S(1)}, u32[]{:S(2)}, u32[]{:S(2)}) async-start(f32[32,1,128]{2,1,0:T(1,128)} %broadcast_in_dim.60), calls=%async_computation.8 | async-start | bytes 32768 | tf_op jit(solution)/shard_map/all_to_all | solution.py:21
  255.3 0.7 collective-permute-start.9

commit v9 on v8

--- a/solution.py
+++ b/solution.py
@@ -73,7 +73,8 @@
     col = (lax.axis_index("y") - shift + 4) % 4 * 8 + lax.axis_index(("h", "c"))
     gap_cols = lax.dynamic_slice_in_dim(orbital_gaps, col * n, n)
     delta = gap_rows[:, None] + gap_cols[None, :]
-    squares = []
+    lane = lax.broadcasted_iota(jnp.int32, (1, 128), 1)
+    local = jnp.zeros((1, 128), jnp.float32)
     for step in range(ITERS):
         if step:
             by_l = gather(amps.astype(jnp.bfloat16), "l", 8).reshape(-1, n)
@@ -81,13 +82,12 @@
         product = jnp.sum(lax.all_to_all(shares, "x", 0, 0, tiled=True), axis=0)
         paired = product + send(product, turned, turned.T).T
         residual = source + delta * amps + paired + amps * paired
-        squares.append(jnp.sum(residual * residual))
+        square = jnp.sum(jnp.sum(residual * residual, axis=0, keepdims=True), axis=1, keepdims=True)
+        local = jnp.where(lane == step, square, local)
         amps = amps - residual / delta
+        if step < ITERS - 1:
+            amps, local = lax.optimization_barrier((amps, local))
 
-    lane = lax.broadcasted_iota(jnp.int32, (1, 128), 1)
-    local = jnp.zeros((1, 128), jnp.float32)
-    for step, square in enumerate(squares):
-        local = jnp.where(lane == step, square, local)
     plane = jnp.sum(gather(local, ("y", "x", "c"), 32), axis=0)
     total = jnp.sum(gather(plane, ("l", "h"), 32), axis=0)
     norms = jnp.sqrt(total[0, :ITERS]) / (NO * NV)

time: 278 us -> 278 us (level)
  no operation moved by 1% of the time
where the time goes in v9:
time: 278 us; the launch traced here: 277 us
  starting transfers between devices  108 us (39%)
  blocking collectives  106 us (38%)
  waiting for transfers between devices  48.7 us (18%)
  other arithmetic  5.2 us (2%)
  local copies, waits for them, and re-layouts  4.91 us (2%)
    all_to_all x3, blocking collectives, gather(): return lax.all_to_all(copies, axes, 0, 0, tiled=True)  90.5 us
    all_to_all x3, starting transfers between devices, gather(): return lax.all_to_all(copies, axes, 0, 0, tiled=True)  61.5 us
    ppermute x7, starting transfers between devices, send(): lax.ppermute(tile, AXES, list(zip(source.ravel().tolist(), target.ravel()...  29.5 us
    all_to_all x3, waiting for transfers between devices, gather(): return lax.all_to_all(copies, axes, 0, 0, tiled=True)  25.7 us
    all_to_all x2, blocking collectives, body(): product = jnp.sum(lax.all_to_all(shares, 'x', 0, 0, tiled=True), axis=0)  15.9 us
    ppermute x3, starting transfers between devices, swap(): return lax.ppermute(tile, axis, [(i, i ^ bit) for i in range(size)])  13.9 us
    ppermute x7, waiting for transfers between devices, send(): lax.ppermute(tile, AXES, list(zip(source.ravel().tolist(), target.ravel()...  9.19 us
    ppermute x3, waiting for transfers between devices, swap(): return lax.ppermute(tile, axis, [(i, i ^ bit) for i in range(size)])  8 us
  transfers between devices with their start and end apart: 14, of which 10 were waited for; matrix products, arithmetic and copies ran while one was open for 1% of the time, Pallas kernels for 0%

profile of v9, /device:TPU:1, one launch (start us, length us, event | category | flops | bytes accessed | tf_op | source)
XLA Modules:
  0.0 276.8 jit_solution(10664837151376766486)
XLA Ops:
  0.6 0.9 copy.41
  2.2 29.0 %all-to-all-start = ((bf16[4,128,128]{2,1,0:T(8,128)(2,1)}), bf16[4,128,128]{2,1,0:T(8,128)(2,1)S(1)}, u32[]{:S(2)}, u32[]{:S(2)}) async-start(bf16[4,128,128]{2,1,0:T(8,128)(2,1)} %broadcast_in_dim.34), calls=%async_computation | async-start | bytes 262144 | tf_op jit(solution)/shard_map/all_to_all | solution.py:21
  31.2 4.0 %collective-permute-start.1 = (bf16[128,128]{1,0:T(8,128)(2,1)S(1)}, bf16[128,128]{1,0:T(8,128)(2,1)S(1)}, u32[]{:S(2)}, u32[]{:S(2)}) collective-permute-start(bf16[128,128]{1,0:T(8,128)(2,1)S(1)} %convert_element_type.9), channel_id=1, source_target_pairs={{0,128},{1,129},{2,130},{3,131},{4,132},{5,133},{6,646},{7,647},{8... | collective-permute-start | bytes 98312 | tf_op jit(solution)/shard_map/ppermute | solution.py:42
  35.9 4.1 %collective-permute-done.1 = bf16[128,128]{1,0:T(8,128)(2,1)S(1)} collective-permute-done((bf16[128,128]{1,0:T(8,128)(2,1)S(1)}, bf16[128,128]{1,0:T(8,128)(2,1)S(1)}, u32[]{:S(2)}, u32[]{:S(2)}) %collective-permute-start.1) | collective-permute-done | bytes 32800 | tf_op jit(solution)/shard_map/ppermute | solution.py:42
  40.0 2.9 %collective-permute-start.2 = (bf16[2,128,128]{2,1,0:T(8,128)(2,1)S(1)}, bf16[2,128,128]{2,1,0:T(8,128)(2,1)S(1)}, u32[]{:S(2)}, u32[]{:S(2)}) collective-permute-start(bf16[2,128,128]{2,1,0:T(8,128)(2,1)S(1)} %pad_maximum_fusion.3), channel_id=1, source_target_pairs={{0,64},{32,96},{64,0},{96,32},{128,192},{160,224},{192,128},{224,1... | collective-permute-start | bytes 196616 | tf_op jit(solution)/shard_map/ppermute | solution.py:25
  43.7 4.0 %collective-permute-done.2 = bf16[2,128,128]{2,1,0:T(8,128)(2,1)S(1)} collective-permute-done((bf16[2,128,128]{2,1,0:T(8,128)(2,1)S(1)}, bf16[2,128,128]{2,1,0:T(8,128)(2,1)S(1)}, u32[]{:S(2)}, u32[]{:S(2)}) %collective-permute-start.2) | collective-permute-done | bytes 65568 | tf_op jit(solution)/shard_map/ppermute | solution.py:25
  47.6 6.0 %all-to-all-done = bf16[4,128,128]{2,1,0:T(8,128)(2,1)S(1)} async-done(((bf16[4,128,128]{2,1,0:T(8,128)(2,1)}), bf16[4,128,128]{2,1,0:T(8,128)(2,1)S(1)}, u32[]{:S(2)}, u32[]{:S(2)}) %all-to-all-start) | async-done | bytes 131104 | tf_op jit(solution)/shard_map/all_to_all | solution.py:21
  53.6 0.9 broadcast_in_dim.35
  54.5 7.4 %all-to-all-start.1 = ((bf16[4,4,128,128]{3,2,1,0:T(8,128)(2,1)}), bf16[4,4,128,128]{3,2,1,0:T(8,128)(2,1)S(1)}, u32[]{:S(2)}, u32[]{:S(2)}) async-start(bf16[4,4,128,128]{3,2,1,0:T(8,128)(2,1)} %broadcast_in_dim.35), calls=%async_computation.1 | async-start | bytes 1048576 | tf_op jit(solution)/shard_map/all_to_all | solution.py:21
  61.9 5.1 %collective-permute-start.3 = (bf16[4,128,128]{2,1,0:T(8,128)(2,1)S(1)}, bf16[4,128,128]{2,1,0:T(8,128)(2,1)S(1)}, u32[]{:S(2)}, u32[]{:S(2)}) collective-permute-start(bf16[4,128,128]{2,1,0:T(8,128)(2,1)S(1)} %bitcast.91), channel_id=1, source_target_pairs={{0,32},{32,0},{64,96},{96,64},{128,160},{160,128},{192,224},{224,1... | collective-permute-start | bytes 393224 | tf_op jit(solution)/shard_map/ppermute | solution.py:25
  67.0 2.6 collective-permute-done.3
  69.6 5.9 %collective-permute-start.5 = (bf16[16,128,128]{2,1,0:T(8,128)(2,1)S(1)}, bf16[16,128,128]{2,1,0:T(8,128)(2,1)S(1)}, u32[]{:S(2)}, u32[]{:S(2)}) collective-permute-start(bf16[16,128,128]{2,1,0:T(8,128)(2,1)S(1)} %bitcast.86), channel_id=1, source_target_pairs={{0,1},{1,0},{2,3},{3,2},{4,5},{5,4},{6,7},{7,6},{8,9},{9,8},{10,11... | collective-permute-start | bytes 1572872 | tf_op jit(solution)/shard_map/ppermute | solution.py:25
  75.7 1.4 collective-permute-done.5
  77.3 1.2 fusion.17
  78.4 3.5 %all-to-all-start.2 = ((f32[4,128,128]{2,1,0:T(8,128)}), f32[4,128,128]{2,1,0:T(8,128)S(1)}, u32[]{:S(2)}, u32[]{:S(2)}) async-start(f32[4,128,128]{2,1,0:T(8,128)} %fusion.17), calls=%async_computation.2 | async-start | bytes 524288 | tf_op jit(solution)/shard_map/all_to_all | solution.py:82
  82.0 5.8 %all-to-all-done.2 = f32[4,128,128]{2,1,0:T(8,128)S(1)} async-done(((f32[4,128,128]{2,1,0:T(8,128)}), f32[4,128,128]{2,1,0:T(8,128)S(1)}, u32[]{:S(2)}, u32[]{:S(2)}) %all-to-all-start.2) | async-done | bytes 262176 | tf_op jit(solution)/shard_map/all_to_all | solution.py:82
  87.9 6.5 %collective-permute-start.6 = (f32[128,128]{0,1:T(8,128)S(1)}, f32[128,128]{0,1:T(8,128)S(1)}, u32[]{:S(2)}, u32[]{:S(2)}) collective-permute-start(f32[128,128]{0,1:T(8,128)S(1)} %copy.46), channel_id=1, source_target_pairs={{0,0},{1,32},{2,64},{3,96},{4,128},{5,160},{518,192},{519,224},{25... | collective-permute-start | bytes 196616 | tf_op jit(solution)/shard_map/ppermute | solution.py:42
  94.4 0.8 fusion.16
  95.2 1.1 collective-permute-done.6
  96.3 0.7 multiply_reduce_fusion.2
  97.8 40.7 %all_to_all.45 = bf16[8,128,128]{2,1,0:T(8,128)(2,1)S(1)} all-to-all(bf16[8,128,128]{2,1,0:T(8,128)(2,1)S(1)} %broadcast_in_dim.38), channel_id=1, replica_groups=mesh['y'=4,'l'=8,'x'=4,'h'=4,'c'=2] {'l'}, dimensions={0} | all-to-all | bytes 524288 | tf_op jit(solution)/shard_map/all_to_all | solution.py:21
  138.9 7.9 %all_to_all.46 = f32[4,128,128]{2,1,0:T(8,128)S(1)} all-to-all(f32[4,128,128]{2,1,0:T(8,128)S(1)} %fusion.18), channel_id=1, replica_groups=mesh['y'=4,'l'=8,'x'=4,'h'=4,'c'=2] {'x'}, dimensions={0} | all-to-all | bytes 524288 | tf_op jit(solution)/shard_map/all_to_all | solution.py:82
  147.0 6.7 %collective-permute-start.7 = (f32[128,128]{0,1:T(8,128)S(1)}, f32[128,128]{0,1:T(8,128)S(1)}, u32[]{:S(2)}, u32[]{:S(2)}) collective-permute-start(f32[128,128]{0,1:T(8,128)S(1)} %copy.48), channel_id=1, source_target_pairs={{0,0},{1,32},{2,64},{3,96},{4,128},{5,160},{518,192},{519,224},{25... | collective-permute-start | bytes 196616 | tf_op jit(solution)/shard_map/ppermute | solution.py:42
  153.7 1.9 collective-permute-done.7
  155.6 0.7 multiply_reduce_fusion.1
  157.1 33.5 %all_to_all.47 = bf16[8,128,128]{2,1,0:T(8,128)(2,1)S(1)} all-to-all(bf16[8,128,128]{2,1,0:T(8,128)(2,1)S(1)} %broadcast_in_dim.73), channel_id=1, replica_groups=mesh['y'=4,'l'=8,'x'=4,'h'=4,'c'=2] {'l'}, dimensions={0} | all-to-all | bytes 524288 | tf_op jit(solution)/shard_map/all_to_all | solution.py:21
  191.1 7.9 %all_to_all.48 = f32[4,128,128]{2,1,0:T(8,128)S(1)} all-to-all(f32[4,128,128]{2,1,0:T(8,128)S(1)} %fusion.19), channel_id=1, replica_groups=mesh['y'=4,'l'=8,'x'=4,'h'=4,'c'=2] {'x'}, dimensions={0} | all-to-all | bytes 524288 | tf_op jit(solution)/shard_map/all_to_all | solution.py:82
  199.1 10.3 %collective-permute-start.8 = (f32[128,128]{0,1:T(8,128)S(1)}, f32[128,128]{0,1:T(8,128)S(1)}, u32[]{:S(2)}, u32[]{:S(2)}) collective-permute-start(f32[128,128]{0,1:T(8,128)S(1)} %copy.50), channel_id=1, source_target_pairs={{0,0},{1,32},{2,64},{3,96},{4,128},{5,160},{518,192},{519,224},{25... | collective-permute-start | bytes 196616 | tf_op jit(solution)/shard_map/ppermute | solution.py:42
  209.5 2.1 collective-permute-done.8
  212.9 16.4 %all_to_all.49 = f32[32,1,128]{2,1,0:T(1,128)S(1)} all-to-all(f32[32,1,128]{2,1,0:T(1,128)S(1)} %broadcast_in_dim.76), channel_id=1, replica_groups=mesh['y'=4,'l'=8,'x'=4,'h'=4,'c'=2] {'y','x','c'}, dimensions={0} | all-to-all | bytes 32768 | tf_op jit(solution)/shard_map/all_to_all | solution.py:21
  229.9 25.2 %all-to-all-start.8 = ((f32[32,1,128]{2,1,0:T(1,128)}), f32[32,1,128]{2,1,0:T(1,128)S(1)}, u32[]{:S(2)}, u32[]{:S(2)}) async-start(f32[32,1,128]{2,1,0:T(1,128)} %broadcast_in_dim.77), calls=%async_computation.8 | async-start | bytes 32768 | tf_op jit(solution)/shard_map/all_to_all | solution.py:21
  255.9 19.8 %all-to-all-done.8 = f32[32,1,128]{2,1,0:T(1,128)S(1)} async-done(((f32[32,1,128]{2,1,0:T(1,128)}), f32[32,1,128]{2,1,0:T(1,128)S(1)}, u32[]{:S(2)}, u32[]{:S(2)}) %all-to-all-start.8) | async-done | bytes 16416 | tf_op jit(solution)/shard_map/all_to_all | solution.py:21
  (48 shorter events, 9.1 us)
Async XLA Ops:
  2.2 29.0 %copy-start = (f32[128,128]{1,0:T(8,128)S(1)}, f32[128,128]{1,0:T(8,128)}, u32[]{:S(2)}) copy-start(f32[128,128]{1,0:T(8,128)} %param.4) | copy-start | bytes 196612
  2.2 51.4 %all-to-all-start = ((bf16[4,128,128]{2,1,0:T(8,128)(2,1)}), bf16[4,128,128]{2,1,0:T(8,128)(2,1)S(1)}, u32[]{:S(2)}, u32[]{:S(2)}) async-start(bf16[4,128,128]{2,1,0:T(8,128)(2,1)} %broadcast_in_dim.34), calls=%async_computation | async-start | bytes 262144 | tf_op jit(solution)/shard_map/all_to_all | solution.py:21
  31.2 8.8 %collective-permute-start.1 = (bf16[128,128]{1,0:T(8,128)(2,1)S(1)}, bf16[128,128]{1,0:T(8,128)(2,1)S(1)}, u32[]{:S(2)}, u32[]{:S(2)}) collective-permute-start(bf16[128,128]{1,0:T(8,128)(2,1)S(1)} %convert_element_type.9), channel_id=1, source_target_pairs={{0,128},{1,129},{2,130},{3,131},{4,132},{5,133},{6,646},{7,647},{8... | collective-permute-start | bytes 98312 | tf_op jit(solution)/shard_map/ppermute | solution.py:42
  35.2 4.8 %collective-permute-start = (bf16[128,128]{1,0:T(8,128)(2,1)S(1)}, bf16[128,128]{1,0:T(8,128)(2,1)S(1)}, u32[]{:S(2)}, u32[]{:S(2)}) collective-permute-start(bf16[128,128]{1,0:T(8,128)(2,1)S(1)} %convert_element_type.9), channel_id=1, source_target_pairs={{0,0},{1,1},{2,2},{3,3},{4,4},{5,5},{6,518},{7,519},{8,256},{9,257... | collective-permute-start | bytes 98312 | tf_op jit(solution)/shard_map/ppermute | solution.py:42
  40.0 2.9 %copy-start.1 = (f32[128,128]{1,0:T(8,128)S(1)}, f32[128,128]{1,0:T(8,128)}, u32[]{:S(2)}) copy-start(f32[128,128]{1,0:T(8,128)} %param.6) | copy-start | bytes 196612
  40.0 7.6 %collective-permute-start.2 = (bf16[2,128,128]{2,1,0:T(8,128)(2,1)S(1)}, bf16[2,128,128]{2,1,0:T(8,128)(2,1)S(1)}, u32[]{:S(2)}, u32[]{:S(2)}) collective-permute-start(bf16[2,128,128]{2,1,0:T(8,128)(2,1)S(1)} %pad_maximum_fusion.3), channel_id=1, source_target_pairs={{0,64},{32,96},{64,0},{96,32},{128,192},{160,224},{192,128},{224,1... | collective-permute-start | bytes 196616 | tf_op jit(solution)/shard_map/ppermute | solution.py:25
  43.0 24.0 %collective-permute-start.4 = (f32[2,128,128]{2,1,0:T(8,128)S(1)}, f32[2,128,128]{2,1,0:T(8,128)S(1)}, u32[]{:S(2)}, u32[]{:S(2)}) collective-permute-start(f32[2,128,128]{2,1,0:T(8,128)S(1)} %pad_maximum_fusion.2), channel_id=1, source_target_pairs={{0,0},{1,1},{2,2},{3,3},{4,4},{5,5},{6,518},{7,519},{8,256},{9,257... | collective-permute-start | bytes 393224 | tf_op jit(solution)/shard_map/ppermute | solution.py:42
  54.5 15.1 %all-to-all-start.1 = ((bf16[4,4,128,128]{3,2,1,0:T(8,128)(2,1)}), bf16[4,4,128,128]{3,2,1,0:T(8,128)(2,1)S(1)}, u32[]{:S(2)}, u32[]{:S(2)}) async-start(bf16[4,4,128,128]{3,2,1,0:T(8,128)(2,1)} %broadcast_in_dim.35), calls=%async_computation.1 | async-start | bytes 1048576 | tf_op jit(solution)/shard_map/all_to_all | solution.py:21
  61.9 7.7 %collective-permute-start.3 = (bf16[4,128,128]{2,1,0:T(8,128)(2,1)S(1)}, bf16[4,128,128]{2,1,0:T(8,128)(2,1)S(1)}, u32[]{:S(2)}, u32[]{:S(2)}) collective-permute-start(bf16[4,128,128]{2,1,0:T(8,128)(2,1)S(1)} %bitcast.91), channel_id=1, source_target_pairs={{0,32},{32,0},{64,96},{96,64},{128,160},{160,128},{192,224},{224,1... | collective-permute-start | bytes 393224 | tf_op jit(solution)/shard_map/ppermute | solution.py:25
  69.6 7.5 %collective-permute-start.5 = (bf16[16,128,128]{2,1,0:T(8,128)(2,1)S(1)}, bf16[16,128,128]{2,1,0:T(8,128)(2,1)S(1)}, u32[]{:S(2)}, u32[]{:S(2)}) collective-permute-start(bf16[16,128,128]{2,1,0:T(8,128)(2,1)S(1)} %bitcast.86), channel_id=1, source_target_pairs={{0,1},{1,0},{2,3},{3,2},{4,5},{5,4},{6,7},{7,6},{8,9},{9,8},{10,11... | collective-permute-start | bytes 1572872 | tf_op jit(solution)/shard_map/ppermute | solution.py:25
  78.4 9.3 %all-to-all-start.2 = ((f32[4,128,128]{2,1,0:T(8,128)}), f32[4,128,128]{2,1,0:T(8,128)S(1)}, u32[]{:S(2)}, u32[]{:S(2)}) async-start(f32[4,128,128]{2,1,0:T(8,128)} %fusion.17), calls=%async_computation.2 | async-start | bytes 524288 | tf_op jit(solution)/shard_map/all_to_all | solution.py:82
  87.9 8.4 %collective-permute-start.6 = (f32[128,128]{0,1:T(8,128)S(1)}, f32[128,128]{0,1:T(8,128)S(1)}, u32[]{:S(2)}, u32[]{:S(2)}) collective-permute-start(f32[128,128]{0,1:T(8,128)S(1)} %copy.46), channel_id=1, source_target_pairs={{0,0},{1,32},{2,64},{3,96},{4,128},{5,160},{518,192},{519,224},{25... | collective-permute-start | bytes 196616 | tf_op jit(solution)/shard_map/ppermute | solution.py:42
  147.0 8.7 %collective-permute-start.7 = (f32[128,128]{0,1:T(8,128)S(1)}, f32[128,128]{0,1:T(8,128)S(1)}, u32[]{:S(2)}, u32[]{:S(2)}) collective-permute-start(f32[128,128]{0,1:T(8,128)S(1)} %copy.48), channel_id=1, source_target_pairs={{0,0},{1,32},{2,64},{3,96},{4,128},{5,160},{518,192},{519,224},{25... | collective-permute-start | bytes 196616 | tf_op jit(solution)/shard_map/ppermute | solution.py:42
  199.1 12.4 %collective-permute-start.8 = (f32[128,128]{0,1:T(8,128)S(1)}, f32[128,128]{0,1:T(8,128)S(1)}, u32[]{:S(2)}, u32[]{:S(2)}) collective-permute-start(f32[128,128]{0,1:T(8,128)S(1)} %copy.50), channel_id=1, source_target_pairs={{0,0},{1,32},{2,64},{3,96},{4,128},{5,160},{518,192},{519,224},{25... | collective-permute-start | bytes 196616 | tf_op jit(solution)/shard_map/ppermute | solution.py:42
  229.9 45.7 %all-to-all-start.8 = ((f32[32,1,128]{2,1,0:T(1,128)}), f32[32,1,128]{2,1,0:T(1,128)S(1)}, u32[]{:S(2)}, u32[]{:S(2)}) async-start(f32[32,1,128]{2,1,0:T(1,128)} %broadcast_in_dim.77), calls=%async_computation.8 | async-start | bytes 32768 | tf_op jit(solution)/shard_map/all_to_all | solution.py:21
  255.2 0.7 collective-permute-start.9

commit v10 on v9

--- a/solution.py
+++ b/solution.py
@@ -59,14 +59,14 @@
     four = jnp.swapaxes(ordered(two, other, l // 2 % 2), 0, 1).reshape(4, n, n)
     other = swap(four, "l", 8, 1)
     by_y = gather(quad, "y", 4).reshape(16, n, n)
-    state = send(jnp.stack([source, amplitudes]), start, turned)
-    four, other, by_y, state = lax.optimization_barrier((four, other, by_y, state))
+    four, other, by_y = lax.optimization_barrier((four, other, by_y))
     eight = ordered(four, other, l % 2)
     by_l = jnp.swapaxes(eight, 0, 1).reshape(-1, n)
     other = swap(by_y, "c", 2, 1)
     both = ordered(by_y, other, lax.axis_index("c"))
     part = jnp.swapaxes(both, 0, 1).reshape(4, -1, n)
 
+    state = send(jnp.stack([source, amplitudes]), start, turned)
     source, amps = state[0], state[1]
     gap_rows = lax.dynamic_slice_in_dim(orbital_gaps, lax.axis_index(("x", "l")) * n, n)
     shift = sum(jnp.where(h == i, SHIFT[i], 0) for i in range(SIZES[3]))
@@ -80,14 +80,16 @@
             by_l = gather(amps.astype(jnp.bfloat16), "l", 8).reshape(-1, n)
         shares = jnp.einsum("ykr,kc->yrc", part, by_l, preferred_element_type=jnp.float32)
         product = jnp.sum(lax.all_to_all(shares, "x", 0, 0, tiled=True), axis=0)
-        paired = product + send(product, turned, turned.T).T
+        mirror = send(product, turned, turned.T)
+        if step:
+            local = jnp.where(lane == step - 1, square, local)
+            mirror, local = lax.optimization_barrier((mirror, local))
+        paired = product + mirror.T
         residual = source + delta * amps + paired + amps * paired
-        square = jnp.sum(jnp.sum(residual * residual, axis=0, keepdims=True), axis=1, keepdims=True)
-        local = jnp.where(lane == step, square, local)
+        square = jnp.sum(residual * residual)
         amps = amps - residual / delta
-        if step < ITERS - 1:
-            amps, local = lax.optimization_barrier((amps, local))
 
+    local = jnp.where(lane == ITERS - 1, square, local)
     plane = jnp.sum(gather(local, ("y", "x", "c"), 32), axis=0)
     total = jnp.sum(gather(plane, ("l", "h"), 32), axis=0)
     norms = jnp.sqrt(total[0, :ITERS]) / (NO * NV)

time: 278 us -> 284 us (1.022)
  starting transfers between devices: 108 us -> 117 us
    all_to_all x3, starting transfers between devices: 61.5 us -> 69.5 us  [gather(): return lax.all_to_all(copies, axes, 0, 0, tiled=True)]
    all_to_all x3, blocking collectives: 90.5 us -> 86.9 us  [gather(): return lax.all_to_all(copies, axes, 0, 0, tiled=True)]
    all_to_all x2, blocking collectives: 15.9 us -> 18.9 us  [body(): product = jnp.sum(lax.all_to_all(shares, 'x', 0, 0, tiled=True), axis=0)]
    ppermute x3, starting transfers between devices: 13.9 us -> 17 us  [swap(): return lax.ppermute(tile, axis, [(i, i ^ bit) for i in range(size)])]
where the time goes in v10:
time: 284 us; the launch traced here: 283 us
  starting transfers between devices  117 us (41%)
  blocking collectives  106 us (37%)
  waiting for transfers between devices  46.8 us (16%)
  other arithmetic  5.19 us (2%)
  local copies, waits for them, and re-layouts  4.9 us (2%)
    all_to_all x3, blocking collectives, gather(): return lax.all_to_all(copies, axes, 0, 0, tiled=True)  86.9 us
    all_to_all x3, starting transfers between devices, gather(): return lax.all_to_all(copies, axes, 0, 0, tiled=True)  69.5 us
    ppermute x7, starting transfers between devices, send(): lax.ppermute(tile, AXES, list(zip(source.ravel().tolist(), target.ravel()...  27.4 us
    all_to_all x3, waiting for transfers between devices, gather(): return lax.all_to_all(copies, axes, 0, 0, tiled=True)  25.5 us
    all_to_all x2, blocking collectives, body(): product = jnp.sum(lax.all_to_all(shares, 'x', 0, 0, tiled=True), axis=0)  18.9 us
    ppermute x3, starting transfers between devices, swap(): return lax.ppermute(tile, axis, [(i, i ^ bit) for i in range(size)])  17 us
    ppermute x7, waiting for transfers between devices, send(): lax.ppermute(tile, AXES, list(zip(source.ravel().tolist(), target.ravel()...  8.17 us
    ppermute x3, waiting for transfers between devices, swap(): return lax.ppermute(tile, axis, [(i, i ^ bit) for i in range(size)])  8.04 us
  transfers between devices with their start and end apart: 14, of which 10 were waited for; matrix products, arithmetic and copies ran while one was open for 1% of the time, Pallas kernels for 0%

profile of v10, /device:TPU:1, one launch (start us, length us, event | category | flops | bytes accessed | tf_op | source)
XLA Modules:
  0.0 283.2 jit_solution(14855145696000383259)
XLA Ops:
  0.6 0.9 copy.41
  2.2 29.0 %all-to-all-start = ((bf16[4,128,128]{2,1,0:T(8,128)(2,1)}), bf16[4,128,128]{2,1,0:T(8,128)(2,1)S(1)}, u32[]{:S(2)}, u32[]{:S(2)}) async-start(bf16[4,128,128]{2,1,0:T(8,128)(2,1)} %broadcast_in_dim.26), calls=%async_computation | async-start | bytes 262144 | tf_op jit(solution)/shard_map/all_to_all | solution.py:21
  31.9 4.0 %collective-permute-start.2 = (bf16[128,128]{1,0:T(8,128)(2,1)S(1)}, bf16[128,128]{1,0:T(8,128)(2,1)S(1)}, u32[]{:S(2)}, u32[]{:S(2)}) collective-permute-start(bf16[128,128]{1,0:T(8,128)(2,1)S(1)} %convert_element_type.9), channel_id=1, source_target_pairs={{0,128},{1,129},{2,130},{3,131},{4,132},{5,133},{6,646},{7,647},{8... | collective-permute-start | bytes 98312 | tf_op jit(solution)/shard_map/ppermute | solution.py:42
  35.9 4.5 %collective-permute-done.2 = bf16[128,128]{1,0:T(8,128)(2,1)S(1)} collective-permute-done((bf16[128,128]{1,0:T(8,128)(2,1)S(1)}, bf16[128,128]{1,0:T(8,128)(2,1)S(1)}, u32[]{:S(2)}, u32[]{:S(2)}) %collective-permute-start.2) | collective-permute-done | bytes 32800 | tf_op jit(solution)/shard_map/ppermute | solution.py:42
  40.5 3.1 %collective-permute-start.3 = (bf16[2,128,128]{2,1,0:T(8,128)(2,1)S(1)}, bf16[2,128,128]{2,1,0:T(8,128)(2,1)S(1)}, u32[]{:S(2)}, u32[]{:S(2)}) collective-permute-start(bf16[2,128,128]{2,1,0:T(8,128)(2,1)S(1)} %pad_maximum_fusion.3), channel_id=1, source_target_pairs={{0,64},{32,96},{64,0},{96,32},{128,192},{160,224},{192,128},{224,1... | collective-permute-start | bytes 196616 | tf_op jit(solution)/shard_map/ppermute | solution.py:25
  43.6 4.3 %collective-permute-done.3 = bf16[2,128,128]{2,1,0:T(8,128)(2,1)S(1)} collective-permute-done((bf16[2,128,128]{2,1,0:T(8,128)(2,1)S(1)}, bf16[2,128,128]{2,1,0:T(8,128)(2,1)S(1)}, u32[]{:S(2)}, u32[]{:S(2)}) %collective-permute-start.3) | collective-permute-done | bytes 65568 | tf_op jit(solution)/shard_map/ppermute | solution.py:25
  47.9 5.7 %all-to-all-done = bf16[4,128,128]{2,1,0:T(8,128)(2,1)S(1)} async-done(((bf16[4,128,128]{2,1,0:T(8,128)(2,1)}), bf16[4,128,128]{2,1,0:T(8,128)(2,1)S(1)}, u32[]{:S(2)}, u32[]{:S(2)}) %all-to-all-start) | async-done | bytes 131104 | tf_op jit(solution)/shard_map/all_to_all | solution.py:21
  53.6 0.9 broadcast_in_dim.27
  54.5 7.8 %all-to-all-start.1 = ((bf16[4,4,128,128]{3,2,1,0:T(8,128)(2,1)}), bf16[4,4,128,128]{3,2,1,0:T(8,128)(2,1)S(1)}, u32[]{:S(2)}, u32[]{:S(2)}) async-start(bf16[4,4,128,128]{3,2,1,0:T(8,128)(2,1)} %broadcast_in_dim.27), calls=%async_computation.1 | async-start | bytes 1048576 | tf_op jit(solution)/shard_map/all_to_all | solution.py:21
  62.3 5.2 %collective-permute-start.4 = (bf16[4,128,128]{2,1,0:T(8,128)(2,1)S(1)}, bf16[4,128,128]{2,1,0:T(8,128)(2,1)S(1)}, u32[]{:S(2)}, u32[]{:S(2)}) collective-permute-start(bf16[4,128,128]{2,1,0:T(8,128)(2,1)S(1)} %bitcast.96), channel_id=1, source_target_pairs={{0,32},{32,0},{64,96},{96,64},{128,160},{160,128},{192,224},{224,1... | collective-permute-start | bytes 393224 | tf_op jit(solution)/shard_map/ppermute | solution.py:25
  67.5 2.3 collective-permute-done.4
  69.9 8.7 %collective-permute-start.5 = (bf16[16,128,128]{2,1,0:T(8,128)(2,1)S(1)}, bf16[16,128,128]{2,1,0:T(8,128)(2,1)S(1)}, u32[]{:S(2)}, u32[]{:S(2)}) collective-permute-start(bf16[16,128,128]{2,1,0:T(8,128)(2,1)S(1)} %bitcast.91), channel_id=1, source_target_pairs={{0,1},{1,0},{2,3},{3,2},{4,5},{5,4},{6,7},{7,6},{8,9},{9,8},{10,11... | collective-permute-start | bytes 1572872 | tf_op jit(solution)/shard_map/ppermute | solution.py:25
  78.6 1.4 collective-permute-done.5
  80.2 1.2 fusion.21
  81.4 3.6 %all-to-all-start.2 = ((f32[4,128,128]{2,1,0:T(8,128)}), f32[4,128,128]{2,1,0:T(8,128)S(1)}, u32[]{:S(2)}, u32[]{:S(2)}) async-start(f32[4,128,128]{2,1,0:T(8,128)} %fusion.21), calls=%async_computation.2 | async-start | bytes 524288 | tf_op jit(solution)/shard_map/all_to_all | solution.py:82
  85.7 5.1 %all-to-all-done.2 = f32[4,128,128]{2,1,0:T(8,128)S(1)} async-done(((f32[4,128,128]{2,1,0:T(8,128)}), f32[4,128,128]{2,1,0:T(8,128)S(1)}, u32[]{:S(2)}, u32[]{:S(2)}) %all-to-all-start.2) | async-done | bytes 262176 | tf_op jit(solution)/shard_map/all_to_all | solution.py:82
  90.9 4.4 %collective-permute-start.6 = (f32[128,128]{0,1:T(8,128)S(1)}, f32[128,128]{0,1:T(8,128)S(1)}, u32[]{:S(2)}, u32[]{:S(2)}) collective-permute-start(f32[128,128]{0,1:T(8,128)S(1)} %copy.46), channel_id=1, source_target_pairs={{0,0},{1,32},{2,64},{3,96},{4,128},{5,160},{518,192},{519,224},{25... | collective-permute-start | bytes 196616 | tf_op jit(solution)/shard_map/ppermute | solution.py:42
  95.3 0.8 fusion.20
  96.2 1.1 collective-permute-done.6
  97.3 0.7 multiply_reduce_fusion.2
  98.1 31.7 %all_to_all.45 = bf16[8,128,128]{2,1,0:T(8,128)(2,1)S(1)} all-to-all(bf16[8,128,128]{2,1,0:T(8,128)(2,1)S(1)} %broadcast_in_dim.28), channel_id=1, replica_groups=mesh['y'=4,'l'=8,'x'=4,'h'=4,'c'=2] {'l'}, dimensions={0} | all-to-all | bytes 524288 | tf_op jit(solution)/shard_map/all_to_all | solution.py:21
  130.3 11.0 %all_to_all.46 = f32[4,128,128]{2,1,0:T(8,128)S(1)} all-to-all(f32[4,128,128]{2,1,0:T(8,128)S(1)} %fusion.22), channel_id=1, replica_groups=mesh['y'=4,'l'=8,'x'=4,'h'=4,'c'=2] {'x'}, dimensions={0} | all-to-all | bytes 524288 | tf_op jit(solution)/shard_map/all_to_all | solution.py:82
  141.4 10.3 %collective-permute-start.7 = (f32[128,128]{0,1:T(8,128)S(1)}, f32[128,128]{0,1:T(8,128)S(1)}, u32[]{:S(2)}, u32[]{:S(2)}) collective-permute-start(f32[128,128]{0,1:T(8,128)S(1)} %copy.48), channel_id=1, source_target_pairs={{0,0},{1,32},{2,64},{3,96},{4,128},{5,160},{518,192},{519,224},{25... | collective-permute-start | bytes 196616 | tf_op jit(solution)/shard_map/ppermute | solution.py:42
  152.3 1.3 collective-permute-done.7
  154.5 40.6 %all_to_all.47 = bf16[8,128,128]{2,1,0:T(8,128)(2,1)S(1)} all-to-all(bf16[8,128,128]{2,1,0:T(8,128)(2,1)S(1)} %broadcast_in_dim.58), channel_id=1, replica_groups=mesh['y'=4,'l'=8,'x'=4,'h'=4,'c'=2] {'l'}, dimensions={0} | all-to-all | bytes 524288 | tf_op jit(solution)/shard_map/all_to_all | solution.py:21
  195.5 7.9 %all_to_all.48 = f32[4,128,128]{2,1,0:T(8,128)S(1)} all-to-all(f32[4,128,128]{2,1,0:T(8,128)S(1)} %fusion.23), channel_id=1, replica_groups=mesh['y'=4,'l'=8,'x'=4,'h'=4,'c'=2] {'x'}, dimensions={0} | all-to-all | bytes 524288 | tf_op jit(solution)/shard_map/all_to_all | solution.py:82
  203.6 6.7 %collective-permute-start.8 = (f32[128,128]{0,1:T(8,128)S(1)}, f32[128,128]{0,1:T(8,128)S(1)}, u32[]{:S(2)}, u32[]{:S(2)}) collective-permute-start(f32[128,128]{0,1:T(8,128)S(1)} %copy.50), channel_id=1, source_target_pairs={{0,0},{1,32},{2,64},{3,96},{4,128},{5,160},{518,192},{519,224},{25... | collective-permute-start | bytes 196616 | tf_op jit(solution)/shard_map/ppermute | solution.py:42
  211.0 1.3 collective-permute-done.8
  212.2 0.7 multiply_reduce_fusion
  213.6 14.6 %all_to_all.49 = f32[32,1,128]{2,1,0:T(1,128)S(1)} all-to-all(f32[32,1,128]{2,1,0:T(1,128)S(1)} %broadcast_in_dim.62), channel_id=1, replica_groups=mesh['y'=4,'l'=8,'x'=4,'h'=4,'c'=2] {'y','x','c'}, dimensions={0} | all-to-all | bytes 32768 | tf_op jit(solution)/shard_map/all_to_all | solution.py:21
  228.8 32.7 %all-to-all-start.8 = ((f32[32,1,128]{2,1,0:T(1,128)}), f32[32,1,128]{2,1,0:T(1,128)S(1)}, u32[]{:S(2)}, u32[]{:S(2)}) async-start(f32[32,1,128]{2,1,0:T(1,128)} %broadcast_in_dim.63), calls=%async_computation.8 | async-start | bytes 32768 | tf_op jit(solution)/shard_map/all_to_all | solution.py:21
  262.3 19.8 %all-to-all-done.8 = f32[32,1,128]{2,1,0:T(1,128)S(1)} async-done(((f32[32,1,128]{2,1,0:T(1,128)}), f32[32,1,128]{2,1,0:T(1,128)S(1)}, u32[]{:S(2)}, u32[]{:S(2)}) %all-to-all-start.8) | async-done | bytes 16416 | tf_op jit(solution)/shard_map/all_to_all | solution.py:21
  (46 shorter events, 9.1 us)
Async XLA Ops:
  2.2 29.0 %copy-start = (f32[128,128]{1,0:T(8,128)S(1)}, f32[128,128]{1,0:T(8,128)}, u32[]{:S(2)}) copy-start(f32[128,128]{1,0:T(8,128)} %param.4) | copy-start | bytes 196612
  2.2 51.4 %all-to-all-start = ((bf16[4,128,128]{2,1,0:T(8,128)(2,1)}), bf16[4,128,128]{2,1,0:T(8,128)(2,1)S(1)}, u32[]{:S(2)}, u32[]{:S(2)}) async-start(bf16[4,128,128]{2,1,0:T(8,128)(2,1)} %broadcast_in_dim.26), calls=%async_computation | async-start | bytes 262144 | tf_op jit(solution)/shard_map/all_to_all | solution.py:21
  31.2 4.7 %collective-permute-start.1 = (bf16[128,128]{1,0:T(8,128)(2,1)S(1)}, bf16[128,128]{1,0:T(8,128)(2,1)S(1)}, u32[]{:S(2)}, u32[]{:S(2)}) collective-permute-start(bf16[128,128]{1,0:T(8,128)(2,1)S(1)} %convert_element_type.9), channel_id=1, source_target_pairs={{0,0},{1,1},{2,2},{3,3},{4,4},{5,5},{6,518},{7,519},{8,256},{9,257... | collective-permute-start | bytes 98312 | tf_op jit(solution)/shard_map/ppermute | solution.py:42
  31.9 8.6 %collective-permute-start.2 = (bf16[128,128]{1,0:T(8,128)(2,1)S(1)}, bf16[128,128]{1,0:T(8,128)(2,1)S(1)}, u32[]{:S(2)}, u32[]{:S(2)}) collective-permute-start(bf16[128,128]{1,0:T(8,128)(2,1)S(1)} %convert_element_type.9), channel_id=1, source_target_pairs={{0,128},{1,129},{2,130},{3,131},{4,132},{5,133},{6,646},{7,647},{8... | collective-permute-start | bytes 98312 | tf_op jit(solution)/shard_map/ppermute | solution.py:42
  40.5 7.4 %collective-permute-start.3 = (bf16[2,128,128]{2,1,0:T(8,128)(2,1)S(1)}, bf16[2,128,128]{2,1,0:T(8,128)(2,1)S(1)}, u32[]{:S(2)}, u32[]{:S(2)}) collective-permute-start(bf16[2,128,128]{2,1,0:T(8,128)(2,1)S(1)} %pad_maximum_fusion.3), channel_id=1, source_target_pairs={{0,64},{32,96},{64,0},{96,32},{128,192},{160,224},{192,128},{224,1... | collective-permute-start | bytes 196616 | tf_op jit(solution)/shard_map/ppermute | solution.py:25
  54.5 15.4 %all-to-all-start.1 = ((bf16[4,4,128,128]{3,2,1,0:T(8,128)(2,1)}), bf16[4,4,128,128]{3,2,1,0:T(8,128)(2,1)S(1)}, u32[]{:S(2)}, u32[]{:S(2)}) async-start(bf16[4,4,128,128]{3,2,1,0:T(8,128)(2,1)} %broadcast_in_dim.27), calls=%async_computation.1 | async-start | bytes 1048576 | tf_op jit(solution)/shard_map/all_to_all | solution.py:21
  62.3 7.5 %collective-permute-start.4 = (bf16[4,128,128]{2,1,0:T(8,128)(2,1)S(1)}, bf16[4,128,128]{2,1,0:T(8,128)(2,1)S(1)}, u32[]{:S(2)}, u32[]{:S(2)}) collective-permute-start(bf16[4,128,128]{2,1,0:T(8,128)(2,1)S(1)} %bitcast.96), channel_id=1, source_target_pairs={{0,32},{32,0},{64,96},{96,64},{128,160},{160,128},{192,224},{224,1... | collective-permute-start | bytes 393224 | tf_op jit(solution)/shard_map/ppermute | solution.py:25
  69.9 10.2 %collective-permute-start.5 = (bf16[16,128,128]{2,1,0:T(8,128)(2,1)S(1)}, bf16[16,128,128]{2,1,0:T(8,128)(2,1)S(1)}, u32[]{:S(2)}, u32[]{:S(2)}) collective-permute-start(bf16[16,128,128]{2,1,0:T(8,128)(2,1)S(1)} %bitcast.91), channel_id=1, source_target_pairs={{0,1},{1,0},{2,3},{3,2},{4,5},{5,4},{6,7},{7,6},{8,9},{9,8},{10,11... | collective-permute-start | bytes 1572872 | tf_op jit(solution)/shard_map/ppermute | solution.py:25
  81.4 3.6 %copy-start.1 = (f32[128,128]{1,0:T(8,128)S(1)}, f32[128,128]{1,0:T(8,128)}, u32[]{:S(2)}) copy-start(f32[128,128]{1,0:T(8,128)} %param.6) | copy-start | bytes 196612
  81.4 9.4 %all-to-all-start.2 = ((f32[4,128,128]{2,1,0:T(8,128)}), f32[4,128,128]{2,1,0:T(8,128)S(1)}, u32[]{:S(2)}, u32[]{:S(2)}) async-start(f32[4,128,128]{2,1,0:T(8,128)} %fusion.21), calls=%async_computation.2 | async-start | bytes 524288 | tf_op jit(solution)/shard_map/all_to_all | solution.py:82
  85.0 11.2 %collective-permute-start = (f32[2,128,128]{2,1,0:T(8,128)S(1)}, f32[2,128,128]{2,1,0:T(8,128)S(1)}, u32[]{:S(2)}, u32[]{:S(2)}) collective-permute-start(f32[2,128,128]{2,1,0:T(8,128)S(1)} %pad_maximum_fusion.1), channel_id=1, source_target_pairs={{0,0},{1,1},{2,2},{3,3},{4,4},{5,5},{6,518},{7,519},{8,256},{9,257... | collective-permute-start | bytes 393224 | tf_op jit(solution)/shard_map/ppermute | solution.py:42
  90.9 6.4 %collective-permute-start.6 = (f32[128,128]{0,1:T(8,128)S(1)}, f32[128,128]{0,1:T(8,128)S(1)}, u32[]{:S(2)}, u32[]{:S(2)}) collective-permute-start(f32[128,128]{0,1:T(8,128)S(1)} %copy.46), channel_id=1, source_target_pairs={{0,0},{1,32},{2,64},{3,96},{4,128},{5,160},{518,192},{519,224},{25... | collective-permute-start | bytes 196616 | tf_op jit(solution)/shard_map/ppermute | solution.py:42
  141.4 12.2 %collective-permute-start.7 = (f32[128,128]{0,1:T(8,128)S(1)}, f32[128,128]{0,1:T(8,128)S(1)}, u32[]{:S(2)}, u32[]{:S(2)}) collective-permute-start(f32[128,128]{0,1:T(8,128)S(1)} %copy.48), channel_id=1, source_target_pairs={{0,0},{1,32},{2,64},{3,96},{4,128},{5,160},{518,192},{519,224},{25... | collective-permute-start | bytes 196616 | tf_op jit(solution)/shard_map/ppermute | solution.py:42
  203.6 8.7 %collective-permute-start.8 = (f32[128,128]{0,1:T(8,128)S(1)}, f32[128,128]{0,1:T(8,128)S(1)}, u32[]{:S(2)}, u32[]{:S(2)}) collective-permute-start(f32[128,128]{0,1:T(8,128)S(1)} %copy.50), channel_id=1, source_target_pairs={{0,0},{1,32},{2,64},{3,96},{4,128},{5,160},{518,192},{519,224},{25... | collective-permute-start | bytes 196616 | tf_op jit(solution)/shard_map/ppermute | solution.py:42
  228.8 53.2 %all-to-all-start.8 = ((f32[32,1,128]{2,1,0:T(1,128)}), f32[32,1,128]{2,1,0:T(1,128)S(1)}, u32[]{:S(2)}, u32[]{:S(2)}) async-start(f32[32,1,128]{2,1,0:T(1,128)} %broadcast_in_dim.63), calls=%async_computation.8 | async-start | bytes 32768 | tf_op jit(solution)/shard_map/all_to_all | solution.py:21
  261.6 0.7 collective-permute-start.9

commit v11 on v10

--- a/solution.py
+++ b/solution.py
@@ -51,8 +51,10 @@
     l = lax.axis_index("l")
     low = amplitudes.astype(jnp.bfloat16)
     across = turned[np.arange(SIDE) ^ 4]
-    own, other = send(low, start, turned), send(low, start, across)
-    two = ordered(own, other, l // 4)
+    other = send(low, start, across)
+    state = send(jnp.stack([source, amplitudes]), start, turned)
+    source, amps = state[0], state[1]
+    two = ordered(amps.astype(jnp.bfloat16), other, l // 4)
     other = swap(two, "l", 8, 2)
     quad = gather(block, "h", 4).reshape(4, n, n)
     two, other, quad = lax.optimization_barrier((two, other, quad))
@@ -66,8 +68,6 @@
     both = ordered(by_y, other, lax.axis_index("c"))
     part = jnp.swapaxes(both, 0, 1).reshape(4, -1, n)
 
-    state = send(jnp.stack([source, amplitudes]), start, turned)
-    source, amps = state[0], state[1]
     gap_rows = lax.dynamic_slice_in_dim(orbital_gaps, lax.axis_index(("x", "l")) * n, n)
     shift = sum(jnp.where(h == i, SHIFT[i], 0) for i in range(SIZES[3]))
     col = (lax.axis_index("y") - shift + 4) % 4 * 8 + lax.axis_index(("h", "c"))

time: 284 us -> 284 us (level)
    ppermute x7 -> x6, waiting for transfers between devices: 8.17 us -> 8.88 us  [send(): lax.ppermute(tile, AXES, list(zip(source.ravel().tolist(), target.ravel()...]
    ppermute x7 -> x6, starting transfers between devices: 27.4 us -> 27.3 us  [send(): lax.ppermute(tile, AXES, list(zip(source.ravel().tolist(), target.ravel()...]
  transfers between devices with their start and end apart: 14 -> 13, of which waited for: 10 -> 10; matrix products, arithmetic and copies ran while one was open for 1% -> 1% of each run, Pallas kernels for 0% -> 0%
where the time goes in v11:
time: 284 us; the launch traced here: 283 us
  starting transfers between devices  117 us (41%)
  blocking collectives  104 us (37%)
  waiting for transfers between devices  48.1 us (17%)
  other arithmetic  5.19 us (2%)
  local copies, waits for them, and re-layouts  4.9 us (2%)
    all_to_all x3, blocking collectives, gather(): return lax.all_to_all(copies, axes, 0, 0, tiled=True)  85.9 us
    all_to_all x3, starting transfers between devices, gather(): return lax.all_to_all(copies, axes, 0, 0, tiled=True)  69.5 us
    ppermute x6, starting transfers between devices, send(): lax.ppermute(tile, AXES, list(zip(source.ravel().tolist(), target.ravel()...  27.3 us
    all_to_all x3, waiting for transfers between devices, gather(): return lax.all_to_all(copies, axes, 0, 0, tiled=True)  25.4 us
    all_to_all x2, blocking collectives, body(): product = jnp.sum(lax.all_to_all(shares, 'x', 0, 0, tiled=True), axis=0)  18.6 us
    ppermute x3, starting transfers between devices, swap(): return lax.ppermute(tile, axis, [(i, i ^ bit) for i in range(size)])  16.9 us
    ppermute x6, waiting for transfers between devices, send(): lax.ppermute(tile, AXES, list(zip(source.ravel().tolist(), target.ravel()...  8.88 us
    ppermute x3, waiting for transfers between devices, swap(): return lax.ppermute(tile, axis, [(i, i ^ bit) for i in range(size)])  8.02 us
  transfers between devices with their start and end apart: 13, of which 10 were waited for; matrix products, arithmetic and copies ran while one was open for 1% of the time, Pallas kernels for 0%

profile of v11, /device:TPU:1, one launch (start us, length us, event | category | flops | bytes accessed | tf_op | source)
XLA Modules:
  0.0 283.0 jit_solution(3283238630724339263)
XLA Ops:
  0.6 0.9 copy.41
  2.2 29.0 %all-to-all-start = ((bf16[4,128,128]{2,1,0:T(8,128)(2,1)}), bf16[4,128,128]{2,1,0:T(8,128)(2,1)S(1)}, u32[]{:S(2)}, u32[]{:S(2)}) async-start(bf16[4,128,128]{2,1,0:T(8,128)(2,1)} %broadcast_in_dim.26), calls=%async_computation | async-start | bytes 262144 | tf_op jit(solution)/shard_map/all_to_all | solution.py:21
  31.9 4.0 %collective-permute-start.1 = (bf16[128,128]{1,0:T(8,128)(2,1)S(1)}, bf16[128,128]{1,0:T(8,128)(2,1)S(1)}, u32[]{:S(2)}, u32[]{:S(2)}) collective-permute-start(bf16[128,128]{1,0:T(8,128)(2,1)S(1)} %convert_element_type.13), channel_id=1, source_target_pairs={{0,128},{1,129},{2,130},{3,131},{4,132},{5,133},{6,646},{7,647},{8... | collective-permute-start | bytes 98312 | tf_op jit(solution)/shard_map/ppermute | solution.py:42
  35.9 4.5 %collective-permute-done.1 = bf16[128,128]{1,0:T(8,128)(2,1)S(1)} collective-permute-done((bf16[128,128]{1,0:T(8,128)(2,1)S(1)}, bf16[128,128]{1,0:T(8,128)(2,1)S(1)}, u32[]{:S(2)}, u32[]{:S(2)}) %collective-permute-start.1) | collective-permute-done | bytes 32800 | tf_op jit(solution)/shard_map/ppermute | solution.py:42
  40.5 3.1 %collective-permute-start.2 = (bf16[2,128,128]{2,1,0:T(8,128)(2,1)S(1)}, bf16[2,128,128]{2,1,0:T(8,128)(2,1)S(1)}, u32[]{:S(2)}, u32[]{:S(2)}) collective-permute-start(bf16[2,128,128]{2,1,0:T(8,128)(2,1)S(1)} %pad_maximum_fusion.2), channel_id=1, source_target_pairs={{0,64},{32,96},{64,0},{96,32},{128,192},{160,224},{192,128},{224,1... | collective-permute-start | bytes 196616 | tf_op jit(solution)/shard_map/ppermute | solution.py:25
  43.6 4.3 %collective-permute-done.2 = bf16[2,128,128]{2,1,0:T(8,128)(2,1)S(1)} collective-permute-done((bf16[2,128,128]{2,1,0:T(8,128)(2,1)S(1)}, bf16[2,128,128]{2,1,0:T(8,128)(2,1)S(1)}, u32[]{:S(2)}, u32[]{:S(2)}) %collective-permute-start.2) | collective-permute-done | bytes 65568 | tf_op jit(solution)/shard_map/ppermute | solution.py:25
  47.9 5.7 %all-to-all-done = bf16[4,128,128]{2,1,0:T(8,128)(2,1)S(1)} async-done(((bf16[4,128,128]{2,1,0:T(8,128)(2,1)}), bf16[4,128,128]{2,1,0:T(8,128)(2,1)S(1)}, u32[]{:S(2)}, u32[]{:S(2)}) %all-to-all-start) | async-done | bytes 131104 | tf_op jit(solution)/shard_map/all_to_all | solution.py:21
  53.6 0.9 broadcast_in_dim.27
  54.5 7.8 %all-to-all-start.1 = ((bf16[4,4,128,128]{3,2,1,0:T(8,128)(2,1)}), bf16[4,4,128,128]{3,2,1,0:T(8,128)(2,1)S(1)}, u32[]{:S(2)}, u32[]{:S(2)}) async-start(bf16[4,4,128,128]{3,2,1,0:T(8,128)(2,1)} %broadcast_in_dim.27), calls=%async_computation.1 | async-start | bytes 1048576 | tf_op jit(solution)/shard_map/all_to_all | solution.py:21
  62.3 5.2 %collective-permute-start.3 = (bf16[4,128,128]{2,1,0:T(8,128)(2,1)S(1)}, bf16[4,128,128]{2,1,0:T(8,128)(2,1)S(1)}, u32[]{:S(2)}, u32[]{:S(2)}) collective-permute-start(bf16[4,128,128]{2,1,0:T(8,128)(2,1)S(1)} %bitcast.100), channel_id=1, source_target_pairs={{0,32},{32,0},{64,96},{96,64},{128,160},{160,128},{192,224},{224,1... | collective-permute-start | bytes 393224 | tf_op jit(solution)/shard_map/ppermute | solution.py:25
  67.5 2.3 collective-permute-done.3
  69.9 8.6 %collective-permute-start.4 = (bf16[16,128,128]{2,1,0:T(8,128)(2,1)S(1)}, bf16[16,128,128]{2,1,0:T(8,128)(2,1)S(1)}, u32[]{:S(2)}, u32[]{:S(2)}) collective-permute-start(bf16[16,128,128]{2,1,0:T(8,128)(2,1)S(1)} %bitcast.95), channel_id=1, source_target_pairs={{0,1},{1,0},{2,3},{3,2},{4,5},{5,4},{6,7},{7,6},{8,9},{9,8},{10,11... | collective-permute-start | bytes 1572872 | tf_op jit(solution)/shard_map/ppermute | solution.py:25
  78.6 1.4 collective-permute-done.4
  80.2 1.2 fusion.22
  81.4 3.4 %all-to-all-start.2 = ((f32[4,128,128]{2,1,0:T(8,128)}), f32[4,128,128]{2,1,0:T(8,128)S(1)}, u32[]{:S(2)}, u32[]{:S(2)}) async-start(f32[4,128,128]{2,1,0:T(8,128)} %fusion.22), calls=%async_computation.2 | async-start | bytes 524288 | tf_op jit(solution)/shard_map/all_to_all | solution.py:82
  84.8 5.8 %all-to-all-done.2 = f32[4,128,128]{2,1,0:T(8,128)S(1)} async-done(((f32[4,128,128]{2,1,0:T(8,128)}), f32[4,128,128]{2,1,0:T(8,128)S(1)}, u32[]{:S(2)}, u32[]{:S(2)}) %all-to-all-start.2) | async-done | bytes 262176 | tf_op jit(solution)/shard_map/all_to_all | solution.py:82
  90.7 4.5 %collective-permute-start.5 = (f32[128,128]{0,1:T(8,128)S(1)}, f32[128,128]{0,1:T(8,128)S(1)}, u32[]{:S(2)}, u32[]{:S(2)}) collective-permute-start(f32[128,128]{0,1:T(8,128)S(1)} %copy.46), channel_id=1, source_target_pairs={{0,0},{1,32},{2,64},{3,96},{4,128},{5,160},{518,192},{519,224},{25... | collective-permute-start | bytes 196616 | tf_op jit(solution)/shard_map/ppermute | solution.py:42
  95.2 0.8 fusion.21
  96.1 1.1 collective-permute-done.5
  97.1 0.7 multiply_reduce_fusion.2
  98.0 32.0 %all_to_all.45 = bf16[8,128,128]{2,1,0:T(8,128)(2,1)S(1)} all-to-all(bf16[8,128,128]{2,1,0:T(8,128)(2,1)S(1)} %broadcast_in_dim.28), channel_id=1, replica_groups=mesh['y'=4,'l'=8,'x'=4,'h'=4,'c'=2] {'l'}, dimensions={0} | all-to-all | bytes 524288 | tf_op jit(solution)/shard_map/all_to_all | solution.py:21
  130.4 10.6 %all_to_all.46 = f32[4,128,128]{2,1,0:T(8,128)S(1)} all-to-all(f32[4,128,128]{2,1,0:T(8,128)S(1)} %fusion.23), channel_id=1, replica_groups=mesh['y'=4,'l'=8,'x'=4,'h'=4,'c'=2] {'x'}, dimensions={0} | all-to-all | bytes 524288 | tf_op jit(solution)/shard_map/all_to_all | solution.py:82
  141.2 10.3 %collective-permute-start.6 = (f32[128,128]{0,1:T(8,128)S(1)}, f32[128,128]{0,1:T(8,128)S(1)}, u32[]{:S(2)}, u32[]{:S(2)}) collective-permute-start(f32[128,128]{0,1:T(8,128)S(1)} %copy.48), channel_id=1, source_target_pairs={{0,0},{1,32},{2,64},{3,96},{4,128},{5,160},{518,192},{519,224},{25... | collective-permute-start | bytes 196616 | tf_op jit(solution)/shard_map/ppermute | solution.py:42
  152.1 1.3 collective-permute-done.6
  153.4 0.7 multiply_reduce_fusion.1
  154.2 39.8 %all_to_all.47 = bf16[8,128,128]{2,1,0:T(8,128)(2,1)S(1)} all-to-all(bf16[8,128,128]{2,1,0:T(8,128)(2,1)S(1)} %broadcast_in_dim.58), channel_id=1, replica_groups=mesh['y'=4,'l'=8,'x'=4,'h'=4,'c'=2] {'l'}, dimensions={0} | all-to-all | bytes 524288 | tf_op jit(solution)/shard_map/all_to_all | solution.py:21
  194.5 7.9 %all_to_all.48 = f32[4,128,128]{2,1,0:T(8,128)S(1)} all-to-all(f32[4,128,128]{2,1,0:T(8,128)S(1)} %fusion.24), channel_id=1, replica_groups=mesh['y'=4,'l'=8,'x'=4,'h'=4,'c'=2] {'x'}, dimensions={0} | all-to-all | bytes 524288 | tf_op jit(solution)/shard_map/all_to_all | solution.py:82
  202.6 7.2 %collective-permute-start.7 = (f32[128,128]{0,1:T(8,128)S(1)}, f32[128,128]{0,1:T(8,128)S(1)}, u32[]{:S(2)}, u32[]{:S(2)}) collective-permute-start(f32[128,128]{0,1:T(8,128)S(1)} %copy.50), channel_id=1, source_target_pairs={{0,0},{1,32},{2,64},{3,96},{4,128},{5,160},{518,192},{519,224},{25... | collective-permute-start | bytes 196616 | tf_op jit(solution)/shard_map/ppermute | solution.py:42
  210.4 2.0 collective-permute-done.7
  213.7 14.1 %all_to_all.49 = f32[32,1,128]{2,1,0:T(1,128)S(1)} all-to-all(f32[32,1,128]{2,1,0:T(1,128)S(1)} %broadcast_in_dim.62), channel_id=1, replica_groups=mesh['y'=4,'l'=8,'x'=4,'h'=4,'c'=2] {'y','x','c'}, dimensions={0} | all-to-all | bytes 32768 | tf_op jit(solution)/shard_map/all_to_all | solution.py:21
  228.5 32.7 %all-to-all-start.8 = ((f32[32,1,128]{2,1,0:T(1,128)}), f32[32,1,128]{2,1,0:T(1,128)S(1)}, u32[]{:S(2)}, u32[]{:S(2)}) async-start(f32[32,1,128]{2,1,0:T(1,128)} %broadcast_in_dim.63), calls=%async_computation.8 | async-start | bytes 32768 | tf_op jit(solution)/shard_map/all_to_all | solution.py:21
  262.0 19.8 %all-to-all-done.8 = f32[32,1,128]{2,1,0:T(1,128)S(1)} async-done(((f32[32,1,128]{2,1,0:T(1,128)}), f32[32,1,128]{2,1,0:T(1,128)S(1)}, u32[]{:S(2)}, u32[]{:S(2)}) %all-to-all-start.8) | async-done | bytes 16416 | tf_op jit(solution)/shard_map/all_to_all | solution.py:21
  (45 shorter events, 8.4 us)
Async XLA Ops:
  2.2 29.0 %copy-start = (f32[128,128]{1,0:T(8,128)S(1)}, f32[128,128]{1,0:T(8,128)}, u32[]{:S(2)}) copy-start(f32[128,128]{1,0:T(8,128)} %param.4) | copy-start | bytes 196612
  2.2 29.0 %copy-start.1 = (f32[128,128]{1,0:T(8,128)S(1)}, f32[128,128]{1,0:T(8,128)}, u32[]{:S(2)}) copy-start(f32[128,128]{1,0:T(8,128)} %param.6) | copy-start | bytes 196612
  2.2 51.4 %all-to-all-start = ((bf16[4,128,128]{2,1,0:T(8,128)(2,1)}), bf16[4,128,128]{2,1,0:T(8,128)(2,1)S(1)}, u32[]{:S(2)}, u32[]{:S(2)}) async-start(bf16[4,128,128]{2,1,0:T(8,128)(2,1)} %broadcast_in_dim.26), calls=%async_computation | async-start | bytes 262144 | tf_op jit(solution)/shard_map/all_to_all | solution.py:21
  31.2 9.3 %collective-permute-start = (f32[2,128,128]{2,1,0:T(8,128)S(1)}, f32[2,128,128]{2,1,0:T(8,128)S(1)}, u32[]{:S(2)}, u32[]{:S(2)}) collective-permute-start(f32[2,128,128]{2,1,0:T(8,128)S(1)} %pad_maximum_fusion.1), channel_id=1, source_target_pairs={{0,0},{1,1},{2,2},{3,3},{4,4},{5,5},{6,518},{7,519},{8,256},{9,257... | collective-permute-start | bytes 393224 | tf_op jit(solution)/shard_map/ppermute | solution.py:42
  31.9 8.6 %collective-permute-start.1 = (bf16[128,128]{1,0:T(8,128)(2,1)S(1)}, bf16[128,128]{1,0:T(8,128)(2,1)S(1)}, u32[]{:S(2)}, u32[]{:S(2)}) collective-permute-start(bf16[128,128]{1,0:T(8,128)(2,1)S(1)} %convert_element_type.13), channel_id=1, source_target_pairs={{0,128},{1,129},{2,130},{3,131},{4,132},{5,133},{6,646},{7,647},{8... | collective-permute-start | bytes 98312 | tf_op jit(solution)/shard_map/ppermute | solution.py:42
  40.5 7.4 %collective-permute-start.2 = (bf16[2,128,128]{2,1,0:T(8,128)(2,1)S(1)}, bf16[2,128,128]{2,1,0:T(8,128)(2,1)S(1)}, u32[]{:S(2)}, u32[]{:S(2)}) collective-permute-start(bf16[2,128,128]{2,1,0:T(8,128)(2,1)S(1)} %pad_maximum_fusion.2), channel_id=1, source_target_pairs={{0,64},{32,96},{64,0},{96,32},{128,192},{160,224},{192,128},{224,1... | collective-permute-start | bytes 196616 | tf_op jit(solution)/shard_map/ppermute | solution.py:25
  54.5 15.4 %all-to-all-start.1 = ((bf16[4,4,128,128]{3,2,1,0:T(8,128)(2,1)}), bf16[4,4,128,128]{3,2,1,0:T(8,128)(2,1)S(1)}, u32[]{:S(2)}, u32[]{:S(2)}) async-start(bf16[4,4,128,128]{3,2,1,0:T(8,128)(2,1)} %broadcast_in_dim.27), calls=%async_computation.1 | async-start | bytes 1048576 | tf_op jit(solution)/shard_map/all_to_all | solution.py:21
  62.3 7.5 %collective-permute-start.3 = (bf16[4,128,128]{2,1,0:T(8,128)(2,1)S(1)}, bf16[4,128,128]{2,1,0:T(8,128)(2,1)S(1)}, u32[]{:S(2)}, u32[]{:S(2)}) collective-permute-start(bf16[4,128,128]{2,1,0:T(8,128)(2,1)S(1)} %bitcast.100), channel_id=1, source_target_pairs={{0,32},{32,0},{64,96},{96,64},{128,160},{160,128},{192,224},{224,1... | collective-permute-start | bytes 393224 | tf_op jit(solution)/shard_map/ppermute | solution.py:25
  69.9 10.2 %collective-permute-start.4 = (bf16[16,128,128]{2,1,0:T(8,128)(2,1)S(1)}, bf16[16,128,128]{2,1,0:T(8,128)(2,1)S(1)}, u32[]{:S(2)}, u32[]{:S(2)}) collective-permute-start(bf16[16,128,128]{2,1,0:T(8,128)(2,1)S(1)} %bitcast.95), channel_id=1, source_target_pairs={{0,1},{1,0},{2,3},{3,2},{4,5},{5,4},{6,7},{7,6},{8,9},{9,8},{10,11... | collective-permute-start | bytes 1572872 | tf_op jit(solution)/shard_map/ppermute | solution.py:25
  81.4 9.2 %all-to-all-start.2 = ((f32[4,128,128]{2,1,0:T(8,128)}), f32[4,128,128]{2,1,0:T(8,128)S(1)}, u32[]{:S(2)}, u32[]{:S(2)}) async-start(f32[4,128,128]{2,1,0:T(8,128)} %fusion.22), calls=%async_computation.2 | async-start | bytes 524288 | tf_op jit(solution)/shard_map/all_to_all | solution.py:82
  90.7 6.4 %collective-permute-start.5 = (f32[128,128]{0,1:T(8,128)S(1)}, f32[128,128]{0,1:T(8,128)S(1)}, u32[]{:S(2)}, u32[]{:S(2)}) collective-permute-start(f32[128,128]{0,1:T(8,128)S(1)} %copy.46), channel_id=1, source_target_pairs={{0,0},{1,32},{2,64},{3,96},{4,128},{5,160},{518,192},{519,224},{25... | collective-permute-start | bytes 196616 | tf_op jit(solution)/shard_map/ppermute | solution.py:42
  141.2 12.2 %collective-permute-start.6 = (f32[128,128]{0,1:T(8,128)S(1)}, f32[128,128]{0,1:T(8,128)S(1)}, u32[]{:S(2)}, u32[]{:S(2)}) collective-permute-start(f32[128,128]{0,1:T(8,128)S(1)} %copy.48), channel_id=1, source_target_pairs={{0,0},{1,32},{2,64},{3,96},{4,128},{5,160},{518,192},{519,224},{25... | collective-permute-start | bytes 196616 | tf_op jit(solution)/shard_map/ppermute | solution.py:42
  202.6 9.8 %collective-permute-start.7 = (f32[128,128]{0,1:T(8,128)S(1)}, f32[128,128]{0,1:T(8,128)S(1)}, u32[]{:S(2)}, u32[]{:S(2)}) collective-permute-start(f32[128,128]{0,1:T(8,128)S(1)} %copy.50), channel_id=1, source_target_pairs={{0,0},{1,32},{2,64},{3,96},{4,128},{5,160},{518,192},{519,224},{25... | collective-permute-start | bytes 196616 | tf_op jit(solution)/shard_map/ppermute | solution.py:42
  228.5 53.3 %all-to-all-start.8 = ((f32[32,1,128]{2,1,0:T(1,128)}), f32[32,1,128]{2,1,0:T(1,128)S(1)}, u32[]{:S(2)}, u32[]{:S(2)}) async-start(f32[32,1,128]{2,1,0:T(1,128)} %broadcast_in_dim.63), calls=%async_computation.8 | async-start | bytes 32768 | tf_op jit(solution)/shard_map/all_to_all | solution.py:21
  261.3 0.7 collective-permute-start.8

commit v12 on v10

--- a/solution.py
+++ b/solution.py
@@ -59,14 +59,14 @@
     four = jnp.swapaxes(ordered(two, other, l // 2 % 2), 0, 1).reshape(4, n, n)
     other = swap(four, "l", 8, 1)
     by_y = gather(quad, "y", 4).reshape(16, n, n)
-    four, other, by_y = lax.optimization_barrier((four, other, by_y))
+    state = send(jnp.stack([source, amplitudes]), start, turned)
+    four, other, by_y, state = lax.optimization_barrier((four, other, by_y, state))
     eight = ordered(four, other, l % 2)
     by_l = jnp.swapaxes(eight, 0, 1).reshape(-1, n)
     other = swap(by_y, "c", 2, 1)
     both = ordered(by_y, other, lax.axis_index("c"))
     part = jnp.swapaxes(both, 0, 1).reshape(4, -1, n)
 
-    state = send(jnp.stack([source, amplitudes]), start, turned)
     source, amps = state[0], state[1]
     gap_rows = lax.dynamic_slice_in_dim(orbital_gaps, lax.axis_index(("x", "l")) * n, n)
     shift = sum(jnp.where(h == i, SHIFT[i], 0) for i in range(SIZES[3]))

time: 284 us -> 276 us (0.972)
  starting transfers between devices: 117 us -> 109 us
    all_to_all x3, starting transfers between devices: 69.5 us -> 61.5 us  [gather(): return lax.all_to_all(copies, axes, 0, 0, tiled=True)]
    all_to_all x3, blocking collectives: 86.9 us -> 90.4 us  [gather(): return lax.all_to_all(copies, axes, 0, 0, tiled=True)]
    all_to_all x2, blocking collectives: 18.9 us -> 15.9 us  [body(): product = jnp.sum(lax.all_to_all(shares, 'x', 0, 0, tiled=True), axis=0)]
    ppermute x3, starting transfers between devices: 17 us -> 13.9 us  [swap(): return lax.ppermute(tile, axis, [(i, i ^ bit) for i in range(size)])]
where the time goes in v12:
time: 276 us; the launch traced here: 275 us
  starting transfers between devices  109 us (39%)
  blocking collectives  106 us (38%)
  waiting for transfers between devices  47.4 us (17%)
  other arithmetic  5.19 us (2%)
  local copies, waits for them, and re-layouts  4.9 us (2%)
    all_to_all x3, blocking collectives, gather(): return lax.all_to_all(copies, axes, 0, 0, tiled=True)  90.4 us
    all_to_all x3, starting transfers between devices, gather(): return lax.all_to_all(copies, axes, 0, 0, tiled=True)  61.5 us
    ppermute x7, starting transfers between devices, send(): lax.ppermute(tile, AXES, list(zip(source.ravel().tolist(), target.ravel()...  29.6 us
    all_to_all x3, waiting for transfers between devices, gather(): return lax.all_to_all(copies, axes, 0, 0, tiled=True)  25.7 us
    all_to_all x2, blocking collectives, body(): product = jnp.sum(lax.all_to_all(shares, 'x', 0, 0, tiled=True), axis=0)  15.9 us
    ppermute x3, starting transfers between devices, swap(): return lax.ppermute(tile, axis, [(i, i ^ bit) for i in range(size)])  13.9 us
    ppermute x3, waiting for transfers between devices, swap(): return lax.ppermute(tile, axis, [(i, i ^ bit) for i in range(size)])  8 us
    ppermute x7, waiting for transfers between devices, send(): lax.ppermute(tile, AXES, list(zip(source.ravel().tolist(), target.ravel()...  7.88 us
  transfers between devices with their start and end apart: 14, of which 10 were waited for; matrix products, arithmetic and copies ran while one was open for 1% of the time, Pallas kernels for 0%

profile of v12, /device:TPU:1, one launch (start us, length us, event | category | flops | bytes accessed | tf_op | source)
XLA Modules:
  0.0 275.5 jit_solution(13577390256032734282)
XLA Ops:
  0.6 0.9 copy.41
  2.2 29.0 %all-to-all-start = ((bf16[4,128,128]{2,1,0:T(8,128)(2,1)}), bf16[4,128,128]{2,1,0:T(8,128)(2,1)S(1)}, u32[]{:S(2)}, u32[]{:S(2)}) async-start(bf16[4,128,128]{2,1,0:T(8,128)(2,1)} %broadcast_in_dim.26), calls=%async_computation | async-start | bytes 262144 | tf_op jit(solution)/shard_map/all_to_all | solution.py:21
  31.2 4.0 %collective-permute-start.1 = (bf16[128,128]{1,0:T(8,128)(2,1)S(1)}, bf16[128,128]{1,0:T(8,128)(2,1)S(1)}, u32[]{:S(2)}, u32[]{:S(2)}) collective-permute-start(bf16[128,128]{1,0:T(8,128)(2,1)S(1)} %convert_element_type.9), channel_id=1, source_target_pairs={{0,128},{1,129},{2,130},{3,131},{4,132},{5,133},{6,646},{7,647},{8... | collective-permute-start | bytes 98312 | tf_op jit(solution)/shard_map/ppermute | solution.py:42
  35.9 4.1 %collective-permute-done.1 = bf16[128,128]{1,0:T(8,128)(2,1)S(1)} collective-permute-done((bf16[128,128]{1,0:T(8,128)(2,1)S(1)}, bf16[128,128]{1,0:T(8,128)(2,1)S(1)}, u32[]{:S(2)}, u32[]{:S(2)}) %collective-permute-start.1) | collective-permute-done | bytes 32800 | tf_op jit(solution)/shard_map/ppermute | solution.py:42
  40.0 2.9 %collective-permute-start.2 = (bf16[2,128,128]{2,1,0:T(8,128)(2,1)S(1)}, bf16[2,128,128]{2,1,0:T(8,128)(2,1)S(1)}, u32[]{:S(2)}, u32[]{:S(2)}) collective-permute-start(bf16[2,128,128]{2,1,0:T(8,128)(2,1)S(1)} %pad_maximum_fusion.3), channel_id=1, source_target_pairs={{0,64},{32,96},{64,0},{96,32},{128,192},{160,224},{192,128},{224,1... | collective-permute-start | bytes 196616 | tf_op jit(solution)/shard_map/ppermute | solution.py:25
  43.7 4.0 %collective-permute-done.2 = bf16[2,128,128]{2,1,0:T(8,128)(2,1)S(1)} collective-permute-done((bf16[2,128,128]{2,1,0:T(8,128)(2,1)S(1)}, bf16[2,128,128]{2,1,0:T(8,128)(2,1)S(1)}, u32[]{:S(2)}, u32[]{:S(2)}) %collective-permute-start.2) | collective-permute-done | bytes 65568 | tf_op jit(solution)/shard_map/ppermute | solution.py:25
  47.6 6.0 %all-to-all-done = bf16[4,128,128]{2,1,0:T(8,128)(2,1)S(1)} async-done(((bf16[4,128,128]{2,1,0:T(8,128)(2,1)}), bf16[4,128,128]{2,1,0:T(8,128)(2,1)S(1)}, u32[]{:S(2)}, u32[]{:S(2)}) %all-to-all-start) | async-done | bytes 131104 | tf_op jit(solution)/shard_map/all_to_all | solution.py:21
  53.6 0.9 broadcast_in_dim.27
  54.5 7.4 %all-to-all-start.1 = ((bf16[4,4,128,128]{3,2,1,0:T(8,128)(2,1)}), bf16[4,4,128,128]{3,2,1,0:T(8,128)(2,1)S(1)}, u32[]{:S(2)}, u32[]{:S(2)}) async-start(bf16[4,4,128,128]{3,2,1,0:T(8,128)(2,1)} %broadcast_in_dim.27), calls=%async_computation.1 | async-start | bytes 1048576 | tf_op jit(solution)/shard_map/all_to_all | solution.py:21
  61.9 5.1 %collective-permute-start.3 = (bf16[4,128,128]{2,1,0:T(8,128)(2,1)S(1)}, bf16[4,128,128]{2,1,0:T(8,128)(2,1)S(1)}, u32[]{:S(2)}, u32[]{:S(2)}) collective-permute-start(bf16[4,128,128]{2,1,0:T(8,128)(2,1)S(1)} %bitcast.92), channel_id=1, source_target_pairs={{0,32},{32,0},{64,96},{96,64},{128,160},{160,128},{192,224},{224,1... | collective-permute-start | bytes 393224 | tf_op jit(solution)/shard_map/ppermute | solution.py:25
  67.0 2.6 collective-permute-done.3
  69.6 5.9 %collective-permute-start.5 = (bf16[16,128,128]{2,1,0:T(8,128)(2,1)S(1)}, bf16[16,128,128]{2,1,0:T(8,128)(2,1)S(1)}, u32[]{:S(2)}, u32[]{:S(2)}) collective-permute-start(bf16[16,128,128]{2,1,0:T(8,128)(2,1)S(1)} %bitcast.87), channel_id=1, source_target_pairs={{0,1},{1,0},{2,3},{3,2},{4,5},{5,4},{6,7},{7,6},{8,9},{9,8},{10,11... | collective-permute-start | bytes 1572872 | tf_op jit(solution)/shard_map/ppermute | solution.py:25
  75.7 1.4 collective-permute-done.5
  77.2 1.2 fusion.21
  78.4 3.5 %all-to-all-start.2 = ((f32[4,128,128]{2,1,0:T(8,128)}), f32[4,128,128]{2,1,0:T(8,128)S(1)}, u32[]{:S(2)}, u32[]{:S(2)}) async-start(f32[4,128,128]{2,1,0:T(8,128)} %fusion.21), calls=%async_computation.2 | async-start | bytes 524288 | tf_op jit(solution)/shard_map/all_to_all | solution.py:82
  82.0 5.8 %all-to-all-done.2 = f32[4,128,128]{2,1,0:T(8,128)S(1)} async-done(((f32[4,128,128]{2,1,0:T(8,128)}), f32[4,128,128]{2,1,0:T(8,128)S(1)}, u32[]{:S(2)}, u32[]{:S(2)}) %all-to-all-start.2) | async-done | bytes 262176 | tf_op jit(solution)/shard_map/all_to_all | solution.py:82
  87.9 6.5 %collective-permute-start.6 = (f32[128,128]{0,1:T(8,128)S(1)}, f32[128,128]{0,1:T(8,128)S(1)}, u32[]{:S(2)}, u32[]{:S(2)}) collective-permute-start(f32[128,128]{0,1:T(8,128)S(1)} %copy.46), channel_id=1, source_target_pairs={{0,0},{1,32},{2,64},{3,96},{4,128},{5,160},{518,192},{519,224},{25... | collective-permute-start | bytes 196616 | tf_op jit(solution)/shard_map/ppermute | solution.py:42
  94.4 0.8 fusion.20
  95.2 1.1 collective-permute-done.6
  96.3 0.7 multiply_reduce_fusion.2
  97.1 40.7 %all_to_all.45 = bf16[8,128,128]{2,1,0:T(8,128)(2,1)S(1)} all-to-all(bf16[8,128,128]{2,1,0:T(8,128)(2,1)S(1)} %broadcast_in_dim.28), channel_id=1, replica_groups=mesh['y'=4,'l'=8,'x'=4,'h'=4,'c'=2] {'l'}, dimensions={0} | all-to-all | bytes 524288 | tf_op jit(solution)/shard_map/all_to_all | solution.py:21
  138.3 7.9 %all_to_all.46 = f32[4,128,128]{2,1,0:T(8,128)S(1)} all-to-all(f32[4,128,128]{2,1,0:T(8,128)S(1)} %fusion.22), channel_id=1, replica_groups=mesh['y'=4,'l'=8,'x'=4,'h'=4,'c'=2] {'x'}, dimensions={0} | all-to-all | bytes 524288 | tf_op jit(solution)/shard_map/all_to_all | solution.py:82
  146.3 6.7 %collective-permute-start.7 = (f32[128,128]{0,1:T(8,128)S(1)}, f32[128,128]{0,1:T(8,128)S(1)}, u32[]{:S(2)}, u32[]{:S(2)}) collective-permute-start(f32[128,128]{0,1:T(8,128)S(1)} %copy.48), channel_id=1, source_target_pairs={{0,0},{1,32},{2,64},{3,96},{4,128},{5,160},{518,192},{519,224},{25... | collective-permute-start | bytes 196616 | tf_op jit(solution)/shard_map/ppermute | solution.py:42
  153.7 1.3 collective-permute-done.7
  155.0 0.7 multiply_reduce_fusion.1
  155.8 33.5 %all_to_all.47 = bf16[8,128,128]{2,1,0:T(8,128)(2,1)S(1)} all-to-all(bf16[8,128,128]{2,1,0:T(8,128)(2,1)S(1)} %broadcast_in_dim.58), channel_id=1, replica_groups=mesh['y'=4,'l'=8,'x'=4,'h'=4,'c'=2] {'l'}, dimensions={0} | all-to-all | bytes 524288 | tf_op jit(solution)/shard_map/all_to_all | solution.py:21
  189.7 7.9 %all_to_all.48 = f32[4,128,128]{2,1,0:T(8,128)S(1)} all-to-all(f32[4,128,128]{2,1,0:T(8,128)S(1)} %fusion.23), channel_id=1, replica_groups=mesh['y'=4,'l'=8,'x'=4,'h'=4,'c'=2] {'x'}, dimensions={0} | all-to-all | bytes 524288 | tf_op jit(solution)/shard_map/all_to_all | solution.py:82
  197.8 10.3 %collective-permute-start.8 = (f32[128,128]{0,1:T(8,128)S(1)}, f32[128,128]{0,1:T(8,128)S(1)}, u32[]{:S(2)}, u32[]{:S(2)}) collective-permute-start(f32[128,128]{0,1:T(8,128)S(1)} %copy.50), channel_id=1, source_target_pairs={{0,0},{1,32},{2,64},{3,96},{4,128},{5,160},{518,192},{519,224},{25... | collective-permute-start | bytes 196616 | tf_op jit(solution)/shard_map/ppermute | solution.py:42
  208.8 1.4 collective-permute-done.8
  211.6 16.3 %all_to_all.49 = f32[32,1,128]{2,1,0:T(1,128)S(1)} all-to-all(f32[32,1,128]{2,1,0:T(1,128)S(1)} %broadcast_in_dim.62), channel_id=1, replica_groups=mesh['y'=4,'l'=8,'x'=4,'h'=4,'c'=2] {'y','x','c'}, dimensions={0} | all-to-all | bytes 32768 | tf_op jit(solution)/shard_map/all_to_all | solution.py:21
  228.6 25.2 %all-to-all-start.8 = ((f32[32,1,128]{2,1,0:T(1,128)}), f32[32,1,128]{2,1,0:T(1,128)S(1)}, u32[]{:S(2)}, u32[]{:S(2)}) async-start(f32[32,1,128]{2,1,0:T(1,128)} %broadcast_in_dim.63), calls=%async_computation.8 | async-start | bytes 32768 | tf_op jit(solution)/shard_map/all_to_all | solution.py:21
  254.5 19.8 %all-to-all-done.8 = f32[32,1,128]{2,1,0:T(1,128)S(1)} async-done(((f32[32,1,128]{2,1,0:T(1,128)}), f32[32,1,128]{2,1,0:T(1,128)S(1)}, u32[]{:S(2)}, u32[]{:S(2)}) %all-to-all-start.8) | async-done | bytes 16416 | tf_op jit(solution)/shard_map/all_to_all | solution.py:21
  (46 shorter events, 9.1 us)
Async XLA Ops:
  2.2 29.0 %copy-start = (f32[128,128]{1,0:T(8,128)S(1)}, f32[128,128]{1,0:T(8,128)}, u32[]{:S(2)}) copy-start(f32[128,128]{1,0:T(8,128)} %param.4) | copy-start | bytes 196612
  2.2 51.4 %all-to-all-start = ((bf16[4,128,128]{2,1,0:T(8,128)(2,1)}), bf16[4,128,128]{2,1,0:T(8,128)(2,1)S(1)}, u32[]{:S(2)}, u32[]{:S(2)}) async-start(bf16[4,128,128]{2,1,0:T(8,128)(2,1)} %broadcast_in_dim.26), calls=%async_computation | async-start | bytes 262144 | tf_op jit(solution)/shard_map/all_to_all | solution.py:21
  31.2 8.8 %collective-permute-start.1 = (bf16[128,128]{1,0:T(8,128)(2,1)S(1)}, bf16[128,128]{1,0:T(8,128)(2,1)S(1)}, u32[]{:S(2)}, u32[]{:S(2)}) collective-permute-start(bf16[128,128]{1,0:T(8,128)(2,1)S(1)} %convert_element_type.9), channel_id=1, source_target_pairs={{0,128},{1,129},{2,130},{3,131},{4,132},{5,133},{6,646},{7,647},{8... | collective-permute-start | bytes 98312 | tf_op jit(solution)/shard_map/ppermute | solution.py:42
  35.2 4.8 %collective-permute-start = (bf16[128,128]{1,0:T(8,128)(2,1)S(1)}, bf16[128,128]{1,0:T(8,128)(2,1)S(1)}, u32[]{:S(2)}, u32[]{:S(2)}) collective-permute-start(bf16[128,128]{1,0:T(8,128)(2,1)S(1)} %convert_element_type.9), channel_id=1, source_target_pairs={{0,0},{1,1},{2,2},{3,3},{4,4},{5,5},{6,518},{7,519},{8,256},{9,257... | collective-permute-start | bytes 98312 | tf_op jit(solution)/shard_map/ppermute | solution.py:42
  40.0 2.9 %copy-start.1 = (f32[128,128]{1,0:T(8,128)S(1)}, f32[128,128]{1,0:T(8,128)}, u32[]{:S(2)}) copy-start(f32[128,128]{1,0:T(8,128)} %param.6) | copy-start | bytes 196612
  40.0 7.6 %collective-permute-start.2 = (bf16[2,128,128]{2,1,0:T(8,128)(2,1)S(1)}, bf16[2,128,128]{2,1,0:T(8,128)(2,1)S(1)}, u32[]{:S(2)}, u32[]{:S(2)}) collective-permute-start(bf16[2,128,128]{2,1,0:T(8,128)(2,1)S(1)} %pad_maximum_fusion.3), channel_id=1, source_target_pairs={{0,64},{32,96},{64,0},{96,32},{128,192},{160,224},{192,128},{224,1... | collective-permute-start | bytes 196616 | tf_op jit(solution)/shard_map/ppermute | solution.py:25
  43.0 24.0 %collective-permute-start.4 = (f32[2,128,128]{2,1,0:T(8,128)S(1)}, f32[2,128,128]{2,1,0:T(8,128)S(1)}, u32[]{:S(2)}, u32[]{:S(2)}) collective-permute-start(f32[2,128,128]{2,1,0:T(8,128)S(1)} %pad_maximum_fusion.2), channel_id=1, source_target_pairs={{0,0},{1,1},{2,2},{3,3},{4,4},{5,5},{6,518},{7,519},{8,256},{9,257... | collective-permute-start | bytes 393224 | tf_op jit(solution)/shard_map/ppermute | solution.py:42
  54.5 15.1 %all-to-all-start.1 = ((bf16[4,4,128,128]{3,2,1,0:T(8,128)(2,1)}), bf16[4,4,128,128]{3,2,1,0:T(8,128)(2,1)S(1)}, u32[]{:S(2)}, u32[]{:S(2)}) async-start(bf16[4,4,128,128]{3,2,1,0:T(8,128)(2,1)} %broadcast_in_dim.27), calls=%async_computation.1 | async-start | bytes 1048576 | tf_op jit(solution)/shard_map/all_to_all | solution.py:21
  61.9 7.7 %collective-permute-start.3 = (bf16[4,128,128]{2,1,0:T(8,128)(2,1)S(1)}, bf16[4,128,128]{2,1,0:T(8,128)(2,1)S(1)}, u32[]{:S(2)}, u32[]{:S(2)}) collective-permute-start(bf16[4,128,128]{2,1,0:T(8,128)(2,1)S(1)} %bitcast.92), channel_id=1, source_target_pairs={{0,32},{32,0},{64,96},{96,64},{128,160},{160,128},{192,224},{224,1... | collective-permute-start | bytes 393224 | tf_op jit(solution)/shard_map/ppermute | solution.py:25
  69.6 7.5 %collective-permute-start.5 = (bf16[16,128,128]{2,1,0:T(8,128)(2,1)S(1)}, bf16[16,128,128]{2,1,0:T(8,128)(2,1)S(1)}, u32[]{:S(2)}, u32[]{:S(2)}) collective-permute-start(bf16[16,128,128]{2,1,0:T(8,128)(2,1)S(1)} %bitcast.87), channel_id=1, source_target_pairs={{0,1},{1,0},{2,3},{3,2},{4,5},{5,4},{6,7},{7,6},{8,9},{9,8},{10,11... | collective-permute-start | bytes 1572872 | tf_op jit(solution)/shard_map/ppermute | solution.py:25
  78.4 9.3 %all-to-all-start.2 = ((f32[4,128,128]{2,1,0:T(8,128)}), f32[4,128,128]{2,1,0:T(8,128)S(1)}, u32[]{:S(2)}, u32[]{:S(2)}) async-start(f32[4,128,128]{2,1,0:T(8,128)} %fusion.21), calls=%async_computation.2 | async-start | bytes 524288 | tf_op jit(solution)/shard_map/all_to_all | solution.py:82
  87.9 8.4 %collective-permute-start.6 = (f32[128,128]{0,1:T(8,128)S(1)}, f32[128,128]{0,1:T(8,128)S(1)}, u32[]{:S(2)}, u32[]{:S(2)}) collective-permute-start(f32[128,128]{0,1:T(8,128)S(1)} %copy.46), channel_id=1, source_target_pairs={{0,0},{1,32},{2,64},{3,96},{4,128},{5,160},{518,192},{519,224},{25... | collective-permute-start | bytes 196616 | tf_op jit(solution)/shard_map/ppermute | solution.py:42
  146.3 8.7 %collective-permute-start.7 = (f32[128,128]{0,1:T(8,128)S(1)}, f32[128,128]{0,1:T(8,128)S(1)}, u32[]{:S(2)}, u32[]{:S(2)}) collective-permute-start(f32[128,128]{0,1:T(8,128)S(1)} %copy.48), channel_id=1, source_target_pairs={{0,0},{1,32},{2,64},{3,96},{4,128},{5,160},{518,192},{519,224},{25... | collective-permute-start | bytes 196616 | tf_op jit(solution)/shard_map/ppermute | solution.py:42
  197.8 12.4 %collective-permute-start.8 = (f32[128,128]{0,1:T(8,128)S(1)}, f32[128,128]{0,1:T(8,128)S(1)}, u32[]{:S(2)}, u32[]{:S(2)}) collective-permute-start(f32[128,128]{0,1:T(8,128)S(1)} %copy.50), channel_id=1, source_target_pairs={{0,0},{1,32},{2,64},{3,96},{4,128},{5,160},{518,192},{519,224},{25... | collective-permute-start | bytes 196616 | tf_op jit(solution)/shard_map/ppermute | solution.py:42
  228.6 45.7 %all-to-all-start.8 = ((f32[32,1,128]{2,1,0:T(1,128)}), f32[32,1,128]{2,1,0:T(1,128)S(1)}, u32[]{:S(2)}, u32[]{:S(2)}) async-start(f32[32,1,128]{2,1,0:T(1,128)} %broadcast_in_dim.63), calls=%async_computation.8 | async-start | bytes 32768 | tf_op jit(solution)/shard_map/all_to_all | solution.py:21
  253.8 0.7 collective-permute-start.9

commit v13 on v12

--- a/solution.py
+++ b/solution.py
@@ -90,10 +90,12 @@
         amps = amps - residual / delta
 
     local = jnp.where(lane == ITERS - 1, square, local)
-    plane = jnp.sum(gather(local, ("y", "x", "c"), 32), axis=0)
+    moved = send(amps, turned, start)
+    plane, moved = lax.optimization_barrier((gather(local, ("y", "x", "c"), 32), moved))
+    plane = jnp.sum(plane, axis=0)
     total = jnp.sum(gather(plane, ("l", "h"), 32), axis=0)
     norms = jnp.sqrt(total[0, :ITERS]) / (NO * NV)
-    return (send(amps, turned, start), norms)
+    return (moved, norms)
 
 
 def solution(mesh):

time: 276 us -> 281 us (1.018)
  blocking collectives: 106 us -> 110 us
    all_to_all x3, blocking collectives: 90.4 us -> 94.6 us  [gather(): return lax.all_to_all(copies, axes, 0, 0, tiled=True)]
where the time goes in v13:
time: 281 us; the launch traced here: 280 us
  blocking collectives  110 us (39%)
  starting transfers between devices  109 us (39%)
  waiting for transfers between devices  48.2 us (17%)
  other arithmetic  5.15 us (2%)
  local copies, waits for them, and re-layouts  4.9 us (2%)
    all_to_all x3, blocking collectives, gather(): return lax.all_to_all(copies, axes, 0, 0, tiled=True)  94.6 us
    all_to_all x3, starting transfers between devices, gather(): return lax.all_to_all(copies, axes, 0, 0, tiled=True)  61.5 us
    ppermute x7, starting transfers between devices, send(): lax.ppermute(tile, AXES, list(zip(source.ravel().tolist(), target.ravel()...  29.6 us
    all_to_all x3, waiting for transfers between devices, gather(): return lax.all_to_all(copies, axes, 0, 0, tiled=True)  26.5 us
    all_to_all x2, blocking collectives, body(): product = jnp.sum(lax.all_to_all(shares, 'x', 0, 0, tiled=True), axis=0)  15.9 us
    ppermute x3, starting transfers between devices, swap(): return lax.ppermute(tile, axis, [(i, i ^ bit) for i in range(size)])  13.9 us
    ppermute x3, waiting for transfers between devices, swap(): return lax.ppermute(tile, axis, [(i, i ^ bit) for i in range(size)])  8 us
    ppermute x7, waiting for transfers between devices, send(): lax.ppermute(tile, AXES, list(zip(source.ravel().tolist(), target.ravel()...  7.87 us
  transfers between devices with their start and end apart: 14, of which 10 were waited for; matrix products, arithmetic and copies ran while one was open for 1% of the time, Pallas kernels for 0%

profile of v13, /device:TPU:1, one launch (start us, length us, event | category | flops | bytes accessed | tf_op | source)
XLA Modules:
  0.0 280.4 jit_solution(16854230396973311648)
XLA Ops:
  0.6 0.9 copy.41
  2.2 29.0 %all-to-all-start = ((bf16[4,128,128]{2,1,0:T(8,128)(2,1)}), bf16[4,128,128]{2,1,0:T(8,128)(2,1)S(1)}, u32[]{:S(2)}, u32[]{:S(2)}) async-start(bf16[4,128,128]{2,1,0:T(8,128)(2,1)} %broadcast_in_dim.26), calls=%async_computation | async-start | bytes 262144 | tf_op jit(solution)/shard_map/all_to_all | solution.py:21
  31.2 4.0 %collective-permute-start.1 = (bf16[128,128]{1,0:T(8,128)(2,1)S(1)}, bf16[128,128]{1,0:T(8,128)(2,1)S(1)}, u32[]{:S(2)}, u32[]{:S(2)}) collective-permute-start(bf16[128,128]{1,0:T(8,128)(2,1)S(1)} %convert_element_type.9), channel_id=1, source_target_pairs={{0,128},{1,129},{2,130},{3,131},{4,132},{5,133},{6,646},{7,647},{8... | collective-permute-start | bytes 98312 | tf_op jit(solution)/shard_map/ppermute | solution.py:42
  35.9 4.1 %collective-permute-done.1 = bf16[128,128]{1,0:T(8,128)(2,1)S(1)} collective-permute-done((bf16[128,128]{1,0:T(8,128)(2,1)S(1)}, bf16[128,128]{1,0:T(8,128)(2,1)S(1)}, u32[]{:S(2)}, u32[]{:S(2)}) %collective-permute-start.1) | collective-permute-done | bytes 32800 | tf_op jit(solution)/shard_map/ppermute | solution.py:42
  40.0 2.9 %collective-permute-start.2 = (bf16[2,128,128]{2,1,0:T(8,128)(2,1)S(1)}, bf16[2,128,128]{2,1,0:T(8,128)(2,1)S(1)}, u32[]{:S(2)}, u32[]{:S(2)}) collective-permute-start(bf16[2,128,128]{2,1,0:T(8,128)(2,1)S(1)} %pad_maximum_fusion.3), channel_id=1, source_target_pairs={{0,64},{32,96},{64,0},{96,32},{128,192},{160,224},{192,128},{224,1... | collective-permute-start | bytes 196616 | tf_op jit(solution)/shard_map/ppermute | solution.py:25
  43.7 4.0 %collective-permute-done.2 = bf16[2,128,128]{2,1,0:T(8,128)(2,1)S(1)} collective-permute-done((bf16[2,128,128]{2,1,0:T(8,128)(2,1)S(1)}, bf16[2,128,128]{2,1,0:T(8,128)(2,1)S(1)}, u32[]{:S(2)}, u32[]{:S(2)}) %collective-permute-start.2) | collective-permute-done | bytes 65568 | tf_op jit(solution)/shard_map/ppermute | solution.py:25
  47.6 6.0 %all-to-all-done = bf16[4,128,128]{2,1,0:T(8,128)(2,1)S(1)} async-done(((bf16[4,128,128]{2,1,0:T(8,128)(2,1)}), bf16[4,128,128]{2,1,0:T(8,128)(2,1)S(1)}, u32[]{:S(2)}, u32[]{:S(2)}) %all-to-all-start) | async-done | bytes 131104 | tf_op jit(solution)/shard_map/all_to_all | solution.py:21
  53.6 0.9 broadcast_in_dim.27
  54.5 7.4 %all-to-all-start.1 = ((bf16[4,4,128,128]{3,2,1,0:T(8,128)(2,1)}), bf16[4,4,128,128]{3,2,1,0:T(8,128)(2,1)S(1)}, u32[]{:S(2)}, u32[]{:S(2)}) async-start(bf16[4,4,128,128]{3,2,1,0:T(8,128)(2,1)} %broadcast_in_dim.27), calls=%async_computation.1 | async-start | bytes 1048576 | tf_op jit(solution)/shard_map/all_to_all | solution.py:21
  61.9 5.1 %collective-permute-start.3 = (bf16[4,128,128]{2,1,0:T(8,128)(2,1)S(1)}, bf16[4,128,128]{2,1,0:T(8,128)(2,1)S(1)}, u32[]{:S(2)}, u32[]{:S(2)}) collective-permute-start(bf16[4,128,128]{2,1,0:T(8,128)(2,1)S(1)} %bitcast.91), channel_id=1, source_target_pairs={{0,32},{32,0},{64,96},{96,64},{128,160},{160,128},{192,224},{224,1... | collective-permute-start | bytes 393224 | tf_op jit(solution)/shard_map/ppermute | solution.py:25
  67.0 2.6 collective-permute-done.3
  69.6 5.9 %collective-permute-start.5 = (bf16[16,128,128]{2,1,0:T(8,128)(2,1)S(1)}, bf16[16,128,128]{2,1,0:T(8,128)(2,1)S(1)}, u32[]{:S(2)}, u32[]{:S(2)}) collective-permute-start(bf16[16,128,128]{2,1,0:T(8,128)(2,1)S(1)} %bitcast.86), channel_id=1, source_target_pairs={{0,1},{1,0},{2,3},{3,2},{4,5},{5,4},{6,7},{7,6},{8,9},{9,8},{10,11... | collective-permute-start | bytes 1572872 | tf_op jit(solution)/shard_map/ppermute | solution.py:25
  75.7 1.4 collective-permute-done.5
  77.2 1.2 fusion.21
  78.4 3.5 %all-to-all-start.2 = ((f32[4,128,128]{2,1,0:T(8,128)}), f32[4,128,128]{2,1,0:T(8,128)S(1)}, u32[]{:S(2)}, u32[]{:S(2)}) async-start(f32[4,128,128]{2,1,0:T(8,128)} %fusion.21), calls=%async_computation.2 | async-start | bytes 524288 | tf_op jit(solution)/shard_map/all_to_all | solution.py:82
  82.0 5.8 %all-to-all-done.2 = f32[4,128,128]{2,1,0:T(8,128)S(1)} async-done(((f32[4,128,128]{2,1,0:T(8,128)}), f32[4,128,128]{2,1,0:T(8,128)S(1)}, u32[]{:S(2)}, u32[]{:S(2)}) %all-to-all-start.2) | async-done | bytes 262176 | tf_op jit(solution)/shard_map/all_to_all | solution.py:82
  87.9 6.5 %collective-permute-start.6 = (f32[128,128]{0,1:T(8,128)S(1)}, f32[128,128]{0,1:T(8,128)S(1)}, u32[]{:S(2)}, u32[]{:S(2)}) collective-permute-start(f32[128,128]{0,1:T(8,128)S(1)} %copy.46), channel_id=1, source_target_pairs={{0,0},{1,32},{2,64},{3,96},{4,128},{5,160},{518,192},{519,224},{25... | collective-permute-start | bytes 196616 | tf_op jit(solution)/shard_map/ppermute | solution.py:42
  94.4 0.8 fusion.20
  95.2 1.1 collective-permute-done.6
  96.3 0.7 multiply_reduce_fusion.2
  97.1 40.6 %all_to_all.45 = bf16[8,128,128]{2,1,0:T(8,128)(2,1)S(1)} all-to-all(bf16[8,128,128]{2,1,0:T(8,128)(2,1)S(1)} %broadcast_in_dim.28), channel_id=1, replica_groups=mesh['y'=4,'l'=8,'x'=4,'h'=4,'c'=2] {'l'}, dimensions={0} | all-to-all | bytes 524288 | tf_op jit(solution)/shard_map/all_to_all | solution.py:21
  138.2 7.9 %all_to_all.46 = f32[4,128,128]{2,1,0:T(8,128)S(1)} all-to-all(f32[4,128,128]{2,1,0:T(8,128)S(1)} %fusion.22), channel_id=1, replica_groups=mesh['y'=4,'l'=8,'x'=4,'h'=4,'c'=2] {'x'}, dimensions={0} | all-to-all | bytes 524288 | tf_op jit(solution)/shard_map/all_to_all | solution.py:82
  146.2 6.8 %collective-permute-start.7 = (f32[128,128]{0,1:T(8,128)S(1)}, f32[128,128]{0,1:T(8,128)S(1)}, u32[]{:S(2)}, u32[]{:S(2)}) collective-permute-start(f32[128,128]{0,1:T(8,128)S(1)} %copy.48), channel_id=1, source_target_pairs={{0,0},{1,32},{2,64},{3,96},{4,128},{5,160},{518,192},{519,224},{25... | collective-permute-start | bytes 196616 | tf_op jit(solution)/shard_map/ppermute | solution.py:42
  153.6 1.3 collective-permute-done.7
  154.9 0.7 multiply_reduce_fusion.1
  155.7 33.5 %all_to_all.47 = bf16[8,128,128]{2,1,0:T(8,128)(2,1)S(1)} all-to-all(bf16[8,128,128]{2,1,0:T(8,128)(2,1)S(1)} %broadcast_in_dim.58), channel_id=1, replica_groups=mesh['y'=4,'l'=8,'x'=4,'h'=4,'c'=2] {'l'}, dimensions={0} | all-to-all | bytes 524288 | tf_op jit(solution)/shard_map/all_to_all | solution.py:21
  189.7 7.9 %all_to_all.48 = f32[4,128,128]{2,1,0:T(8,128)S(1)} all-to-all(f32[4,128,128]{2,1,0:T(8,128)S(1)} %fusion.23), channel_id=1, replica_groups=mesh['y'=4,'l'=8,'x'=4,'h'=4,'c'=2] {'x'}, dimensions={0} | all-to-all | bytes 524288 | tf_op jit(solution)/shard_map/all_to_all | solution.py:82
  197.8 10.3 %collective-permute-start.8 = (f32[128,128]{0,1:T(8,128)S(1)}, f32[128,128]{0,1:T(8,128)S(1)}, u32[]{:S(2)}, u32[]{:S(2)}) collective-permute-start(f32[128,128]{0,1:T(8,128)S(1)} %copy.50), channel_id=1, source_target_pairs={{0,0},{1,32},{2,64},{3,96},{4,128},{5,160},{518,192},{519,224},{25... | collective-permute-start | bytes 196616 | tf_op jit(solution)/shard_map/ppermute | solution.py:42
  208.8 1.4 collective-permute-done.8
  212.3 20.5 %all_to_all.49 = f32[32,1,128]{2,1,0:T(1,128)S(1)} all-to-all(f32[32,1,128]{2,1,0:T(1,128)S(1)} %broadcast_in_dim.62), channel_id=1, replica_groups=mesh['y'=4,'l'=8,'x'=4,'h'=4,'c'=2] {'y','x','c'}, dimensions={0} | all-to-all | bytes 32768 | tf_op jit(solution)/shard_map/all_to_all | solution.py:21
  233.5 25.2 %all-to-all-start.8 = ((f32[32,1,128]{2,1,0:T(1,128)}), f32[32,1,128]{2,1,0:T(1,128)S(1)}, u32[]{:S(2)}, u32[]{:S(2)}) async-start(f32[32,1,128]{2,1,0:T(1,128)} %broadcast_in_dim.63), calls=%async_computation.8 | async-start | bytes 32768 | tf_op jit(solution)/shard_map/all_to_all | solution.py:21
  258.7 20.6 %all-to-all-done.8 = f32[32,1,128]{2,1,0:T(1,128)S(1)} async-done(((f32[32,1,128]{2,1,0:T(1,128)}), f32[32,1,128]{2,1,0:T(1,128)S(1)}, u32[]{:S(2)}, u32[]{:S(2)}) %all-to-all-start.8) | async-done | bytes 16416 | tf_op jit(solution)/shard_map/all_to_all | solution.py:21
  (46 shorter events, 9.0 us)
Async XLA Ops:
  2.2 29.0 %copy-start = (f32[128,128]{1,0:T(8,128)S(1)}, f32[128,128]{1,0:T(8,128)}, u32[]{:S(2)}) copy-start(f32[128,128]{1,0:T(8,128)} %param.4) | copy-start | bytes 196612
  2.2 51.4 %all-to-all-start = ((bf16[4,128,128]{2,1,0:T(8,128)(2,1)}), bf16[4,128,128]{2,1,0:T(8,128)(2,1)S(1)}, u32[]{:S(2)}, u32[]{:S(2)}) async-start(bf16[4,128,128]{2,1,0:T(8,128)(2,1)} %broadcast_in_dim.26), calls=%async_computation | async-start | bytes 262144 | tf_op jit(solution)/shard_map/all_to_all | solution.py:21
  31.2 8.8 %collective-permute-start.1 = (bf16[128,128]{1,0:T(8,128)(2,1)S(1)}, bf16[128,128]{1,0:T(8,128)(2,1)S(1)}, u32[]{:S(2)}, u32[]{:S(2)}) collective-permute-start(bf16[128,128]{1,0:T(8,128)(2,1)S(1)} %convert_element_type.9), channel_id=1, source_target_pairs={{0,128},{1,129},{2,130},{3,131},{4,132},{5,133},{6,646},{7,647},{8... | collective-permute-start | bytes 98312 | tf_op jit(solution)/shard_map/ppermute | solution.py:42
  35.2 4.8 %collective-permute-start = (bf16[128,128]{1,0:T(8,128)(2,1)S(1)}, bf16[128,128]{1,0:T(8,128)(2,1)S(1)}, u32[]{:S(2)}, u32[]{:S(2)}) collective-permute-start(bf16[128,128]{1,0:T(8,128)(2,1)S(1)} %convert_element_type.9), channel_id=1, source_target_pairs={{0,0},{1,1},{2,2},{3,3},{4,4},{5,5},{6,518},{7,519},{8,256},{9,257... | collective-permute-start | bytes 98312 | tf_op jit(solution)/shard_map/ppermute | solution.py:42
  40.0 2.9 %copy-start.1 = (f32[128,128]{1,0:T(8,128)S(1)}, f32[128,128]{1,0:T(8,128)}, u32[]{:S(2)}) copy-start(f32[128,128]{1,0:T(8,128)} %param.6) | copy-start | bytes 196612
  40.0 7.6 %collective-permute-start.2 = (bf16[2,128,128]{2,1,0:T(8,128)(2,1)S(1)}, bf16[2,128,128]{2,1,0:T(8,128)(2,1)S(1)}, u32[]{:S(2)}, u32[]{:S(2)}) collective-permute-start(bf16[2,128,128]{2,1,0:T(8,128)(2,1)S(1)} %pad_maximum_fusion.3), channel_id=1, source_target_pairs={{0,64},{32,96},{64,0},{96,32},{128,192},{160,224},{192,128},{224,1... | collective-permute-start | bytes 196616 | tf_op jit(solution)/shard_map/ppermute | solution.py:25
  43.0 24.0 %collective-permute-start.4 = (f32[2,128,128]{2,1,0:T(8,128)S(1)}, f32[2,128,128]{2,1,0:T(8,128)S(1)}, u32[]{:S(2)}, u32[]{:S(2)}) collective-permute-start(f32[2,128,128]{2,1,0:T(8,128)S(1)} %pad_maximum_fusion.2), channel_id=1, source_target_pairs={{0,0},{1,1},{2,2},{3,3},{4,4},{5,5},{6,518},{7,519},{8,256},{9,257... | collective-permute-start | bytes 393224 | tf_op jit(solution)/shard_map/ppermute | solution.py:42
  54.5 15.1 %all-to-all-start.1 = ((bf16[4,4,128,128]{3,2,1,0:T(8,128)(2,1)}), bf16[4,4,128,128]{3,2,1,0:T(8,128)(2,1)S(1)}, u32[]{:S(2)}, u32[]{:S(2)}) async-start(bf16[4,4,128,128]{3,2,1,0:T(8,128)(2,1)} %broadcast_in_dim.27), calls=%async_computation.1 | async-start | bytes 1048576 | tf_op jit(solution)/shard_map/all_to_all | solution.py:21
  61.9 7.7 %collective-permute-start.3 = (bf16[4,128,128]{2,1,0:T(8,128)(2,1)S(1)}, bf16[4,128,128]{2,1,0:T(8,128)(2,1)S(1)}, u32[]{:S(2)}, u32[]{:S(2)}) collective-permute-start(bf16[4,128,128]{2,1,0:T(8,128)(2,1)S(1)} %bitcast.91), channel_id=1, source_target_pairs={{0,32},{32,0},{64,96},{96,64},{128,160},{160,128},{192,224},{224,1... | collective-permute-start | bytes 393224 | tf_op jit(solution)/shard_map/ppermute | solution.py:25
  69.6 7.5 %collective-permute-start.5 = (bf16[16,128,128]{2,1,0:T(8,128)(2,1)S(1)}, bf16[16,128,128]{2,1,0:T(8,128)(2,1)S(1)}, u32[]{:S(2)}, u32[]{:S(2)}) collective-permute-start(bf16[16,128,128]{2,1,0:T(8,128)(2,1)S(1)} %bitcast.86), channel_id=1, source_target_pairs={{0,1},{1,0},{2,3},{3,2},{4,5},{5,4},{6,7},{7,6},{8,9},{9,8},{10,11... | collective-permute-start | bytes 1572872 | tf_op jit(solution)/shard_map/ppermute | solution.py:25
  78.4 9.3 %all-to-all-start.2 = ((f32[4,128,128]{2,1,0:T(8,128)}), f32[4,128,128]{2,1,0:T(8,128)S(1)}, u32[]{:S(2)}, u32[]{:S(2)}) async-start(f32[4,128,128]{2,1,0:T(8,128)} %fusion.21), calls=%async_computation.2 | async-start | bytes 524288 | tf_op jit(solution)/shard_map/all_to_all | solution.py:82
  87.9 8.4 %collective-permute-start.6 = (f32[128,128]{0,1:T(8,128)S(1)}, f32[128,128]{0,1:T(8,128)S(1)}, u32[]{:S(2)}, u32[]{:S(2)}) collective-permute-start(f32[128,128]{0,1:T(8,128)S(1)} %copy.46), channel_id=1, source_target_pairs={{0,0},{1,32},{2,64},{3,96},{4,128},{5,160},{518,192},{519,224},{25... | collective-permute-start | bytes 196616 | tf_op jit(solution)/shard_map/ppermute | solution.py:42
  146.2 8.7 %collective-permute-start.7 = (f32[128,128]{0,1:T(8,128)S(1)}, f32[128,128]{0,1:T(8,128)S(1)}, u32[]{:S(2)}, u32[]{:S(2)}) collective-permute-start(f32[128,128]{0,1:T(8,128)S(1)} %copy.48), channel_id=1, source_target_pairs={{0,0},{1,32},{2,64},{3,96},{4,128},{5,160},{518,192},{519,224},{25... | collective-permute-start | bytes 196616 | tf_op jit(solution)/shard_map/ppermute | solution.py:42
  197.8 12.5 %collective-permute-start.8 = (f32[128,128]{0,1:T(8,128)S(1)}, f32[128,128]{0,1:T(8,128)S(1)}, u32[]{:S(2)}, u32[]{:S(2)}) collective-permute-start(f32[128,128]{0,1:T(8,128)S(1)} %copy.50), channel_id=1, source_target_pairs={{0,0},{1,32},{2,64},{3,96},{4,128},{5,160},{518,192},{519,224},{25... | collective-permute-start | bytes 196616 | tf_op jit(solution)/shard_map/ppermute | solution.py:42
  210.9 21.9 %collective-permute-start.9 = (f32[128,128]{1,0:T(8,128)S(1)}, f32[128,128]{1,0:T(8,128)S(1)}, u32[]{:S(2)}, u32[]{:S(2)}) collective-permute-start(f32[128,128]{1,0:T(8,128)S(1)} %get-tuple-element.28), channel_id=1, source_target_pairs={{0,0},{1,1},{2,2},{3,3},{4,4},{5,5},{518,6},{519,7},{256,8},{257,9... | collective-permute-start | bytes 196616 | tf_op jit(solution)/shard_map/ppermute | solution.py:42
  233.5 45.7 %all-to-all-start.8 = ((f32[32,1,128]{2,1,0:T(1,128)}), f32[32,1,128]{2,1,0:T(1,128)S(1)}, u32[]{:S(2)}, u32[]{:S(2)}) async-start(f32[32,1,128]{2,1,0:T(1,128)} %broadcast_in_dim.63), calls=%async_computation.8 | async-start | bytes 32768 | tf_op jit(solution)/shard_map/all_to_all | solution.py:21
